TPU v7x, 128 devices: a whole 4x4x4 slice. The times are simulated.
128 devices in a mesh: kv: 16 (over y, x), head: 8 (over z, core).
Axes of the slice: x: 4, y: 4, z: 4, core: 2. Of those that a mesh axis runs over, the one named last changes fastest.
Arguments:
- hidden_in: bfloat16 [64, 6144], P(None, 'kv'), may hold values from -1 to 1
- attn_gain: float32 [6144], P('kv'), may hold values from 0.1 to 1.9
- attn_weight: bfloat16 [6144, 10240], P('kv', 'head'), may hold values from -0.078125 to 0.078125
- attn_out_weight: bfloat16 [8192, 6144], P('head', 'kv'), may hold values from -0.25 to 0.25
- cache_keys: bfloat16 [1024, 8, 256, 128], P('kv', 'head'), may hold values from -600 to 600
- cache_values: bfloat16 [1024, 8, 256, 128], P('kv', 'head'), may hold values from -6 to 6
- stretch_counts: int32 [64], replicated, may hold values from 1 to 64, 896 in all
- tail_tokens: int32 [64], replicated, may hold values from 0 to 255
- slot_stretch: int32 [1024], P('kv'), may hold values from 0 to 1023, each once
- lin_gain: float32 [6144], P('kv'), may hold values from 0.1 to 1.9
- lin_weight: bfloat16 [6144, 32768], P('kv', 'head'), may hold values from -0.078125 to 0.078125
- decay_rate: float32 [64], P('head'), may hold values from 0.02 to 2
- states: float32 [64, 64, 128, 128], P('kv', 'head'), may hold values from -2 to 2
- out_gain: float32 [8192], P('head'), may hold values from 0.1 to 1.9
- lin_out_weight: bfloat16 [8192, 6144], P('head', 'kv'), may hold values from -0.0625 to 0.0625
- state_request: int32 [64], replicated, may hold values from 0 to 63, each once
Outputs:
- hidden_out: bfloat16 [64, 6144], P(None, 'kv')
- new_states: float32 [64, 64, 128, 128], P('kv', 'head')
Inputs may be any that keep to these rules, and one draw needn't show every extreme that they name: `stretch_counts`: the counts sum to 896; some request has exactly 64 stretches. `slot_stretch`: each id of 0 to 1023 once; ids of 896 or more mark empty slots. `state_request`: each request once.
All inputs are finite; a program needn't handle non-finite values.
Results may differ from a plain program's by a relative error of at most 0.014.
The roundings to bfloat16 on the way count: a program that leaves them out, or rounds other values in their place, can miss the bound.
Values may be sent and summed in bfloat16 or wider, within the bound.
No kernel may reach another device: no remote copies, remote signals or barrier semaphores. Data moves between devices by JAX's collectives and lax.ppermute only.
A program may use at most 64 MiB of HBM per device.

v0:
```python
import math

import jax
import jax.numpy as jnp
from jax import lax
from jax.sharding import PartitionSpec as P

D = 6144
HD = 128
LH = 64
REQ_DEV = 4
CH = 256
GQ = 8


EPS = 1e-05
NEGATIVE = -1e30


def merged(shard, axis, combine):
    everything = jax.tree.map(lambda part: lax.all_gather(part, axis), shard)
    initial = jax.tree.map(lambda part: part[0], everything)

    def hop(k, so_far):
        return combine(so_far, jax.tree.map(lambda part: part[k], everything))

    return lax.fori_loop(1, lax.axis_size(axis), hop, initial)


def stretch_table(stretch_counts, tail_tokens, slot_stretch, span):
    number = stretch_counts.shape[0]
    ends = jnp.cumsum(stretch_counts)
    starts = ends - stretch_counts
    limits = stretch_counts * span - tail_tokens
    owner = jnp.sum((slot_stretch[:, None] >= ends[None, :]).astype(jnp.int32), axis=1)
    hits = owner[:, None] == jnp.arange(number, dtype=jnp.int32)[None, :]
    first = jnp.sum(jnp.where(hits, starts[None, :], 0), axis=1)
    limit = jnp.sum(jnp.where(hits, limits[None, :], 0), axis=1)
    offset = (slot_stretch - first) * span
    valid = offset[:, None] + jnp.arange(span, dtype=jnp.int32)[None, :] < limit[:, None]
    return (hits, valid)


def fold_slots(hits, highest, totals, partial_value):
    chosen = hits.T[:, :, None, None]
    best = jnp.max(jnp.where(chosen, highest[None], NEGATIVE), axis=1)
    factor = jnp.where(chosen, jnp.exp(jnp.minimum(highest[None] - best[:, None], 0.0)), 0.0)
    summed = jnp.sum(factor * totals[None], axis=1)
    mixed = jnp.einsum("rskg,skgd->rkgd", factor, partial_value, precision=lax.Precision.HIGHEST)
    return (best, summed, mixed)


def finish(best, summed, mixed, queries, fresh_key, fresh_value):
    fresh = jnp.einsum(
        "rkgd,rkd->rkg", queries, fresh_key, preferred_element_type=jnp.float32
    ) / math.sqrt(queries.shape[-1])
    peak = jnp.maximum(best, fresh)
    earlier = jnp.exp(best - peak)
    latest = jnp.exp(fresh - peak)
    result = (
        earlier[..., None] * mixed
        + latest[..., None] * fresh_value.astype(jnp.float32)[:, :, None, :]
    ) / (earlier * summed + latest)[..., None]
    return result.astype(jnp.bfloat16)


def combine(first, second):
    peak = jnp.maximum(first[0], second[0])
    early = jnp.exp(first[0] - peak)
    later = jnp.exp(second[0] - peak)
    return (
        peak,
        early * first[1] + later * second[1],
        early[..., None] * first[2] + later[..., None] * second[2],
    )


def per_device(
    hidden_in,
    attn_gain,
    attn_weight,
    attn_out_weight,
    cache_keys,
    cache_values,
    stretch_counts,
    tail_tokens,
    slot_stretch,
    lin_gain,
    lin_weight,
    decay_rate,
    states,
    out_gain,
    lin_out_weight,
    state_request,
):
    requests = hidden_in.shape[0]
    heads_here = cache_keys.shape[1]
    lin_heads = decay_rate.shape[0]
    inputs = hidden_in.astype(jnp.float32)
    scaled = (inputs * attn_gain).astype(jnp.bfloat16)
    projected, squares = lax.psum(
        (
            jnp.dot(scaled, attn_weight, preferred_element_type=jnp.float32),
            jnp.sum(inputs * inputs, axis=1),
        ),
        "kv",
    )
    projected = (projected / jnp.sqrt(squares / D + EPS)[:, None]).astype(jnp.bfloat16)
    projected = projected.reshape(requests, heads_here, GQ + 2, HD)
    queries = projected[:, :, :GQ]
    fresh_key = projected[:, :, GQ]
    fresh_value = projected[:, :, GQ + 1]
    hits, valid = stretch_table(stretch_counts, tail_tokens, slot_stretch, CH)
    picked = jnp.einsum(
        "sr,rkgd->skgd", hits.astype(jnp.bfloat16), queries, preferred_element_type=jnp.float32
    ).astype(jnp.bfloat16)
    scores = jnp.einsum(
        "skgd,sktd->skgt", picked, cache_keys, preferred_element_type=jnp.float32
    ) / math.sqrt(HD)
    mask = valid[:, None, None, :]
    highest = jnp.max(jnp.where(mask, scores, NEGATIVE), axis=-1)
    weights = jnp.where(mask, jnp.exp(scores - highest[..., None]), 0.0)
    totals = jnp.sum(weights, axis=-1)
    partial_value = jnp.einsum(
        "skgt,sktd->skgd",
        weights.astype(jnp.bfloat16),
        cache_values,
        preferred_element_type=jnp.float32,
    )
    best, summed, mixed = fold_slots(hits, highest, totals, partial_value)
    best, summed, mixed = merged((best, summed, mixed), "kv", combine)
    attended = finish(best, summed, mixed, queries, fresh_key, fresh_value).reshape(
        requests, heads_here * GQ * HD
    )
    first_part = jnp.dot(attended, attn_out_weight, preferred_element_type=jnp.float32)
    first_out = lax.psum(first_part, "head")
    middle = (inputs + first_out).astype(jnp.bfloat16)
    inner = middle.astype(jnp.float32)
    squares_two = lax.psum(jnp.sum(inner * inner, axis=1), "kv")
    scaled_two = (inner * lin_gain).astype(jnp.bfloat16)
    ordered = jnp.take(scaled_two, state_request, axis=0)
    mixing = lax.psum_scatter(
        jnp.dot(ordered, lin_weight, preferred_element_type=jnp.float32),
        "kv",
        scatter_dimension=0,
        tiled=True,
    )
    mine = lax.dynamic_slice_in_dim(state_request, lax.axis_index("kv") * REQ_DEV, REQ_DEV, 0)
    mixing = mixing / jnp.sqrt(jnp.take(squares_two, mine) / D + EPS)[:, None]
    mixing = mixing.reshape(REQ_DEV, lin_heads, 4, HD)
    query = jax.nn.silu(mixing[:, :, 0])
    keyed = jax.nn.silu(mixing[:, :, 1])
    valued = jax.nn.silu(mixing[:, :, 2])
    gate = jax.nn.sigmoid(mixing[:, :, 3])
    keep = jnp.exp(-decay_rate)[None, :, None, None]
    renewed = keep * states + keyed[..., :, None] * valued[..., None, :]
    readout = jnp.einsum("rhi,rhij->rhj", query, renewed, precision=lax.Precision.HIGHEST)
    read_squares = lax.psum(jnp.sum(readout * readout, axis=(1, 2)), "head")
    gated = (
        (
            readout
            / jnp.sqrt(read_squares / (LH * HD) + EPS)[:, None, None]
            * out_gain.reshape(lin_heads, HD)
            * gate
        )
        .astype(jnp.bfloat16)
        .reshape(REQ_DEV, lin_heads * HD)
    )
    second_part = jnp.dot(
        lax.all_gather(gated, "kv", axis=0, tiled=True),
        lin_out_weight,
        preferred_element_type=jnp.float32,
    )
    second_out = lax.psum(second_part, "head")
    placed = jnp.zeros_like(second_out).at[state_request].set(second_out)
    return ((inner + placed).astype(jnp.bfloat16), renewed)


def solution(mesh):
    placed = (
        P(None, "kv"),
        P("kv"),
        P("kv", "head"),
        P("head", "kv"),
        P("kv", "head", None, None),
        P("kv", "head", None, None),
        P(),
        P(),
        P("kv"),
        P("kv"),
        P("kv", "head"),
        P("head"),
        P("kv", "head", None, None),
        P("head"),
        P("head", "kv"),
        P(),
    )
    return jax.shard_map(
        per_device,
        mesh=mesh,
        in_specs=placed,
        out_specs=(P(None, "kv"), P("kv", "head", None, None)),
        check_vma=False,
    )
```

profile of v0, /device:TPU:0, one launch (start us, length us, event | category | flops | bytes accessed | tf_op | source)
XLA Modules:
  0.0 461.9 jit_solution(244052363437510420)
XLA Ops:
  7.2 2.4 fusion.40
  9.7 0.9 fusion.35
  10.6 40.8 %psum.43 = f32[64]{0:T(128)S(1)} all-reduce(f32[64]{0:T(128)S(1)} %fusion.35), channel_id=1, replica_groups=mesh['kv'=16,'head'=8] {'kv'}, use_global_device_ids=true, to_apply=%region_6.7 | all-reduce | flops 64 | bytes 512 | tf_op jit(solution)/shard_map/psum | solution.py:101
  51.4 0.7 copy.117
  52.3 0.8 convert_reduce_fusion
  54.8 42.8 %all-reduce.6.cloned.1.call-done = f32[64,1280]{1,0:T(8,128)} async-done(((f32[64,1280]{1,0:T(8,128)}), f32[64,1280]{1,0:T(8,128)}) %all-reduce.6.cloned.1.call-update) | async-done | bytes 327696 | tf_op jit(solution)/shard_map/psum | solution.py:101
  97.6 1.7 divide_convert_fusion
  99.3 1.0 reshape.266
  100.6 4.2 select_reduce_fusion
  105.1 3.1 fusion.6
  108.2 1.1 convolution_bitcast_fusion
  109.7 1.3 fusion.14
  111.4 24.6 %all-gather.4 = f32[16,64,8]{1,2,0:T(8,128)} all-gather(f32[1,64,8]{1,2,0:T(8,128)S(1)} %copy.123), channel_id=3, replica_groups=mesh['kv'=16,'head'=8] {'kv'}, dimensions={0}, use_global_device_ids=true | all-gather | bytes 34816 | tf_op jit(solution)/shard_map/all_gather | solution.py:21
  136.1 23.3 %all-gather.3 = f32[16,64,8]{1,2,0:T(8,128)} all-gather(f32[1,64,8]{1,2,0:T(8,128)S(1)} %copy.121), channel_id=2, replica_groups=mesh['kv'=16,'head'=8] {'kv'}, dimensions={0}, use_global_device_ids=true | all-gather | bytes 34816 | tf_op jit(solution)/shard_map/all_gather | solution.py:21
  161.3 1.0 slice.52
  162.5 42.9 %while.19 = (s32[]{:T(128)}, f32[64,1,8]{0,2,1:T(8,128)S(1)}, f32[64,1,8]{0,2,1:T(8,128)S(1)}, f32[64,1,8,128]{3,2,1,0:T(8,128)S(1)}, f32[16,64,1,8]{1,3,2,0:T(8...) while((s32[]{:T(128)}, f32[64,1,8]{0,2,1:T(8,128)S(1)}, ...), condition=%wide.region_12.13_spmd, body=%wide.region_11.12_spmd.sunk | while | flops 200197 | bytes 1349779 | solution.py:27
  164.1 1.0 constant_dynamic-slice_fusion.2
  165.4 0.7 fusion.75
  166.1 0.7 fusion.76
  166.9 1.0 constant_dynamic-slice_fusion.2
  168.9 0.7 fusion.76
  169.8 1.0 constant_dynamic-slice_fusion.2
  171.8 0.7 fusion.76
  172.7 1.0 constant_dynamic-slice_fusion.2
  174.0 0.7 fusion.75
  174.7 0.7 fusion.76
  175.5 1.0 constant_dynamic-slice_fusion.2
  178.4 1.0 constant_dynamic-slice_fusion.2
  181.2 1.0 constant_dynamic-slice_fusion.2
  183.2 0.7 fusion.76
  184.1 1.0 constant_dynamic-slice_fusion.2
  186.9 1.0 constant_dynamic-slice_fusion.2
  188.9 0.7 fusion.76
  189.8 1.0 constant_dynamic-slice_fusion.2
  191.8 0.7 fusion.76
  192.7 1.0 constant_dynamic-slice_fusion.2
  194.6 0.7 fusion.76
  195.5 1.0 constant_dynamic-slice_fusion.2
  197.5 0.7 fusion.76
  198.4 1.0 constant_dynamic-slice_fusion.2
  199.7 0.7 fusion.75
  200.4 0.7 fusion.76
  201.2 1.0 constant_dynamic-slice_fusion.2
  202.5 0.7 fusion.75
  203.2 0.7 fusion.76
  204.1 1.0 constant_dynamic-slice_fusion.2
  205.6 0.7 copy.132
  206.3 1.0 divide_convert_fusion.1
  207.3 2.0 fusion.24
  209.4 56.6 %all-reduce.8.cloned.1.call-done = f32[64,384]{1,0:T(8,128)} async-done(((f32[64,384]{1,0:T(8,128)}), f32[64,384]{1,0:T(8,128)}) %all-reduce.8.cloned.1.call-update) | async-done | bytes 98320 | tf_op jit(solution)/shard_map/psum | solution.py:136
  266.0 1.0 fusion.38
  267.1 0.7 gather_fusion
  267.8 1.7 fusion.42
  270.9 40.4 %psum.45 = f32[64]{0:T(128)S(1)} all-reduce(f32[64]{0:T(128)S(1)} %get-tuple-element.250), channel_id=1, replica_groups=mesh['kv'=16,'head'=8] {'kv'}, use_global_device_ids=true, to_apply=%region_16.17 | all-reduce | flops 64 | bytes 512 | tf_op jit(solution)/shard_map/psum | solution.py:139
  312.0 43.6 %all-reduce.12.cloned.1.call-done = f32[64,4096]{1,0:T(8,128)} async-done(((f32[64,4096]{1,0:T(8,128)}), f32[64,4096]{1,0:T(8,128)}) %all-reduce.12.cloned.1.call-update) | async-done | bytes 1048592
  355.6 1.0 dynamic-slice_divide_fusion
  356.8 2.0 multiply_add_fusion
  358.8 1.3 copy-done.1
  360.1 1.9 fusion.63
  362.1 13.3 %psum.46 = f32[4]{0:T(128)S(1)} all-reduce(f32[4]{0:T(128)S(1)} %multiply_reduce_fusion.1), channel_id=1, replica_groups=mesh['kv'=16,'head'=8] {'head'}, use_global_device_ids=true, to_apply=%region_18.19 | all-reduce | flops 4 | bytes 32 | tf_op jit(solution)/shard_map/psum | solution.py:158
  375.5 22.1 %all-gather.5 = bf16[16,4,1024]{2,1,0:T(4,128)(2,1)S(1)} all-gather(bf16[1,4,1024]{2,1,0:T(4,128)(2,1)S(1)} %reshape.315), channel_id=1, replica_groups=mesh['kv'=16,'head'=8] {'kv'}, dimensions={0}, use_global_device_ids=true | all-gather | bytes 139264 | tf_op jit(solution)/shard_map/all_gather | solution.py:170
  397.7 2.0 fusion.64
  399.7 53.8 %all-reduce.10.cloned.1.call-done = f32[64,384]{1,0:T(8,128)} async-done(((f32[64,384]{1,0:T(8,128)}), f32[64,384]{1,0:T(8,128)}) %all-reduce.10.cloned.1.call-update) | async-done | bytes 98320 | tf_op jit(solution)/shard_map/psum | solution.py:174
  453.5 1.2 scatter_custom_fusion
  (150 shorter events, 25.5 us)
Async XLA Ops:
  7.2 260.6 %copy-start = (bf16[384,4096]{1,0:T(8,128)(2,1)S(1)}, bf16[384,4096]{1,0:T(8,128)(2,1)}, u32[]{:S(2)}) copy-start(bf16[384,4096]{1,0:T(8,128)(2,1)} %param.28) | copy-start | bytes 9437188
  7.2 90.4 %all-reduce.6.cloned.1.call-start = ((), (), s32[]{:S(2)}) async-start(), calls=%async_computation | async-start | bytes 655360 | tf_op jit(solution)/shard_map/psum | solution.py:101
  9.6 151.7 %all-gather.8.cloned.1.call-start = ((), (), s32[]{:S(2)}) async-start(), calls=%async_computation.3 | async-start | bytes 4456448 | tf_op jit(solution)/shard_map/all_gather | solution.py:21
  104.8 4.6 copy-start.5
  109.3 156.7 %all-reduce.8.cloned.1.call-start = ((), (), s32[]{:S(2)}) async-start(), calls=%async_computation.1 | async-start | bytes 196608 | tf_op jit(solution)/shard_map/psum | solution.py:136
  162.5 103.5 %copy-start.2 = (bf16[64,384]{1,0:T(8,128)(2,1)S(1)}, bf16[64,384]{1,0:T(8,128)(2,1)}, u32[]{:S(2)}) copy-start(bf16[64,384]{1,0:T(8,128)(2,1)} %param.18) | copy-start | bytes 147460
  162.5 104.5 %copy-start.4 = (f32[384]{0:T(512)S(1)}, f32[384]{0:T(512)}, u32[]{:S(2)}) copy-start(f32[384]{0:T(512)} %param.27) | copy-start | bytes 4612
  209.3 60.2 %copy-start.8 = (u32[128]{0:T(128)S(1)}, u32[128]{0:T(128)}, u32[]{:S(2)}) copy-start(u32[128]{0:T(128)} %constant.117) | copy-start | bytes 1540
  209.3 61.4 %copy-start.6 = (s32[64]{0:T(128)S(1)}, s32[64]{0:T(128)}, u32[]{:S(2)}) copy-start(s32[64]{0:T(128)} %param.33) | copy-start | bytes 772
  209.4 61.5 %copy-start.7 = (f32[8]{0:T(128)S(1)}, f32[8]{0:T(128)}, u32[]{:S(2)}) copy-start(f32[8]{0:T(128)} %param.29) | copy-start | bytes 100
  209.4 146.3 %all-reduce.12.cloned.1.call-start = ((), (), s32[]{:S(2)}) async-start(), calls=%async_computation.4 | async-start | bytes 2097152
  269.5 184.0 %all-reduce.10.cloned.1.call-start = ((), (), s32[]{:S(2)}) async-start(), calls=%async_computation.2 | async-start | bytes 196608 | tf_op jit(solution)/shard_map/psum | solution.py:174
  356.8 18.6 %copy-start.3 = (f32[1024]{0:T(1024)S(1)}, f32[1024]{0:T(1024)}, u32[]{:S(2)}) copy-start(f32[1024]{0:T(1024)} %param.31) | copy-start | bytes 12292
  358.8 1.3 copy-start.1
Sparse Core Ops, SparseCore 0:
  11.8 85.7 all-reduce.5
  109.5 51.2 all-gather.7
  209.5 56.4 all-reduce.7
  270.0 85.5 all-reduce.11
  399.8 53.6 all-reduce.9
where the time goes:
time: 464 us; the launch traced here: 462 us
  waiting for transfers between devices  197 us (42%)
  blocking collectives  164 us (35%)
  other arithmetic  39.1 us (8%)
  local copies, waits for them, and re-layouts  27.2 us (6%)
  matrix products  18.8 us (4%)
  between operations  14.7 us (3%)
    psum x1, waiting for transfers between devices, per_device(): first_out = lax.psum(first_part, 'head')  56.6 us
    psum x1, waiting for transfers between devices, per_device(): second_out = lax.psum(second_part, 'head')  53.8 us
    all_gather x2, blocking collectives, merged(): everything = jax.tree.map(lambda part: lax.all_gather(part, axis), shard)  47.9 us
    unnamed x6, waiting for transfers between devices  43.7 us
    psum x1, waiting for transfers between devices, per_device(): lax.psum((jnp.dot(scaled, attn_weight, preferred_element_type=jnp.float32...  42.8 us
    psum x1, blocking collectives, per_device(): lax.psum((jnp.dot(scaled, attn_weight, preferred_element_type=jnp.float32...  40.8 us
    psum x1, blocking collectives, per_device(): squares_two = lax.psum(jnp.sum(inner * inner, axis=1), 'kv')  40.4 us
    all_gather x1, blocking collectives, per_device(): lax.all_gather(gated, 'kv', axis=0, tiled=True)  22.1 us
  transfers between devices with their start and end apart: 5, of which 4 were waited for; matrix products, arithmetic and copies ran while one was open for 2% of the time, Pallas kernels for 0%

commit v1 on v0

v1 whole, which is shorter than its diff:
```python
import functools
import math

import jax
import jax.numpy as jnp
from jax import lax
from jax.experimental import pallas as pl
from jax.experimental.pallas import tpu as pltpu
from jax.sharding import PartitionSpec as P

D = 6144
HD = 128
LH = 64
CH = 256
GQ = 8
REQ = 64
EPS = 1e-05
NEGATIVE = -1e30
F32 = jnp.float32
BF16 = jnp.bfloat16
MIB = 1 << 20


def iota(shape, dim):
    return lax.broadcasted_iota(jnp.int32, shape, dim)


def as_column(row):
    n = row.shape[1]
    eye = iota((n, n), 0) == iota((n, n), 1)
    return jnp.sum(jnp.where(eye, row, jnp.zeros_like(row)), axis=1, keepdims=True)


def as_row(column):
    n = column.shape[0]
    eye = iota((n, n), 0) == iota((n, n), 1)
    return jnp.sum(jnp.where(eye, column, jnp.zeros_like(column)), axis=0, keepdims=True)


def kernel_call(body, outs, ins, limit, flops, moved, scratch=()):
    return pl.pallas_call(
        body,
        out_shape=outs,
        in_specs=ins,
        out_specs=jax.tree.map(lambda _: pl.BlockSpec(memory_space=pltpu.VMEM), outs),
        scratch_shapes=scratch,
        compiler_params=pltpu.CompilerParams(vmem_limit_bytes=limit),
        cost_estimate=pl.CostEstimate(flops=flops, bytes_accessed=moved, transcendentals=0),
    )


VMEM = pl.BlockSpec(memory_space=pltpu.VMEM)
SMEM = pl.BlockSpec(memory_space=pltpu.SMEM)


def project_kernel(hidden, gain, weight, counts, tails, slots, out, info):
    x = hidden[...].astype(F32)
    scaled = (x * gain[...]).astype(BF16)
    squares = jnp.sum(x * x, axis=1, keepdims=True)
    y = jnp.dot(scaled, weight[...], preferred_element_type=F32)
    groups, rows, _ = out.shape
    width = weight.shape[1]
    wide = jnp.broadcast_to(squares, (x.shape[0], HD))
    for p in range(groups):
        out[p, :, :width] = y[p * rows:(p + 1) * rows]
        out[p, :, width:] = wide[p * rows:(p + 1) * rows]
    number = counts[...]
    n = number.shape[1]
    below = iota((n, n), 1) <= iota((n, n), 0)
    ends = jnp.sum(jnp.where(below, number, 0), axis=1, keepdims=True)
    count = as_column(number)
    starts = ends - count
    limits = count * CH - as_column(tails[...])
    slot = slots[...]
    owner = jnp.sum((slot >= ends).astype(jnp.int32), axis=0, keepdims=True)
    hits = iota((n, slot.shape[1]), 0) == owner
    first = jnp.sum(jnp.where(hits, starts, 0), axis=0, keepdims=True)
    limit = jnp.sum(jnp.where(hits, limits, 0), axis=0, keepdims=True)
    live = jnp.clip(limit - (slot - first) * CH, 0, CH)
    info[0:1, :] = owner
    info[1:2, :] = jnp.where(owner < n, live, 0)


def normalise_kernel(parts, out, own):
    total = parts[0]
    for p in range(1, parts.shape[0]):
        total = total + parts[p]
    width = own.shape[1] * HD
    mean = total[:, width:width + 1] / D
    projected = (total[:, :width] / jnp.sqrt(mean + EPS)).astype(BF16).astype(F32)
    for g in range(own.shape[1]):
        own[:, g, :] = projected[:, g * HD:(g + 1) * HD]
    queries = own[:, :GQ, :].astype(BF16)
    for p in range(out.shape[0]):
        out[p] = queries


def attention_kernel(queries, keys, values, info, out, slot_max, slot_sum, slot_value, best, summed, mixed):
    slots = keys.shape[0]
    rows = out.shape[1] // (GQ + 2)
    best[...] = jnp.full(best.shape, NEGATIVE, F32)
    summed[...] = jnp.zeros(summed.shape, F32)
    mixed[...] = jnp.zeros(mixed.shape, F32)
    token = iota((GQ, CH), 1)
    scale = 1.0 / math.sqrt(HD)
    batch = 8

    @pl.loop(0, slots, step=batch)
    def _(base):
        for u in range(batch):
            s = base + u
            owner = info[0, s]
            q = queries[jnp.minimum(owner, REQ - 1)]
            scores = lax.dot_general(
                q, keys[s], (((1,), (1,)), ((), ())), preferred_element_type=F32
            ) * scale
            live = token < info[1, s]
            top = jnp.max(jnp.where(live, scores, NEGATIVE), axis=1, keepdims=True)
            weights = jnp.where(live, jnp.exp(scores - top), 0.0)
            slot_sum[s] = jnp.broadcast_to(jnp.sum(weights, axis=1, keepdims=True), (GQ, HD))
            slot_max[s] = jnp.broadcast_to(top, (GQ, HD))
            slot_value[s] = jnp.dot(weights.astype(BF16), values[s], preferred_element_type=F32)

    @pl.loop(0, slots, step=batch)
    def _(base):
        for u in range(batch):
            s = base + u
            r = info[0, s]
            best[r] = jnp.maximum(best[r], slot_max[s])

    @pl.loop(0, slots, step=batch)
    def _(base):
        for u in range(batch):
            s = base + u
            r = info[0, s]
            factor = jnp.exp(slot_max[s] - best[r])
            summed[r] = summed[r] + factor * slot_sum[s]
            mixed[r] = mixed[r] + factor * slot_value[s]

    lane, sub = iota((GQ, HD), 1), iota((GQ, HD), 0)

    @pl.loop(0, out.shape[0])
    def _(p):
        for i in range(rows):
            r = p * rows + i
            out[p, i * GQ:(i + 1) * GQ, :] = mixed[r]
            packed = jnp.where(lane == sub, best[r], 0.0) + jnp.where(lane == sub + GQ, summed[r], 0.0)
            out[p, rows * GQ + i:rows * GQ + i + 1, :] = jnp.sum(packed, axis=0, keepdims=True)


def finish_kernel(parts, own, out, flat, fresh_rows):
    peers, rows = parts.shape[0], own.shape[0]
    lane, sub = iota((GQ, HD), 1), iota((GQ, HD), 0)
    diagonal = lane == sub
    for i in range(rows):
        fresh = jnp.sum(own[i, :GQ, :] * own[i, GQ:GQ + 1, :], axis=1, keepdims=True) / math.sqrt(HD)
        fresh_rows[i:i + 1, :] = jnp.sum(jnp.where(diagonal, fresh, 0.0), axis=0, keepdims=True)
    fresh = fresh_rows[0:rows, :]
    stats = [parts[p, rows * GQ:rows * GQ + rows, :] for p in range(peers)]
    top = fresh
    for p in range(peers):
        top = jnp.maximum(top, stats[p])
    latest = jnp.exp(fresh - top)
    below = latest
    factors = []
    for p in range(peers):
        factor = jnp.exp(stats[p] - top)
        below = below + factor * pltpu.roll(stats[p], HD - GQ, axis=1)
        factors.append(factor)
    for i in range(rows):
        def column(value):
            return jnp.sum(jnp.where(diagonal, value[i:i + 1, :], 0.0), axis=1, keepdims=True)

        above = column(latest) * own[i, GQ + 1:GQ + 2, :]
        for p in range(peers):
            above = above + column(factors[p]) * parts[p, i * GQ:(i + 1) * GQ, :]
        result = above / column(below)
        for g in range(GQ):
            flat[i:i + 1, g * HD:(g + 1) * HD] = result[g:g + 1, :]
    attended = flat[0:rows, :].astype(BF16)
    for p in range(out.shape[0]):
        out[p] = attended


def stacked(blocks, flat):
    peers, rows, _ = blocks.shape
    for p in range(peers):
        flat[p * rows:(p + 1) * rows, :] = blocks[p].astype(F32)


def attention_out_kernel(attended, weight, out, flat):
    stacked(attended, flat)
    out[...] = jnp.dot(flat[...].astype(BF16), weight[...], preferred_element_type=F32)


def mixing_kernel(one, two, hidden, gain, request, weight, out, middle):
    total = hidden[...].astype(F32) + (one[...] + two[...])
    inner = total.astype(BF16)
    middle[...] = inner
    n = request.shape[1]
    pick = (as_column(request[...]) == iota((n, n), 1)).astype(F32).astype(BF16)
    ordered = jnp.dot(pick, inner, preferred_element_type=F32)
    squares = jnp.broadcast_to(jnp.sum(ordered * ordered, axis=1, keepdims=True), (n, HD))
    scaled = (ordered * gain[...]).astype(BF16)
    groups, rows, _ = out.shape
    width = weight.shape[1]
    step = 512
    for c in range(0, width, step):
        y = jnp.dot(scaled, weight[:, c:c + step], preferred_element_type=F32)
        for p in range(groups):
            out[p, :, c:c + step] = y[p * rows:(p + 1) * rows].astype(out.dtype)
    for p in range(groups):
        out[p, :, width:] = squares[p * rows:(p + 1) * rows].astype(out.dtype)


def lightning_kernel(parts, decay, states, gain, renewed, out, flat, mixing, columns):
    total = parts[0].astype(F32)
    for p in range(1, parts.shape[0]):
        total = total + parts[p].astype(F32)
    rows, heads = states.shape[0], states.shape[1]
    width = heads * 4 * HD
    mixing[0:rows, :] = total[:, :width] / jnp.sqrt(total[:, width:width + 1] / D + EPS)
    keep_row = jnp.exp(-decay[...])
    squares = jnp.zeros((rows, 1), F32)
    for h in range(heads):
        at = h * 4 * HD
        mixed = [mixing[0:rows, at + k * HD:at + (k + 1) * HD] for k in range(4)]
        gate = 1.0 / (1.0 + jnp.exp(-mixed[3]))
        query, key, value = (m / (1.0 + jnp.exp(-m)) for m in mixed[:3])
        columns[0:rows, :] = query
        columns[rows:2 * rows, :] = key
        turned = columns[...].T
        inner = jnp.sum(query * key, axis=1, keepdims=True)
        keep = keep_row[:, h:h + 1]
        for j in range(rows):
            state = keep * states[j, h]
            renewed[j, h] = state + turned[:, rows + j:rows + j + 1] * value[j:j + 1, :]
            read = jnp.sum(turned[:, j:j + 1] * state, axis=0, keepdims=True)
            flat[j:j + 1, h * HD:(h + 1) * HD] = read + inner[j:j + 1, :] * value[j:j + 1, :]
        read = flat[0:rows, h * HD:(h + 1) * HD]
        squares = squares + jnp.sum(read * read, axis=1, keepdims=True)
        flat[0:rows, h * HD:(h + 1) * HD] = read * gain[:, h * HD:(h + 1) * HD] * gate
    size = heads * HD
    gated = flat[0:rows, 0:size].astype(BF16)
    upper = squares.astype(BF16).astype(F32)
    lane = iota((rows, HD), 1)
    tail = jnp.where(lane == 0, upper, jnp.where(lane == 1, squares - upper, 0.0)).astype(BF16)
    for p in range(out.shape[0]):
        out[p, :, :size] = gated
        out[p, :, size:] = tail


def lightning_out_kernel(blocks, request, weight, out, flat):
    stacked(blocks, flat)
    n = request.shape[1]
    size = weight.shape[0]
    pick = (iota((n, n), 0) == request[...]).astype(F32).astype(BF16)
    placed = jnp.dot(pick, flat[...].astype(BF16), preferred_element_type=F32)
    out[0:n, :] = jnp.dot(placed[:, :size].astype(BF16), weight[...], preferred_element_type=F32)
    squares = as_row(placed[:, size:size + 1] + placed[:, size + 1:size + 2])
    out[n:, :] = jnp.zeros((out.shape[0] - n, out.shape[1]), F32)
    out[n:n + 1, 0:n] = squares


def last_kernel(one, two, middle, out):
    n = middle.shape[0]
    squares = as_column(one[n:n + 1, 0:n] + two[n:n + 1, 0:n])
    scale = 1.0 / jnp.sqrt(squares / (LH * HD) + EPS)
    out[...] = (middle[...].astype(F32) + (one[0:n, :] + two[0:n, :]) * scale).astype(BF16)


def exchange(blocks):
    return lax.all_to_all(blocks, "kv", 0, 0, tiled=True)


def all_but_last_sum(value):
    size = lax.axis_size("head")
    value = value + lax.ppermute(value, "head", [(i, i ^ 1) for i in range(size)])
    value = value + lax.ppermute(value, "head", [(i, i ^ 2) for i in range(size)])
    last = [(i, (3 - i // 2) * 2 + i % 2) for i in range(size)]
    return value, lax.ppermute(value, "head", last)


def per_device(
    hidden_in,
    attn_gain,
    attn_weight,
    attn_out_weight,
    cache_keys,
    cache_values,
    stretch_counts,
    tail_tokens,
    slot_stretch,
    lin_gain,
    lin_weight,
    decay_rate,
    states,
    out_gain,
    lin_out_weight,
    state_request,
):
    peers = lax.axis_size("kv")
    requests, features = hidden_in.shape
    rows = requests // peers
    width = attn_weight.shape[1]
    slots = cache_keys.shape[0]
    heads = decay_rate.shape[0]
    lin_width = lin_weight.shape[1]
    size = heads * HD
    S = jax.ShapeDtypeStruct
    request = state_request[None, :]

    parts, info = kernel_call(
        project_kernel,
        (S((peers, rows, width + HD), F32), S((2, slots), jnp.int32)),
        [VMEM] * 6, 8 * MIB, 2 * requests * features * width, 2 * features * width,
    )(hidden_in, attn_gain[None, :], attn_weight, stretch_counts[None, :], tail_tokens[None, :], slot_stretch[None, :])
    queries, own = kernel_call(
        normalise_kernel,
        (S((peers, rows, GQ, HD), BF16), S((rows, GQ + 2, HD), F32)),
        [VMEM], 8 * MIB, 0, 8 * peers * rows * width,
    )(exchange(parts))
    queries = exchange(queries).reshape(requests, GQ, HD)
    tiles = [pltpu.VMEM((slots, GQ, HD), F32)] * 3 + [pltpu.VMEM((requests + 1, GQ, HD), F32)] * 3
    partial = kernel_call(
        attention_kernel,
        S((peers, rows * (GQ + 2), HD), F32),
        [VMEM, VMEM, VMEM, SMEM], 24 * MIB, 4 * slots * GQ * CH * HD, 4 * slots * CH * HD, tiles,
    )(queries, cache_keys.reshape(slots, CH, HD), cache_values.reshape(slots, CH, HD), info)
    attended = kernel_call(
        finish_kernel,
        S((peers, rows, GQ * HD), BF16),
        [VMEM, VMEM], 8 * MIB, 0, 8 * peers * rows * GQ * HD,
        [pltpu.VMEM((8, GQ * HD), F32), pltpu.VMEM((8, HD), F32)],
    )(exchange(partial), own)
    first = kernel_call(
        attention_out_kernel,
        S((requests, features), F32),
        [VMEM, VMEM], 8 * MIB, 2 * requests * GQ * HD * features, 2 * GQ * HD * features,
        [pltpu.VMEM((requests, GQ * HD), F32)],
    )(exchange(attended), attn_out_weight)
    one, two = all_but_last_sum(first)
    mixing, middle = kernel_call(
        mixing_kernel,
        (S((peers, rows, lin_width + HD), F32), S((requests, features), BF16)),
        [VMEM] * 6, 16 * MIB, 2 * requests * features * lin_width, 2 * features * lin_width,
    )(one, two, hidden_in, lin_gain[None, :], request, lin_weight)
    renewed, gated = kernel_call(
        lightning_kernel,
        (S(states.shape, F32), S((peers, rows, size + HD), BF16)),
        [VMEM] * 4, 16 * MIB, 0, 8 * rows * size * HD,
        [pltpu.VMEM((8, size), F32), pltpu.VMEM((8, lin_width), F32), pltpu.VMEM((2 * rows, HD), F32)],
    )(exchange(mixing), decay_rate[None, :], states, out_gain[None, :])
    second = kernel_call(
        lightning_out_kernel,
        S((requests + 8, features), F32),
        [VMEM] * 3, 8 * MIB, 2 * requests * size * features, 2 * size * features,
        [pltpu.VMEM((requests, size + HD), F32)],
    )(exchange(gated), request, lin_out_weight)
    one, two = all_but_last_sum(second)
    hidden_out = kernel_call(
        last_kernel,
        S((requests, features), BF16),
        [VMEM] * 3, 4 * MIB, 0, 16 * requests * features,
    )(one, two, middle)
    return hidden_out, renewed


def solution(mesh):
    placed = (
        P(None, "kv"),
        P("kv"),
        P("kv", "head"),
        P("head", "kv"),
        P("kv", "head", None, None),
        P("kv", "head", None, None),
        P(),
        P(),
        P("kv"),
        P("kv"),
        P("kv", "head"),
        P("head"),
        P("kv", "head", None, None),
        P("head"),
        P("head", "kv"),
        P(),
    )
    return jax.shard_map(
        per_device,
        mesh=mesh,
        in_specs=placed,
        out_specs=(P(None, "kv"), P("kv", "head", None, None)),
        check_vma=False,
    )
```

time: 464 us -> 142 us (0.31)
  waiting for transfers between devices: 197 us -> 16.8 us
  blocking collectives: 164 us -> 81.5 us
  other arithmetic: 39.1 us -> 0.06 us
  Pallas kernels: 0 us -> 24.1 us
  matrix products: 18.8 us -> 0 us
  local copies, waits for them, and re-layouts: 27.2 us -> 9.07 us
  between operations: 14.7 us -> 0.78 us
  starting transfers between devices: 0.21 us -> 8.83 us
    psum x3 -> x0, waiting for transfers between devices: 153 us -> none  [the longest x1 56.6 us: per_device(): first_out = lax.psum(first_part, 'head')]
    psum x3 -> x0, blocking collectives: 94.4 us -> none  [the longest x1 40.8 us: per_device(): lax.psum((jnp.dot(scaled, attn_weight, preferred_element_type=jnp.float32...]
    all_to_all x0 -> x6, blocking collectives: none -> 81.5 us  [exchange(): return lax.all_to_all(blocks, 'kv', 0, 0, tiled=True)]
    all_gather x3 -> x0, blocking collectives: 70 us -> none  [the longest x2 47.9 us: merged(): everything = jax.tree.map(lambda part: lax.all_gather(part, axis), shard)]
    unnamed x6 -> x0, waiting for transfers between devices: 43.7 us -> none
    pallas_call x0 -> x9, Pallas kernels: none -> 24.1 us  [the longest x1 17.3 us: per_device(): kernel_call(attention_kernel, S((peers, rows * (GQ + 2), HD), F32), [VMEM...]
    mul x36 -> x0, other arithmetic: 22.2 us -> none  [the longest x15 10.5 us: combine(): later[..., None] * second[2]]
    dot_general x10 -> x0, matrix products: 18.8 us -> none  [the longest x1 4.19 us: per_device(): jnp.einsum('skgd,sktd->skgt', picked, cache_keys, preferred_element_type=...]
  transfers between devices with their start and end apart: 5 -> 6, of which waited for: 4 -> 6; matrix products, arithmetic and copies ran while one was open for 2% -> 0% of each run, Pallas kernels for 0% -> 0%
where the time goes in v1:
time: 142 us; the launch traced here: 141 us
  blocking collectives  81.5 us (57%)
  Pallas kernels  24.1 us (17%)
  waiting for transfers between devices  16.8 us (12%)
  local copies, waits for them, and re-layouts  9.07 us (6%)
  starting transfers between devices  8.83 us (6%)
    all_to_all x6, blocking collectives, exchange(): return lax.all_to_all(blocks, 'kv', 0, 0, tiled=True)  81.5 us
    pallas_call x1, Pallas kernels, per_device(): kernel_call(attention_kernel, S((peers, rows * (GQ + 2), HD), F32), [VMEM...  17.3 us
    unnamed x32, local copies, waits for them, and re-layouts  8.39 us
    ppermute x2, waiting for transfers between devices, all_but_last_sum(): lax.ppermute(value, 'head', [(i, i ^ 2) for i in range(size)])  8.21 us
    ppermute x2, starting transfers between devices, all_but_last_sum(): return (value, lax.ppermute(value, 'head', last))  6.58 us
    ppermute x2, waiting for transfers between devices, all_but_last_sum(): return (value, lax.ppermute(value, 'head', last))  5.99 us
    pallas_call x1, Pallas kernels, per_device(): kernel_call(lightning_kernel, (S(states.shape, F32), S((peers, rows, size...  3.99 us
  transfers between devices with their start and end apart: 6, of which 6 were waited for; matrix products, arithmetic and copies ran while one was open for 0% of the time, Pallas kernels for 0%

profile of v1, /device:TPU:0, one launch (start us, length us, event | category | flops | bytes accessed | tf_op | source)
XLA Modules:
  0.0 141.2 jit_solution(11852914572452683915)
XLA Ops:
  0.6 0.7 broadcast_in_dim.24.gain
  1.3 0.0 copy-start.4
  1.3 1.2 copy-done.4
  2.5 0.0 copy-start.7
  2.5 0.8 copy-done.7
  3.3 0.0 copy-start.11
  3.3 0.7 copy-done.11
  4.0 0.0 copy-start.12
  4.0 0.7 copy-done.12
  4.6 0.0 copy-start.13
  4.6 0.7 copy-done.13
  5.3 0.3 shard_map.167
  5.6 16.7 %all_to_all.30.parts = f32[16,4,1408]{2,1,0:T(4,128)S(1)} all-to-all(f32[16,4,1408]{2,1,0:T(4,128)S(1)} %get-tuple-element.10), channel_id=1, replica_groups=mesh['kv'=16,'head'=8] {'kv'}, dimensions={0} | all-to-all | bytes 720896 | tf_op jit(solution)/shard_map/all_to_all | solution.py:273
  22.2 0.1 shard_map.168
  22.3 10.9 %all_to_all.31 = bf16[16,4,8,128]{3,2,1,0:T(8,128)(2,1)S(1)} all-to-all(bf16[16,4,8,128]{3,2,1,0:T(8,128)(2,1)S(1)} %get-tuple-element.11), channel_id=1, replica_groups=mesh['kv'=16,'head'=8] {'kv'}, dimensions={0} | all-to-all | bytes 262144 | tf_op jit(solution)/shard_map/all_to_all | solution.py:273
  33.2 0.0 copy-start
  33.2 2.2 %copy-done = bf16[64,1,256,128]{3,2,1,0:T(8,128)(2,1)S(1)} copy-done((bf16[64,1,256,128]{3,2,1,0:T(8,128)(2,1)S(1)}, bf16[64,1,256,128]{3,2,1,0:T(8,128)(2,1)}, u32[]{:S(2)}) %copy-start) | copy-done | bytes 4194328
  35.4 0.0 copy-start.1
  35.4 2.2 %copy-done.1 = bf16[64,1,256,128]{3,2,1,0:T(8,128)(2,1)S(1)} copy-done((bf16[64,1,256,128]{3,2,1,0:T(8,128)(2,1)S(1)}, bf16[64,1,256,128]{3,2,1,0:T(8,128)(2,1)}, u32[]{:S(2)}) %copy-start.1) | copy-done | bytes 4194328
  37.6 0.0 copy-start.5
  37.6 0.0 copy-start.2
  37.6 17.3 %shard_map.169 = f32[16,40,128]{2,1,0:T(8,128)S(1)} custom-call(bf16[64,8,128]{2,1,0:T(8,128)(2,1)S(1)} %bitcast.11, bf16[64,256,128]{2,1,0:T(8,128)(2,1)S(1)} %bitcast.9, bf16[64,256,128]{2,1,0:T(8,128)(2,1)S(1)} %bitcast.10, s32[2,64]{1,0:T(2,128)S(1)} %get-tuple-element.12.info), custom_call_target="tpu_custom_call" | custom-call | flops 67108864 | bytes 8388608 | tf_op jit(solution)/shard_map/pallas_call | solution.py:325
  54.9 0.0 copy-start.15
  54.9 0.0 copy-start.8
  54.9 0.0 copy-start.10
  54.9 12.2 %all_to_all.32.parts = f32[16,40,128]{2,1,0:T(8,128)S(1)} all-to-all(f32[16,40,128]{2,1,0:T(8,128)S(1)} %shard_map.169), channel_id=1, replica_groups=mesh['kv'=16,'head'=8] {'kv'}, dimensions={0} | all-to-all | bytes 655360 | tf_op jit(solution)/shard_map/all_to_all | solution.py:273
  67.1 0.3 shard_map.170
  67.4 10.9 %all_to_all.33.attended = bf16[16,4,1024]{2,1,0:T(4,128)(2,1)S(1)} all-to-all(bf16[16,4,1024]{2,1,0:T(4,128)(2,1)S(1)} %shard_map.170), channel_id=1, replica_groups=mesh['kv'=16,'head'=8] {'kv'}, dimensions={0} | all-to-all | bytes 262144 | tf_op jit(solution)/shard_map/all_to_all | solution.py:273
  78.3 0.0 copy-done.5
  78.3 0.3 shard_map.171
  78.5 0.1 collective-permute-start
  78.6 1.3 collective-permute-done
  79.9 2.0 %collective-permute-start.1 = (f32[64,384]{1,0:T(8,128)S(1)}, f32[64,384]{1,0:T(8,128)S(1)}, u32[]{:S(2)}, u32[]{:S(2)}) collective-permute-start(f32[64,384]{1,0:T(8,128)S(1)} %add.12), channel_id=1, source_target_pairs={{0,2},{1,3},{2,0},{3,1},{4,6},{5,7},{6,4},{7,5},{8,10},{9,11},{10,... | collective-permute-start | bytes 294920 | tf_op jit(solution)/shard_map/ppermute | solution.py:279
  81.9 3.1 %collective-permute-done.1 = f32[64,384]{1,0:T(8,128)S(1)} collective-permute-done((f32[64,384]{1,0:T(8,128)S(1)}, f32[64,384]{1,0:T(8,128)S(1)}, u32[]{:S(2)}, u32[]{:S(2)}) %collective-permute-start.1) | collective-permute-done | bytes 98336 | tf_op jit(solution)/shard_map/ppermute | solution.py:279
  85.1 3.9 %collective-permute-start.2 = (f32[64,384]{1,0:T(8,128)S(1)}, f32[64,384]{1,0:T(8,128)S(1)}, u32[]{:S(2)}, u32[]{:S(2)}) collective-permute-start(f32[64,384]{1,0:T(8,128)S(1)} %add.13.one), channel_id=1, source_target_pairs={{0,6},{1,7},{2,4},{3,5},{4,2},{5,3},{6,0},{7,1},{8,14},{9,15},{10,... | collective-permute-start | bytes 294920 | tf_op jit(solution)/shard_map/ppermute | solution.py:281
  89.0 0.0 copy-done.15
  89.0 2.6 %collective-permute-done.2.two = f32[64,384]{1,0:T(8,128)S(1)} collective-permute-done((f32[64,384]{1,0:T(8,128)S(1)}, f32[64,384]{1,0:T(8,128)S(1)}, u32[]{:S(2)}, u32[]{:S(2)}) %collective-permute-start.2) | collective-permute-done | bytes 98336 | tf_op jit(solution)/shard_map/ppermute | solution.py:281
  91.6 0.0 copy-done.2
  91.6 0.0 copy-done.8
  91.6 0.0 copy-done.10
  91.6 0.0 copy-start.3
  91.6 0.0 copy-start.9
  91.6 0.0 copy-start.14
  91.7 0.9 shard_map.172
  92.5 19.8 %all_to_all.34.parts = f32[16,4,4224]{2,1,0:T(4,128)S(1)} all-to-all(f32[16,4,4224]{2,1,0:T(4,128)S(1)} %get-tuple-element.14), channel_id=1, replica_groups=mesh['kv'=16,'head'=8] {'kv'}, dimensions={0} | all-to-all | bytes 2162688 | tf_op jit(solution)/shard_map/all_to_all | solution.py:273
  112.4 0.0 copy-start.6
  112.4 0.0 copy-done.3
  112.4 0.0 copy-done.9
  112.4 0.0 copy-done.14
  112.4 4.0 %shard_map.173 = (f32[4,8,128,128]{3,2,1,0:T(8,128)}, bf16[16,4,1152]{2,1,0:T(4,128)(2,1)S(1)}) custom-call(f32[16,4,4224]{2,1,0:T(4,128)S(1)} %all_to_all.34.parts, f32[1,8]{1,0:T(1,128)S(1)} %bitcast.18, f32[4,8,128,128]{3,2,1,0:T(8,128)S(1)} %copy-done.3, f32[1,1024]{1,0:T(1,128)S(1)} %bitcast.12), custom_call_target="tpu_custom_call" | custom-call | bytes 4194304 | tf_op jit(solution)/shard_map/pallas_call | solution.py:348
  116.4 11.1 %all_to_all.35.blocks = bf16[16,4,1152]{2,1,0:T(4,128)(2,1)S(1)} all-to-all(bf16[16,4,1152]{2,1,0:T(4,128)(2,1)S(1)} %get-tuple-element.15), channel_id=1, replica_groups=mesh['kv'=16,'head'=8] {'kv'}, dimensions={0} | all-to-all | bytes 294912 | tf_op jit(solution)/shard_map/all_to_all | solution.py:273
  127.4 0.0 copy-done.6
  127.4 0.4 shard_map.174
  127.8 0.1 collective-permute-start.3
  127.9 1.3 collective-permute-done.3
  129.2 0.1 collective-permute-start.4
  129.3 5.1 %collective-permute-done.4 = f32[72,384]{1,0:T(8,128)S(1)} collective-permute-done((f32[72,384]{1,0:T(8,128)S(1)}, f32[72,384]{1,0:T(8,128)S(1)}, u32[]{:S(2)}, u32[]{:S(2)}) %collective-permute-start.4) | collective-permute-done | bytes 110624 | tf_op jit(solution)/shard_map/ppermute | solution.py:279
  134.4 2.6 %collective-permute-start.5 = (f32[72,384]{1,0:T(8,128)S(1)}, f32[72,384]{1,0:T(8,128)S(1)}, u32[]{:S(2)}, u32[]{:S(2)}) collective-permute-start(f32[72,384]{1,0:T(8,128)S(1)} %add.15.one), channel_id=1, source_target_pairs={{0,6},{1,7},{2,4},{3,5},{4,2},{5,3},{6,0},{7,1},{8,14},{9,15},{10,... | collective-permute-start | bytes 331784 | tf_op jit(solution)/shard_map/ppermute | solution.py:281
  137.1 3.4 %collective-permute-done.5.two = f32[72,384]{1,0:T(8,128)S(1)} collective-permute-done((f32[72,384]{1,0:T(8,128)S(1)}, f32[72,384]{1,0:T(8,128)S(1)}, u32[]{:S(2)}, u32[]{:S(2)}) %collective-permute-start.5) | collective-permute-done | bytes 110624 | tf_op jit(solution)/shard_map/ppermute | solution.py:281
  140.5 0.7 shard_map.175
  (5 shorter events, 0.1 us)
Async XLA Ops:
  1.3 1.2 copy-start.4
  2.5 0.8 copy-start.7
  3.3 0.7 copy-start.11
  4.0 0.7 copy-start.12
  4.6 0.7 copy-start.13
  33.2 2.2 %copy-start = (bf16[64,1,256,128]{3,2,1,0:T(8,128)(2,1)S(1)}, bf16[64,1,256,128]{3,2,1,0:T(8,128)(2,1)}, u32[]{:S(2)}) copy-start(bf16[64,1,256,128]{3,2,1,0:T(8,128)(2,1)} %param.20) | copy-start | bytes 12582916
  35.4 2.2 %copy-start.1 = (bf16[64,1,256,128]{3,2,1,0:T(8,128)(2,1)S(1)}, bf16[64,1,256,128]{3,2,1,0:T(8,128)(2,1)}, u32[]{:S(2)}) copy-start(bf16[64,1,256,128]{3,2,1,0:T(8,128)(2,1)} %param.21) | copy-start | bytes 12582916
  37.6 40.7 %copy-start.5 = (bf16[1024,384]{1,0:T(8,128)(2,1)S(1)}, bf16[1024,384]{1,0:T(8,128)(2,1)}, u32[]{:S(2)}) copy-start(bf16[1024,384]{1,0:T(8,128)(2,1)} %weight.5) | copy-start | bytes 2359300
  37.6 54.0 %copy-start.2 = (bf16[384,4096]{1,0:T(8,128)(2,1)S(1)}, bf16[384,4096]{1,0:T(8,128)(2,1)}, u32[]{:S(2)}) copy-start(bf16[384,4096]{1,0:T(8,128)(2,1)} %weight.6) | copy-start | bytes 9437188
  54.9 34.1 %copy-start.15 = (f32[384]{0:T(512)S(1)}, f32[384]{0:T(512)}, u32[]{:S(2)}) copy-start(f32[384]{0:T(512)} %param.25) | copy-start | bytes 4612
  54.9 36.7 %copy-start.8 = (bf16[64,384]{1,0:T(8,128)(2,1)S(1)}, bf16[64,384]{1,0:T(8,128)(2,1)}, u32[]{:S(2)}) copy-start(bf16[64,384]{1,0:T(8,128)(2,1)} %hidden.3) | copy-start | bytes 147460
  54.9 36.7 %copy-start.10 = (s32[64]{0:T(128)S(1)}, s32[64]{0:T(128)}, u32[]{:S(2)}) copy-start(s32[64]{0:T(128)} %param.31) | copy-start | bytes 772
  78.5 1.4 collective-permute-start
  79.9 5.1 %collective-permute-start.1 = (f32[64,384]{1,0:T(8,128)S(1)}, f32[64,384]{1,0:T(8,128)S(1)}, u32[]{:S(2)}, u32[]{:S(2)}) collective-permute-start(f32[64,384]{1,0:T(8,128)S(1)} %add.12), channel_id=1, source_target_pairs={{0,2},{1,3},{2,0},{3,1},{4,6},{5,7},{6,4},{7,5},{8,10},{9,11},{10,... | collective-permute-start | bytes 294920 | tf_op jit(solution)/shard_map/ppermute | solution.py:279
  85.1 6.5 %collective-permute-start.2 = (f32[64,384]{1,0:T(8,128)S(1)}, f32[64,384]{1,0:T(8,128)S(1)}, u32[]{:S(2)}, u32[]{:S(2)}) collective-permute-start(f32[64,384]{1,0:T(8,128)S(1)} %add.13.one), channel_id=1, source_target_pairs={{0,6},{1,7},{2,4},{3,5},{4,2},{5,3},{6,0},{7,1},{8,14},{9,15},{10,... | collective-permute-start | bytes 294920 | tf_op jit(solution)/shard_map/ppermute | solution.py:281
  91.6 20.7 %copy-start.3 = (f32[4,8,128,128]{3,2,1,0:T(8,128)S(1)}, f32[4,8,128,128]{3,2,1,0:T(8,128)}, u32[]{:S(2)}) copy-start(f32[4,8,128,128]{3,2,1,0:T(8,128)} %states.1) | copy-start | bytes 6291460
  91.6 20.7 %copy-start.9 = (f32[1024]{0:T(1024)S(1)}, f32[1024]{0:T(1024)}, u32[]{:S(2)}) copy-start(f32[1024]{0:T(1024)} %param.29) | copy-start | bytes 12292
  91.6 20.7 %copy-start.14 = (f32[8]{0:T(128)S(1)}, f32[8]{0:T(128)}, u32[]{:S(2)}) copy-start(f32[8]{0:T(128)} %param.27) | copy-start | bytes 100
  112.4 15.1 %copy-start.6 = (bf16[1024,384]{1,0:T(8,128)(2,1)S(1)}, bf16[1024,384]{1,0:T(8,128)(2,1)}, u32[]{:S(2)}) copy-start(bf16[1024,384]{1,0:T(8,128)(2,1)} %weight.7) | copy-start | bytes 2359300
  127.8 1.4 collective-permute-start.3
  129.2 5.2 %collective-permute-start.4 = (f32[72,384]{1,0:T(8,128)S(1)}, f32[72,384]{1,0:T(8,128)S(1)}, u32[]{:S(2)}, u32[]{:S(2)}) collective-permute-start(f32[72,384]{1,0:T(8,128)S(1)} %add.14), channel_id=1, source_target_pairs={{0,2},{1,3},{2,0},{3,1},{4,6},{5,7},{6,4},{7,5},{8,10},{9,11},{10,... | collective-permute-start | bytes 331784 | tf_op jit(solution)/shard_map/ppermute | solution.py:279
  134.4 6.0 %collective-permute-start.5 = (f32[72,384]{1,0:T(8,128)S(1)}, f32[72,384]{1,0:T(8,128)S(1)}, u32[]{:S(2)}, u32[]{:S(2)}) collective-permute-start(f32[72,384]{1,0:T(8,128)S(1)} %add.15.one), channel_id=1, source_target_pairs={{0,6},{1,7},{2,4},{3,5},{4,2},{5,3},{6,0},{7,1},{8,14},{9,15},{10,... | collective-permute-start | bytes 331784 | tf_op jit(solution)/shard_map/ppermute | solution.py:281

commit v2 on v1

--- a/solution.py
+++ b/solution.py
@@ -51,19 +51,56 @@
 
 VMEM = pl.BlockSpec(memory_space=pltpu.VMEM)
 SMEM = pl.BlockSpec(memory_space=pltpu.SMEM)
-
-
-def project_kernel(hidden, gain, weight, counts, tails, slots, out, info):
+HBM = pl.BlockSpec(memory_space=pltpu.HBM)
+
+
+def in_hbm(value):
+    return pltpu.with_memory_space_constraint(value, pltpu.HBM)
+
+
+def project_kernel(hidden_hbm, gain_hbm, weight_hbm, counts, tails, slots, out, hidden, gain, weight, sems):
+    chunks = gain.shape[0]
+    copies = [
+        pltpu.make_async_copy(hidden_hbm, hidden, sems.at[0]),
+        pltpu.make_async_copy(gain_hbm, gain, sems.at[1]),
+    ]
+    blocks = [
+        pltpu.make_async_copy(
+            weight_hbm.at[c * HD:(c + 1) * HD, :], weight.at[c * HD:(c + 1) * HD, :], sems.at[2 + c]
+        )
+        for c in range(chunks)
+    ]
+    for copy in copies + blocks:
+        copy.start()
+    for copy in copies:
+        copy.wait()
     x = hidden[...].astype(F32)
-    scaled = (x * gain[...]).astype(BF16)
     squares = jnp.sum(x * x, axis=1, keepdims=True)
-    y = jnp.dot(scaled, weight[...], preferred_element_type=F32)
+    y = jnp.zeros((x.shape[0], weight.shape[1]), F32)
+    for c in range(chunks):
+        scaled = (x[:, c * HD:(c + 1) * HD] * gain[c:c + 1, :]).astype(BF16)
+        blocks[c].wait()
+        y = y + jnp.dot(scaled, weight[c * HD:(c + 1) * HD, :], preferred_element_type=F32)
     groups, rows, _ = out.shape
     width = weight.shape[1]
     wide = jnp.broadcast_to(squares, (x.shape[0], HD))
     for p in range(groups):
         out[p, :, :width] = y[p * rows:(p + 1) * rows]
         out[p, :, width:] = wide[p * rows:(p + 1) * rows]
+
+
+def normalise_kernel(parts, counts, tails, slots, keys, values, out, own, info):
+    total = parts[0]
+    for p in range(1, parts.shape[0]):
+        total = total + parts[p]
+    width = own.shape[1] * HD
+    mean = total[:, width:width + 1] / D
+    projected = (total[:, :width] / jnp.sqrt(mean + EPS)).astype(BF16).astype(F32)
+    for g in range(own.shape[1]):
+        own[:, g, :] = projected[:, g * HD:(g + 1) * HD]
+    queries = own[:, :GQ, :].astype(BF16)
+    for p in range(out.shape[0]):
+        out[p] = queries
     number = counts[...]
     n = number.shape[1]
     below = iota((n, n), 1) <= iota((n, n), 0)
@@ -81,20 +118,6 @@
     info[1:2, :] = jnp.where(owner < n, live, 0)
 
 
-def normalise_kernel(parts, out, own):
-    total = parts[0]
-    for p in range(1, parts.shape[0]):
-        total = total + parts[p]
-    width = own.shape[1] * HD
-    mean = total[:, width:width + 1] / D
-    projected = (total[:, :width] / jnp.sqrt(mean + EPS)).astype(BF16).astype(F32)
-    for g in range(own.shape[1]):
-        own[:, g, :] = projected[:, g * HD:(g + 1) * HD]
-    queries = own[:, :GQ, :].astype(BF16)
-    for p in range(out.shape[0]):
-        out[p] = queries
-
-
 def attention_kernel(queries, keys, values, info, out, slot_max, slot_sum, slot_value, best, summed, mixed):
     slots = keys.shape[0]
     rows = out.shape[1] // (GQ + 2)
@@ -103,34 +126,42 @@
     mixed[...] = jnp.zeros(mixed.shape, F32)
     token = iota((GQ, CH), 1)
     scale = 1.0 / math.sqrt(HD)
-    batch = 8
+    batch = 32
 
     @pl.loop(0, slots, step=batch)
     def _(base):
-        for u in range(batch):
-            s = base + u
-            owner = info[0, s]
-            q = queries[jnp.minimum(owner, REQ - 1)]
-            scores = lax.dot_general(
-                q, keys[s], (((1,), (1,)), ((), ())), preferred_element_type=F32
+        span = [base + u for u in range(batch)]
+        scores = [
+            lax.dot_general(
+                queries[jnp.minimum(info[0, s], REQ - 1)], keys[s], (((1,), (1,)), ((), ())),
+                preferred_element_type=F32,
             ) * scale
-            live = token < info[1, s]
-            top = jnp.max(jnp.where(live, scores, NEGATIVE), axis=1, keepdims=True)
-            weights = jnp.where(live, jnp.exp(scores - top), 0.0)
-            slot_sum[s] = jnp.broadcast_to(jnp.sum(weights, axis=1, keepdims=True), (GQ, HD))
+            for s in span
+        ]
+        live = [token < info[1, s] for s in span]
+        scores = [jnp.where(m, x, NEGATIVE) for m, x in zip(live, scores)]
+        tops = [jnp.max(x, axis=1, keepdims=True) for x in scores]
+        weights = [jnp.where(m, jnp.exp(x - t), 0.0) for m, x, t in zip(live, scores, tops)]
+        totals = [jnp.sum(w, axis=1, keepdims=True) for w in weights]
+        mixes = [
+            jnp.dot(w.astype(BF16), values[s], preferred_element_type=F32) for w, s in zip(weights, span)
+        ]
+        for s, top, total, mix in zip(span, tops, totals, mixes):
             slot_max[s] = jnp.broadcast_to(top, (GQ, HD))
-            slot_value[s] = jnp.dot(weights.astype(BF16), values[s], preferred_element_type=F32)
-
-    @pl.loop(0, slots, step=batch)
+            slot_sum[s] = jnp.broadcast_to(total, (GQ, HD))
+            slot_value[s] = mix
+
+    step = 8
+
+    @pl.loop(0, slots, step=step)
     def _(base):
-        for u in range(batch):
-            s = base + u
-            r = info[0, s]
-            best[r] = jnp.maximum(best[r], slot_max[s])
-
-    @pl.loop(0, slots, step=batch)
+        for u in range(step):
+            r = info[0, base + u]
+            best[r] = jnp.maximum(best[r], slot_max[base + u])
+
+    @pl.loop(0, slots, step=step)
     def _(base):
-        for u in range(batch):
+        for u in range(step):
             s = base + u
             r = info[0, s]
             factor = jnp.exp(slot_max[s] - best[r])
@@ -193,61 +224,85 @@
     out[...] = jnp.dot(flat[...].astype(BF16), weight[...], preferred_element_type=F32)
 
 
-def mixing_kernel(one, two, hidden, gain, request, weight, out, middle):
-    total = hidden[...].astype(F32) + (one[...] + two[...])
+def mixing_kernel(own, near, far, cross, hidden, gain, request, weight, out, middle, turned):
+    total = hidden[...].astype(F32) + ((own[...] + near[...]) + (far[...] + cross[...]))
     inner = total.astype(BF16)
     middle[...] = inner
     n = request.shape[1]
     pick = (as_column(request[...]) == iota((n, n), 1)).astype(F32).astype(BF16)
     ordered = jnp.dot(pick, inner, preferred_element_type=F32)
-    squares = jnp.broadcast_to(jnp.sum(ordered * ordered, axis=1, keepdims=True), (n, HD))
-    scaled = (ordered * gain[...]).astype(BF16)
-    groups, rows, _ = out.shape
+    squares = jnp.sum(ordered * ordered, axis=1, keepdims=True)
+    upper = squares.astype(BF16).astype(F32)
+    scaled = jnp.concatenate(
+        [(ordered[:, c * HD:(c + 1) * HD] * gain[c:c + 1, :]).astype(BF16) for c in range(gain.shape[0])], axis=1
+    )
+    groups, height, _ = out.shape
+    rows = n // groups
     width = weight.shape[1]
-    step = 512
-    for c in range(0, width, step):
-        y = jnp.dot(scaled, weight[:, c:c + step], preferred_element_type=F32)
+    used = rows * (width // HD)
+    step = 4
+    for c in range(0, width // HD, step):
+        y = jnp.dot(scaled, weight[:, c * HD:(c + step) * HD], preferred_element_type=F32)
         for p in range(groups):
-            out[p, :, c:c + step] = y[p * rows:(p + 1) * rows].astype(out.dtype)
+            for k in range(step):
+                turned[p, k * rows:(k + 1) * rows, :] = y[p * rows:(p + 1) * rows, k * HD:(k + 1) * HD]
+        for p in range(groups):
+            out[p, c * rows:(c + step) * rows, :] = turned[p].astype(BF16)
+    lane, sub = iota((rows, HD), 1), iota((rows, HD), 0)
     for p in range(groups):
-        out[p, :, width:] = squares[p * rows:(p + 1) * rows].astype(out.dtype)
-
-
-def lightning_kernel(parts, decay, states, gain, renewed, out, flat, mixing, columns):
+        at = slice(p * rows, (p + 1) * rows)
+        both = jnp.where(lane == sub, upper[at], 0.0) + jnp.where(lane == sub + rows, (squares - upper)[at], 0.0)
+        line = jnp.sum(both, axis=0, keepdims=True)
+        out[p, used:, :] = jnp.where(iota((height - used, HD), 0) == 0, line, 0.0).astype(BF16)
+
+
+def lightning_kernel(parts, decay, states, gain, out, turned, mixed, flat):
+    rows, heads = states.shape[0], states.shape[1]
+    used = 4 * rows * heads
     total = parts[0].astype(F32)
     for p in range(1, parts.shape[0]):
         total = total + parts[p].astype(F32)
-    rows, heads = states.shape[0], states.shape[1]
-    width = heads * 4 * HD
-    mixing[0:rows, :] = total[:, :width] / jnp.sqrt(total[:, width:width + 1] / D + EPS)
+    line = total[used:used + 1, :]
+    sums = line + pltpu.roll(line, HD - rows, axis=1)
+    block = 4 * rows
+    pattern = iota((block, HD), 1) == lax.rem(iota((block, HD), 0), rows)
+    squares = jnp.sum(jnp.where(pattern, sums, 0.0), axis=1, keepdims=True)
+    scale = jnp.sqrt(squares / D + EPS)
     keep_row = jnp.exp(-decay[...])
-    squares = jnp.zeros((rows, 1), F32)
+    read_squares = jnp.zeros((rows, 1), F32)
     for h in range(heads):
-        at = h * 4 * HD
-        mixed = [mixing[0:rows, at + k * HD:at + (k + 1) * HD] for k in range(4)]
-        gate = 1.0 / (1.0 + jnp.exp(-mixed[3]))
-        query, key, value = (m / (1.0 + jnp.exp(-m)) for m in mixed[:3])
-        columns[0:rows, :] = query
-        columns[rows:2 * rows, :] = key
-        turned = columns[...].T
+        mixing = total[block * h:block * (h + 1), :] / scale
+        below = 1.0 + jnp.exp(-mixing)
+        mixed[h] = mixing / below
+        gate = 1.0 / below[3 * rows:, :]
+        query, key, value = (mixed[h, k * rows:(k + 1) * rows, :] for k in range(3))
+        turned[h] = mixed[h, :2 * rows, :].T
         inner = jnp.sum(query * key, axis=1, keepdims=True)
         keep = keep_row[:, h:h + 1]
         for j in range(rows):
-            state = keep * states[j, h]
-            renewed[j, h] = state + turned[:, rows + j:rows + j + 1] * value[j:j + 1, :]
-            read = jnp.sum(turned[:, j:j + 1] * state, axis=0, keepdims=True)
-            flat[j:j + 1, h * HD:(h + 1) * HD] = read + inner[j:j + 1, :] * value[j:j + 1, :]
+            read = jnp.sum(turned[h, :, j:j + 1] * states[j, h], axis=0, keepdims=True)
+            flat[j:j + 1, h * HD:(h + 1) * HD] = keep * read + inner[j:j + 1, :] * value[j:j + 1, :]
         read = flat[0:rows, h * HD:(h + 1) * HD]
-        squares = squares + jnp.sum(read * read, axis=1, keepdims=True)
-        flat[0:rows, h * HD:(h + 1) * HD] = read * gain[:, h * HD:(h + 1) * HD] * gate
+        read_squares = read_squares + jnp.sum(read * read, axis=1, keepdims=True)
+        flat[0:rows, h * HD:(h + 1) * HD] = read * gain[h:h + 1, :] * gate
     size = heads * HD
     gated = flat[0:rows, 0:size].astype(BF16)
-    upper = squares.astype(BF16).astype(F32)
+    upper = read_squares.astype(BF16).astype(F32)
     lane = iota((rows, HD), 1)
-    tail = jnp.where(lane == 0, upper, jnp.where(lane == 1, squares - upper, 0.0)).astype(BF16)
+    tail = jnp.where(lane == 0, upper, jnp.where(lane == 1, read_squares - upper, 0.0)).astype(BF16)
     for p in range(out.shape[0]):
         out[p, :, :size] = gated
         out[p, :, size:] = tail
+
+
+def renew_kernel(turned, mixed, decay, states, renewed):
+    rows, heads = states.shape[0], states.shape[1]
+    keep_row = jnp.exp(-decay[...])
+    for h in range(heads):
+        keep = keep_row[:, h:h + 1]
+        for j in range(rows):
+            value = mixed[h, 2 * rows + j:2 * rows + j + 1, :]
+            renewed[j, h] = keep * states[j, h] + turned[h, :, rows + j:rows + j + 1] * value
 
 
 def lightning_out_kernel(blocks, request, weight, out, flat):
@@ -262,23 +317,25 @@
     out[n:n + 1, 0:n] = squares
 
 
-def last_kernel(one, two, middle, out):
+def last_kernel(own, near, far, cross, middle, out):
     n = middle.shape[0]
-    squares = as_column(one[n:n + 1, 0:n] + two[n:n + 1, 0:n])
+    total = (own[...] + near[...]) + (far[...] + cross[...])
+    squares = as_column(total[n:n + 1, 0:n])
     scale = 1.0 / jnp.sqrt(squares / (LH * HD) + EPS)
-    out[...] = (middle[...].astype(F32) + (one[0:n, :] + two[0:n, :]) * scale).astype(BF16)
+    out[...] = (middle[...].astype(F32) + total[0:n, :] * scale).astype(BF16)
 
 
 def exchange(blocks):
     return lax.all_to_all(blocks, "kv", 0, 0, tiled=True)
 
 
-def all_but_last_sum(value):
+def head_parts(value):
     size = lax.axis_size("head")
     value = value + lax.ppermute(value, "head", [(i, i ^ 1) for i in range(size)])
-    value = value + lax.ppermute(value, "head", [(i, i ^ 2) for i in range(size)])
-    last = [(i, (3 - i // 2) * 2 + i % 2) for i in range(size)]
-    return value, lax.ppermute(value, "head", last)
+    near = lax.ppermute(value, "head", [(i, i ^ 2) for i in range(size)])
+    far = lax.ppermute(value, "head", [(i, (3 - i // 2) * 2 + i % 2) for i in range(size)])
+    cross = lax.ppermute(value, "head", [(i, i ^ 4) for i in range(size)])
+    return value, near, far, cross
 
 
 def per_device(
@@ -310,23 +367,39 @@
     S = jax.ShapeDtypeStruct
     request = state_request[None, :]
 
-    parts, info = kernel_call(
+    chunks = features // HD
+    keys = cache_keys.reshape(slots, CH, HD)
+    values = cache_values.reshape(slots, CH, HD)
+    plan = stretch_counts[None, :], tail_tokens[None, :], slot_stretch[None, :]
+
+    parts = kernel_call(
         project_kernel,
-        (S((peers, rows, width + HD), F32), S((2, slots), jnp.int32)),
-        [VMEM] * 6, 8 * MIB, 2 * requests * features * width, 2 * features * width,
-    )(hidden_in, attn_gain[None, :], attn_weight, stretch_counts[None, :], tail_tokens[None, :], slot_stretch[None, :])
-    queries, own = kernel_call(
+        S((peers, rows, width + HD), F32),
+        [HBM] * 6, 8 * MIB, 2 * requests * features * width, 2 * features * width,
+        [
+            pltpu.VMEM((requests, features), BF16),
+            pltpu.VMEM((chunks, HD), F32),
+            pltpu.VMEM((features, width), BF16),
+            pltpu.SemaphoreType.DMA((2 + chunks,)),
+        ],
+    )(
+        in_hbm(hidden_in), in_hbm(attn_gain.reshape(chunks, HD)), in_hbm(attn_weight),
+        *(in_hbm(row) for row in plan),
+    )
+    queries, own, info = kernel_call(
         normalise_kernel,
-        (S((peers, rows, GQ, HD), BF16), S((rows, GQ + 2, HD), F32)),
-        [VMEM], 8 * MIB, 0, 8 * peers * rows * width,
-    )(exchange(parts))
+        (S((peers, rows, GQ, HD), BF16), S((rows, GQ + 2, HD), F32), S((2, slots), jnp.int32)),
+        [VMEM] * 4 + [HBM] * 2, 8 * MIB, 0, 8 * peers * rows * width,
+    )(
+        exchange(parts), *plan, in_hbm(keys), in_hbm(values)
+    )
     queries = exchange(queries).reshape(requests, GQ, HD)
     tiles = [pltpu.VMEM((slots, GQ, HD), F32)] * 3 + [pltpu.VMEM((requests + 1, GQ, HD), F32)] * 3
     partial = kernel_call(
         attention_kernel,
         S((peers, rows * (GQ + 2), HD), F32),
         [VMEM, VMEM, VMEM, SMEM], 24 * MIB, 4 * slots * GQ * CH * HD, 4 * slots * CH * HD, tiles,
-    )(queries, cache_keys.reshape(slots, CH, HD), cache_values.reshape(slots, CH, HD), info)
+    )(queries, keys, values, info)
     attended = kernel_call(
         finish_kernel,
         S((peers, rows, GQ * HD), BF16),
@@ -339,30 +412,38 @@
         [VMEM, VMEM], 8 * MIB, 2 * requests * GQ * HD * features, 2 * GQ * HD * features,
         [pltpu.VMEM((requests, GQ * HD), F32)],
     )(exchange(attended), attn_out_weight)
-    one, two = all_but_last_sum(first)
+    height = rows * (lin_width // HD) + 16
     mixing, middle = kernel_call(
         mixing_kernel,
-        (S((peers, rows, lin_width + HD), F32), S((requests, features), BF16)),
-        [VMEM] * 6, 16 * MIB, 2 * requests * features * lin_width, 2 * features * lin_width,
-    )(one, two, hidden_in, lin_gain[None, :], request, lin_weight)
-    renewed, gated = kernel_call(
+        (S((peers, height, HD), BF16), S((requests, features), BF16)),
+        [VMEM] * 8, 16 * MIB, 2 * requests * features * lin_width, 2 * features * lin_width,
+        [pltpu.VMEM((peers, 4 * rows, HD), F32)],
+    )(*head_parts(first), hidden_in, lin_gain.reshape(chunks, HD), request, lin_weight)
+    decay = decay_rate[None, :]
+    gated, turned, mixed = kernel_call(
         lightning_kernel,
-        (S(states.shape, F32), S((peers, rows, size + HD), BF16)),
+        (
+            S((peers, rows, size + HD), BF16),
+            S((heads, HD, 2 * rows), F32),
+            S((heads, 4 * rows, HD), F32),
+        ),
         [VMEM] * 4, 16 * MIB, 0, 8 * rows * size * HD,
-        [pltpu.VMEM((8, size), F32), pltpu.VMEM((8, lin_width), F32), pltpu.VMEM((2 * rows, HD), F32)],
-    )(exchange(mixing), decay_rate[None, :], states, out_gain[None, :])
+        [pltpu.VMEM((8, size), F32)],
+    )(exchange(mixing), decay, states, out_gain.reshape(heads, HD))
     second = kernel_call(
         lightning_out_kernel,
         S((requests + 8, features), F32),
         [VMEM] * 3, 8 * MIB, 2 * requests * size * features, 2 * size * features,
         [pltpu.VMEM((requests, size + HD), F32)],
     )(exchange(gated), request, lin_out_weight)
-    one, two = all_but_last_sum(second)
+    renewed = kernel_call(
+        renew_kernel, S(states.shape, F32), [VMEM] * 4, 8 * MIB, 0, 8 * rows * size * HD,
+    )(turned, mixed, decay, states)
     hidden_out = kernel_call(
         last_kernel,
         S((requests, features), BF16),
-        [VMEM] * 3, 4 * MIB, 0, 16 * requests * features,
-    )(one, two, middle)
+        [VMEM] * 5, 4 * MIB, 0, 16 * requests * features,
+    )(*head_parts(second), middle)
     return hidden_out, renewed
 
 

time: 142 us -> 112 us (0.79)
  Pallas kernels: 24.1 us -> 11.5 us
  local copies, waits for them, and re-layouts: 9.07 us -> 2.02 us
  waiting for transfers between devices: 16.8 us -> 11.1 us
  blocking collectives: 81.5 us -> 77 us
    pallas_call x1, Pallas kernels: 17.3 us -> 3.18 us  [per_device(): kernel_call(attention_kernel, S((peers, rows * (GQ + 2), HD), F32), [VMEM...]
    unnamed x32 -> x28, local copies, waits for them, and re-layouts: 8.39 us -> 2.02 us
    ppermute x6 -> x8, waiting for transfers between devices: 16.8 us -> 11.1 us  [the longest x2 4.92 us: head_parts(): lax.ppermute(value, 'head', [(i, (3 - i // 2) * 2 + i % 2) for i in range...]
    all_to_all x6, blocking collectives: 81.5 us -> 77 us  [exchange(): return lax.all_to_all(blocks, 'kv', 0, 0, tiled=True)]
    pallas_call x4 -> x5, Pallas kernels: 5.85 us -> 7.2 us  [the longest x1 1.99 us: per_device(): kernel_call(renew_kernel, S(states.shape, F32), [VMEM] * 4, 8 * MIB, 0, 8...]
    ppermute x6 -> x8, starting transfers between devices: 8.83 us -> 9.33 us  [the longest x2 6.31 us: head_parts(): cross = lax.ppermute(value, 'head', [(i, i ^ 4) for i in range(size)])]
  transfers between devices with their start and end apart: 6 -> 8, of which waited for: 6 -> 8; matrix products, arithmetic and copies ran while one was open for 0% -> 0% of each run, Pallas kernels for 0% -> 2%
where the time goes in v2:
time: 112 us
  blocking collectives  77 us (69%)
  Pallas kernels  11.5 us (10%)
  waiting for transfers between devices  11.1 us (10%)
  starting transfers between devices  9.33 us (8%)
  local copies, waits for them, and re-layouts  2.02 us (2%)
    all_to_all x6, blocking collectives, exchange(): return lax.all_to_all(blocks, 'kv', 0, 0, tiled=True)  77 us
    ppermute x2, starting transfers between devices, head_parts(): cross = lax.ppermute(value, 'head', [(i, i ^ 4) for i in range(size)])  6.31 us
    ppermute x2, waiting for transfers between devices, head_parts(): lax.ppermute(value, 'head', [(i, (3 - i // 2) * 2 + i % 2) for i in range...  4.92 us
    pallas_call x1, Pallas kernels, per_device(): kernel_call(attention_kernel, S((peers, rows * (GQ + 2), HD), F32), [VMEM...  3.18 us
    ppermute x2, waiting for transfers between devices, head_parts(): cross = lax.ppermute(value, 'head', [(i, i ^ 4) for i in range(size)])  2.77 us
    ppermute x2, waiting for transfers between devices, head_parts(): lax.ppermute(value, 'head', [(i, i ^ 1) for i in range(size)])  2.59 us
  transfers between devices with their start and end apart: 8, of which 8 were waited for; matrix products, arithmetic and copies ran while one was open for 0% of the time, Pallas kernels for 2%

profile of v2, /device:TPU:0, one launch (start us, length us, event | category | flops | bytes accessed | tf_op | source)
XLA Modules:
  0.0 111.7 jit_solution(9013043288054333460)
XLA Ops:
  0.6 1.6 %shard_map.167 = f32[16,4,1408]{2,1,0:T(4,128)S(1)} custom-call(bf16[64,384]{1,0:T(8,128)(2,1)} %hidden.1, f32[3,128]{1,0:T(4,128)} %bitcast.28, bf16[384,1280]{1,0:T(8,128)(2,1)} %weight_hbm.1, s32[1,64]{1,0:T(1,128)} %bitcast.18, s32[1,64]{1,0:T(1,128)} %bitcast.20, s32[1,64]{1,0:T(1,128)} %bitcast.22), custom_call_target="tpu_custom_call" | custom-call | flops 62914560 | bytes 983040 | tf_op jit(solution)/shard_map/pallas_call | solution.py:375
  2.2 16.7 %all_to_all.30.parts = f32[16,4,1408]{2,1,0:T(4,128)S(1)} all-to-all(f32[16,4,1408]{2,1,0:T(4,128)S(1)} %shard_map.167), channel_id=1, replica_groups=mesh['kv'=16,'head'=8] {'kv'}, dimensions={0} | all-to-all | bytes 720896 | tf_op jit(solution)/shard_map/all_to_all | solution.py:329
  18.9 0.0 copy-start.9
  18.9 0.7 copy-done.9
  19.5 0.0 copy-start.10
  19.5 0.7 copy-done.10
  20.2 0.0 copy-start.11
  20.2 0.7 copy-done.11
  20.9 0.0 copy-start
  20.9 0.0 copy-start.1
  20.9 0.2 shard_map.168
  21.0 11.1 %all_to_all.31 = bf16[16,4,8,128]{3,2,1,0:T(8,128)(2,1)S(1)} all-to-all(bf16[16,4,8,128]{3,2,1,0:T(8,128)(2,1)S(1)} %get-tuple-element.10), channel_id=1, replica_groups=mesh['kv'=16,'head'=8] {'kv'}, dimensions={0} | all-to-all | bytes 262144 | tf_op jit(solution)/shard_map/all_to_all | solution.py:329
  32.2 0.0 copy-done
  32.2 0.0 copy-done.1
  32.2 0.0 copy-start.4
  32.2 0.0 copy-start.3
  32.2 0.0 copy-start.6
  32.2 0.0 copy-start.8
  32.2 0.0 copy-start.12
  32.2 3.2 %shard_map.169 = f32[16,40,128]{2,1,0:T(8,128)S(1)} custom-call(bf16[64,8,128]{2,1,0:T(8,128)(2,1)S(1)} %bitcast.15, bf16[64,256,128]{2,1,0:T(8,128)(2,1)S(1)} %bitcast.12, bf16[64,256,128]{2,1,0:T(8,128)(2,1)S(1)} %bitcast.14, s32[2,64]{1,0:T(2,128)S(1)} %get-tuple-element.11.info), custom_call_target="tpu_custom_call" | custom-call | flops 67108864 | bytes 8388608 | tf_op jit(solution)/shard_map/pallas_call | solution.py:398
  35.4 12.1 %all_to_all.32.parts = f32[16,40,128]{2,1,0:T(8,128)S(1)} all-to-all(f32[16,40,128]{2,1,0:T(8,128)S(1)} %shard_map.169), channel_id=1, replica_groups=mesh['kv'=16,'head'=8] {'kv'}, dimensions={0} | all-to-all | bytes 655360 | tf_op jit(solution)/shard_map/all_to_all | solution.py:329
  47.5 0.3 shard_map.170
  47.8 0.0 copy-start.2
  47.8 0.0 copy-start.7
  47.8 0.0 copy-start.13
  47.9 11.0 %all_to_all.33.attended = bf16[16,4,1024]{2,1,0:T(4,128)(2,1)S(1)} all-to-all(bf16[16,4,1024]{2,1,0:T(4,128)(2,1)S(1)} %shard_map.170), channel_id=1, replica_groups=mesh['kv'=16,'head'=8] {'kv'}, dimensions={0} | all-to-all | bytes 262144 | tf_op jit(solution)/shard_map/all_to_all | solution.py:329
  58.8 0.0 copy-done.4
  58.8 0.3 shard_map.171
  59.1 0.1 collective-permute-start
  59.2 1.3 %collective-permute-done = f32[64,384]{1,0:T(8,128)S(1)} collective-permute-done((f32[64,384]{1,0:T(8,128)S(1)}, f32[64,384]{1,0:T(8,128)S(1)}, u32[]{:S(2)}, u32[]{:S(2)}) %collective-permute-start) | collective-permute-done | bytes 98336 | tf_op jit(solution)/shard_map/ppermute | solution.py:334
  60.5 4.0 %collective-permute-start.3 = (f32[64,384]{1,0:T(8,128)S(1)}, f32[64,384]{1,0:T(8,128)S(1)}, u32[]{:S(2)}, u32[]{:S(2)}) collective-permute-start(f32[64,384]{1,0:T(8,128)S(1)} %add.6.own), channel_id=1, source_target_pairs={{0,4},{1,5},{2,6},{3,7},{4,0},{5,1},{6,2},{7,3},{8,12},{9,13},{10,... | collective-permute-start | bytes 294920 | tf_op jit(solution)/shard_map/ppermute | solution.py:337
  64.5 0.7 collective-permute-start.2
  65.2 0.3 collective-permute-start.1
  65.5 2.2 %collective-permute-done.3.cross = f32[64,384]{1,0:T(8,128)S(1)} collective-permute-done((f32[64,384]{1,0:T(8,128)S(1)}, f32[64,384]{1,0:T(8,128)S(1)}, u32[]{:S(2)}, u32[]{:S(2)}) %collective-permute-start.3) | collective-permute-done | bytes 98336 | tf_op jit(solution)/shard_map/ppermute | solution.py:337
  67.7 2.6 %collective-permute-done.2.far = f32[64,384]{1,0:T(8,128)S(1)} collective-permute-done((f32[64,384]{1,0:T(8,128)S(1)}, f32[64,384]{1,0:T(8,128)S(1)}, u32[]{:S(2)}, u32[]{:S(2)}) %collective-permute-start.2) | collective-permute-done | bytes 98336 | tf_op jit(solution)/shard_map/ppermute | solution.py:336
  70.3 0.2 collective-permute-done.1.near
  70.5 0.0 copy-done.3
  70.5 0.0 copy-done.6
  70.5 0.0 copy-done.8
  70.5 0.0 copy-done.12
  70.5 0.0 copy-start.5
  70.5 0.9 shard_map.172
  71.4 14.8 %all_to_all.34.parts = bf16[16,144,128]{2,1,0:T(8,128)(2,1)S(1)} all-to-all(bf16[16,144,128]{2,1,0:T(8,128)(2,1)S(1)} %get-tuple-element.13), channel_id=1, replica_groups=mesh['kv'=16,'head'=8] {'kv'}, dimensions={0} | all-to-all | bytes 1179648 | tf_op jit(solution)/shard_map/all_to_all | solution.py:329
  86.3 0.0 copy-done.2
  86.3 0.0 copy-done.7
  86.3 0.0 copy-done.13
  86.3 2.0 %shard_map.173 = (bf16[16,4,1152]{2,1,0:T(4,128)(2,1)S(1)}, f32[8,128,8]{2,1,0:T(8,128)S(1)}, f32[8,16,128]{2,1,0:T(8,128)S(1)}) custom-call(bf16[16,144,128]{2,1,0:T(8,128)(2,1)S(1)} %all_to_all.34.parts, f32[1,8]{1,0:T(1,128)S(1)} %bitcast.26, f32[4,8,128,128]{3,2,1,0:T(8,128)S(1)} %copy-done.2, f32[8,128]{1,0:T(8,128)S(1)} %bitcast.16), custom_call_target="tpu_custom_call" | custom-call | bytes 4194304 | tf_op jit(solution)/shard_map/pallas_call | solution.py:423
  88.2 11.2 %all_to_all.35.blocks = bf16[16,4,1152]{2,1,0:T(4,128)(2,1)S(1)} all-to-all(bf16[16,4,1152]{2,1,0:T(4,128)(2,1)S(1)} %get-tuple-element.14), channel_id=1, replica_groups=mesh['kv'=16,'head'=8] {'kv'}, dimensions={0} | all-to-all | bytes 294912 | tf_op jit(solution)/shard_map/all_to_all | solution.py:329
  99.5 0.0 copy-done.5
  99.5 0.4 shard_map.174
  99.9 0.1 collective-permute-start.4
  100.0 1.3 %collective-permute-done.4 = f32[72,384]{1,0:T(8,128)S(1)} collective-permute-done((f32[72,384]{1,0:T(8,128)S(1)}, f32[72,384]{1,0:T(8,128)S(1)}, u32[]{:S(2)}, u32[]{:S(2)}) %collective-permute-start.4) | collective-permute-done | bytes 110624 | tf_op jit(solution)/shard_map/ppermute | solution.py:334
  101.3 2.4 %collective-permute-start.7 = (f32[72,384]{1,0:T(8,128)S(1)}, f32[72,384]{1,0:T(8,128)S(1)}, u32[]{:S(2)}, u32[]{:S(2)}) collective-permute-start(f32[72,384]{1,0:T(8,128)S(1)} %add.7.own), channel_id=1, source_target_pairs={{0,4},{1,5},{2,6},{3,7},{4,0},{5,1},{6,2},{7,3},{8,12},{9,13},{10,... | collective-permute-start | bytes 331784 | tf_op jit(solution)/shard_map/ppermute | solution.py:337
  103.6 1.5 %collective-permute-start.6 = (f32[72,384]{1,0:T(8,128)S(1)}, f32[72,384]{1,0:T(8,128)S(1)}, u32[]{:S(2)}, u32[]{:S(2)}) collective-permute-start(f32[72,384]{1,0:T(8,128)S(1)} %add.7.own), channel_id=1, source_target_pairs={{0,6},{1,7},{2,4},{3,5},{4,2},{5,3},{6,0},{7,1},{8,14},{9,15},{10,... | collective-permute-start | bytes 331784 | tf_op jit(solution)/shard_map/ppermute | solution.py:336
  105.1 0.4 collective-permute-start.5
  105.5 2.0 %shard_map.176 = f32[4,8,128,128]{3,2,1,0:T(8,128)} custom-call(f32[8,128,8]{2,1,0:T(8,128)S(1)} %get-tuple-element.16.turned, f32[8,16,128]{2,1,0:T(8,128)S(1)} %get-tuple-element.17.mixed, f32[1,8]{1,0:T(1,128)S(1)} %bitcast.27, f32[4,8,128,128]{3,2,1,0:T(8,128)S(1)} %copy-done.2), custom_call_target="tpu_custom_call" | custom-call | bytes 4194304 | tf_op jit(solution)/shard_map/pallas_call | solution.py:439
  107.5 0.6 collective-permute-done.7.cross
  108.1 2.3 %collective-permute-done.6.far = f32[72,384]{1,0:T(8,128)S(1)} collective-permute-done((f32[72,384]{1,0:T(8,128)S(1)}, f32[72,384]{1,0:T(8,128)S(1)}, u32[]{:S(2)}, u32[]{:S(2)}) %collective-permute-start.6) | collective-permute-done | bytes 110624 | tf_op jit(solution)/shard_map/ppermute | solution.py:336
  110.4 0.6 collective-permute-done.5.near
  111.0 0.7 shard_map.175
  (2 shorter events, 0.0 us)
Async XLA Ops:
  18.9 0.7 copy-start.9
  19.5 0.7 copy-start.10
  20.2 0.7 copy-start.11
  20.9 11.3 %copy-start = (bf16[64,1,256,128]{3,2,1,0:T(8,128)(2,1)S(1)}, bf16[64,1,256,128]{3,2,1,0:T(8,128)(2,1)}, u32[]{:S(2)}) copy-start(bf16[64,1,256,128]{3,2,1,0:T(8,128)(2,1)} %param.20) | copy-start | bytes 12582916
  20.9 11.3 %copy-start.1 = (bf16[64,1,256,128]{3,2,1,0:T(8,128)(2,1)S(1)}, bf16[64,1,256,128]{3,2,1,0:T(8,128)(2,1)}, u32[]{:S(2)}) copy-start(bf16[64,1,256,128]{3,2,1,0:T(8,128)(2,1)} %param.21) | copy-start | bytes 12582916
  32.2 26.7 %copy-start.4 = (bf16[1024,384]{1,0:T(8,128)(2,1)S(1)}, bf16[1024,384]{1,0:T(8,128)(2,1)}, u32[]{:S(2)}) copy-start(bf16[1024,384]{1,0:T(8,128)(2,1)} %weight.3) | copy-start | bytes 2359300
  32.2 38.3 %copy-start.3 = (bf16[384,4096]{1,0:T(8,128)(2,1)S(1)}, bf16[384,4096]{1,0:T(8,128)(2,1)}, u32[]{:S(2)}) copy-start(bf16[384,4096]{1,0:T(8,128)(2,1)} %weight.4) | copy-start | bytes 9437188
  32.2 38.3 %copy-start.6 = (bf16[64,384]{1,0:T(8,128)(2,1)S(1)}, bf16[64,384]{1,0:T(8,128)(2,1)}, u32[]{:S(2)}) copy-start(bf16[64,384]{1,0:T(8,128)(2,1)} %hidden.1) | copy-start | bytes 147460
  32.2 38.3 %copy-start.8 = (f32[384]{0:T(512)S(1)}, f32[384]{0:T(512)}, u32[]{:S(2)}) copy-start(f32[384]{0:T(512)} %param.25) | copy-start | bytes 4612
  32.2 38.3 %copy-start.12 = (s32[64]{0:T(128)S(1)}, s32[64]{0:T(128)}, u32[]{:S(2)}) copy-start(s32[64]{0:T(128)} %param.31) | copy-start | bytes 772
  47.8 38.4 %copy-start.2 = (f32[4,8,128,128]{3,2,1,0:T(8,128)S(1)}, f32[4,8,128,128]{3,2,1,0:T(8,128)}, u32[]{:S(2)}) copy-start(f32[4,8,128,128]{3,2,1,0:T(8,128)} %states.3) | copy-start | bytes 6291460
  47.8 38.4 %copy-start.7 = (f32[1024]{0:T(1024)S(1)}, f32[1024]{0:T(1024)}, u32[]{:S(2)}) copy-start(f32[1024]{0:T(1024)} %param.29) | copy-start | bytes 12292
  47.8 38.4 %copy-start.13 = (f32[8]{0:T(128)S(1)}, f32[8]{0:T(128)}, u32[]{:S(2)}) copy-start(f32[8]{0:T(128)} %param.27) | copy-start | bytes 100
  59.1 1.4 %collective-permute-start = (f32[64,384]{1,0:T(8,128)S(1)}, f32[64,384]{1,0:T(8,128)S(1)}, u32[]{:S(2)}, u32[]{:S(2)}) collective-permute-start(f32[64,384]{1,0:T(8,128)S(1)} %shard_map.171), channel_id=1, source_target_pairs={{0,1},{1,0},{2,3},{3,2},{4,5},{5,4},{6,7},{7,6},{8,9},{9,8},{10,11... | collective-permute-start | bytes 294920 | tf_op jit(solution)/shard_map/ppermute | solution.py:334
  60.5 7.2 %collective-permute-start.3 = (f32[64,384]{1,0:T(8,128)S(1)}, f32[64,384]{1,0:T(8,128)S(1)}, u32[]{:S(2)}, u32[]{:S(2)}) collective-permute-start(f32[64,384]{1,0:T(8,128)S(1)} %add.6.own), channel_id=1, source_target_pairs={{0,4},{1,5},{2,6},{3,7},{4,0},{5,1},{6,2},{7,3},{8,12},{9,13},{10,... | collective-permute-start | bytes 294920 | tf_op jit(solution)/shard_map/ppermute | solution.py:337
  64.5 5.8 %collective-permute-start.2 = (f32[64,384]{1,0:T(8,128)S(1)}, f32[64,384]{1,0:T(8,128)S(1)}, u32[]{:S(2)}, u32[]{:S(2)}) collective-permute-start(f32[64,384]{1,0:T(8,128)S(1)} %add.6.own), channel_id=1, source_target_pairs={{0,6},{1,7},{2,4},{3,5},{4,2},{5,3},{6,0},{7,1},{8,14},{9,15},{10,... | collective-permute-start | bytes 294920 | tf_op jit(solution)/shard_map/ppermute | solution.py:336
  65.2 5.3 %collective-permute-start.1 = (f32[64,384]{1,0:T(8,128)S(1)}, f32[64,384]{1,0:T(8,128)S(1)}, u32[]{:S(2)}, u32[]{:S(2)}) collective-permute-start(f32[64,384]{1,0:T(8,128)S(1)} %add.6.own), channel_id=1, source_target_pairs={{0,2},{1,3},{2,0},{3,1},{4,6},{5,7},{6,4},{7,5},{8,10},{9,11},{10,... | collective-permute-start | bytes 294920 | tf_op jit(solution)/shard_map/ppermute | solution.py:335
  70.5 29.0 %copy-start.5 = (bf16[1024,384]{1,0:T(8,128)(2,1)S(1)}, bf16[1024,384]{1,0:T(8,128)(2,1)}, u32[]{:S(2)}) copy-start(bf16[1024,384]{1,0:T(8,128)(2,1)} %weight.5) | copy-start | bytes 2359300
  99.9 1.4 %collective-permute-start.4 = (f32[72,384]{1,0:T(8,128)S(1)}, f32[72,384]{1,0:T(8,128)S(1)}, u32[]{:S(2)}, u32[]{:S(2)}) collective-permute-start(f32[72,384]{1,0:T(8,128)S(1)} %shard_map.174), channel_id=1, source_target_pairs={{0,1},{1,0},{2,3},{3,2},{4,5},{5,4},{6,7},{7,6},{8,9},{9,8},{10,11... | collective-permute-start | bytes 331784 | tf_op jit(solution)/shard_map/ppermute | solution.py:334
  101.3 6.8 %collective-permute-start.7 = (f32[72,384]{1,0:T(8,128)S(1)}, f32[72,384]{1,0:T(8,128)S(1)}, u32[]{:S(2)}, u32[]{:S(2)}) collective-permute-start(f32[72,384]{1,0:T(8,128)S(1)} %add.7.own), channel_id=1, source_target_pairs={{0,4},{1,5},{2,6},{3,7},{4,0},{5,1},{6,2},{7,3},{8,12},{9,13},{10,... | collective-permute-start | bytes 331784 | tf_op jit(solution)/shard_map/ppermute | solution.py:337
  103.6 6.7 %collective-permute-start.6 = (f32[72,384]{1,0:T(8,128)S(1)}, f32[72,384]{1,0:T(8,128)S(1)}, u32[]{:S(2)}, u32[]{:S(2)}) collective-permute-start(f32[72,384]{1,0:T(8,128)S(1)} %add.7.own), channel_id=1, source_target_pairs={{0,6},{1,7},{2,4},{3,5},{4,2},{5,3},{6,0},{7,1},{8,14},{9,15},{10,... | collective-permute-start | bytes 331784 | tf_op jit(solution)/shard_map/ppermute | solution.py:336
  105.1 5.9 %collective-permute-start.5 = (f32[72,384]{1,0:T(8,128)S(1)}, f32[72,384]{1,0:T(8,128)S(1)}, u32[]{:S(2)}, u32[]{:S(2)}) collective-permute-start(f32[72,384]{1,0:T(8,128)S(1)} %add.7.own), channel_id=1, source_target_pairs={{0,2},{1,3},{2,0},{3,1},{4,6},{5,7},{6,4},{7,5},{8,10},{9,11},{10,... | collective-permute-start | bytes 331784 | tf_op jit(solution)/shard_map/ppermute | solution.py:335

commit v3 on v2

--- a/solution.py
+++ b/solution.py
@@ -58,29 +58,51 @@
     return pltpu.with_memory_space_constraint(value, pltpu.HBM)
 
 
-def project_kernel(hidden_hbm, gain_hbm, weight_hbm, counts, tails, slots, out, hidden, gain, weight, sems):
+def halves(value):
+    upper = value.astype(BF16).astype(F32)
+    return upper, (value - upper).astype(BF16).astype(F32)
+
+
+def project_kernel(
+    hidden_hbm, gain_hbm, weight_hbm, counts_hbm, tails_hbm, slots_hbm, out, info,
+    hidden, gain, weight, counts, tails, slots, sems,
+):
     chunks = gain.shape[0]
+    first = [(hidden_hbm, hidden), (gain_hbm, gain)]
+    blocks = [
+        (weight_hbm.at[c * HD:(c + 1) * HD, :], weight.at[c * HD:(c + 1) * HD, :]) for c in range(chunks)
+    ]
+    last = [(counts_hbm, counts), (tails_hbm, tails), (slots_hbm, slots)]
     copies = [
-        pltpu.make_async_copy(hidden_hbm, hidden, sems.at[0]),
-        pltpu.make_async_copy(gain_hbm, gain, sems.at[1]),
+        pltpu.make_async_copy(source, target, sems.at[k])
+        for k, (source, target) in enumerate(first + blocks + last)
     ]
-    blocks = [
-        pltpu.make_async_copy(
-            weight_hbm.at[c * HD:(c + 1) * HD, :], weight.at[c * HD:(c + 1) * HD, :], sems.at[2 + c]
-        )
-        for c in range(chunks)
-    ]
-    for copy in copies + blocks:
+    for copy in copies:
         copy.start()
-    for copy in copies:
+    for copy in copies[:2] + copies[2 + chunks:]:
         copy.wait()
     x = hidden[...].astype(F32)
     squares = jnp.sum(x * x, axis=1, keepdims=True)
+    scaled = [(x[:, c * HD:(c + 1) * HD] * gain[c:c + 1, :]).astype(BF16) for c in range(chunks)]
+    number = counts[...]
+    n = number.shape[1]
+    below = iota((n, n), 1) <= iota((n, n), 0)
+    ends = jnp.sum(jnp.where(below, number, 0), axis=1, keepdims=True)
+    count = as_column(number)
+    starts = ends - count
+    limits = count * CH - as_column(tails[...])
+    slot = slots[...]
+    owner = jnp.sum((slot >= ends).astype(jnp.int32), axis=0, keepdims=True)
+    hits = iota((n, slot.shape[1]), 0) == owner
+    begin = jnp.sum(jnp.where(hits, starts, 0), axis=0, keepdims=True)
+    limit = jnp.sum(jnp.where(hits, limits, 0), axis=0, keepdims=True)
+    live = jnp.clip(limit - (slot - begin) * CH, 0, CH)
+    info[0:1, :] = owner
+    info[1:2, :] = jnp.where(owner < n, live, 0)
     y = jnp.zeros((x.shape[0], weight.shape[1]), F32)
     for c in range(chunks):
-        scaled = (x[:, c * HD:(c + 1) * HD] * gain[c:c + 1, :]).astype(BF16)
-        blocks[c].wait()
-        y = y + jnp.dot(scaled, weight[c * HD:(c + 1) * HD, :], preferred_element_type=F32)
+        copies[2 + c].wait()
+        y = y + jnp.dot(scaled[c], weight[c * HD:(c + 1) * HD, :], preferred_element_type=F32)
     groups, rows, _ = out.shape
     width = weight.shape[1]
     wide = jnp.broadcast_to(squares, (x.shape[0], HD))
@@ -89,7 +111,7 @@
         out[p, :, width:] = wide[p * rows:(p + 1) * rows]
 
 
-def normalise_kernel(parts, counts, tails, slots, keys, values, out, own, info):
+def normalise_kernel(parts, keys, values, out, own):
     total = parts[0]
     for p in range(1, parts.shape[0]):
         total = total + parts[p]
@@ -101,26 +123,11 @@
     queries = own[:, :GQ, :].astype(BF16)
     for p in range(out.shape[0]):
         out[p] = queries
-    number = counts[...]
-    n = number.shape[1]
-    below = iota((n, n), 1) <= iota((n, n), 0)
-    ends = jnp.sum(jnp.where(below, number, 0), axis=1, keepdims=True)
-    count = as_column(number)
-    starts = ends - count
-    limits = count * CH - as_column(tails[...])
-    slot = slots[...]
-    owner = jnp.sum((slot >= ends).astype(jnp.int32), axis=0, keepdims=True)
-    hits = iota((n, slot.shape[1]), 0) == owner
-    first = jnp.sum(jnp.where(hits, starts, 0), axis=0, keepdims=True)
-    limit = jnp.sum(jnp.where(hits, limits, 0), axis=0, keepdims=True)
-    live = jnp.clip(limit - (slot - first) * CH, 0, CH)
-    info[0:1, :] = owner
-    info[1:2, :] = jnp.where(owner < n, live, 0)
 
 
 def attention_kernel(queries, keys, values, info, out, slot_max, slot_sum, slot_value, best, summed, mixed):
     slots = keys.shape[0]
-    rows = out.shape[1] // (GQ + 2)
+    rows = REQ // out.shape[0]
     best[...] = jnp.full(best.shape, NEGATIVE, F32)
     summed[...] = jnp.zeros(summed.shape, F32)
     mixed[...] = jnp.zeros(mixed.shape, F32)
@@ -131,12 +138,13 @@
     @pl.loop(0, slots, step=batch)
     def _(base):
         span = [base + u for u in range(batch)]
+        owners = [info[0, s] for s in span]
         scores = [
             lax.dot_general(
-                queries[jnp.minimum(info[0, s], REQ - 1)], keys[s], (((1,), (1,)), ((), ())),
+                queries[jnp.minimum(r, REQ - 1)], keys[s], (((1,), (1,)), ((), ())),
                 preferred_element_type=F32,
             ) * scale
-            for s in span
+            for r, s in zip(owners, span)
         ]
         live = [token < info[1, s] for s in span]
         scores = [jnp.where(m, x, NEGATIVE) for m, x in zip(live, scores)]
@@ -146,18 +154,16 @@
         mixes = [
             jnp.dot(w.astype(BF16), values[s], preferred_element_type=F32) for w, s in zip(weights, span)
         ]
-        for s, top, total, mix in zip(span, tops, totals, mixes):
-            slot_max[s] = jnp.broadcast_to(top, (GQ, HD))
+        for r, s, top, total, mix in zip(owners, span, tops, totals, mixes):
+            wide = jnp.broadcast_to(top, (GQ, HD))
+            best[r] = jnp.maximum(best[r], wide)
+            slot_max[s] = wide
             slot_sum[s] = jnp.broadcast_to(total, (GQ, HD))
             slot_value[s] = mix
 
+    upper, lower = halves(best[...])
+    best[...] = upper + lower
     step = 8
-
-    @pl.loop(0, slots, step=step)
-    def _(base):
-        for u in range(step):
-            r = info[0, base + u]
-            best[r] = jnp.maximum(best[r], slot_max[base + u])
 
     @pl.loop(0, slots, step=step)
     def _(base):
@@ -169,14 +175,19 @@
             mixed[r] = mixed[r] + factor * slot_value[s]
 
     lane, sub = iota((GQ, HD), 1), iota((GQ, HD), 0)
+    line = iota((2 * GQ, HD), 0)
 
     @pl.loop(0, out.shape[0])
     def _(p):
+        stats = jnp.zeros((2 * GQ, HD), F32)
         for i in range(rows):
             r = p * rows + i
-            out[p, i * GQ:(i + 1) * GQ, :] = mixed[r]
-            packed = jnp.where(lane == sub, best[r], 0.0) + jnp.where(lane == sub + GQ, summed[r], 0.0)
-            out[p, rows * GQ + i:rows * GQ + i + 1, :] = jnp.sum(packed, axis=0, keepdims=True)
+            packed = jnp.zeros((GQ, HD), F32)
+            for k, part in enumerate(halves(best[r]) + halves(summed[r])):
+                packed = jnp.where(lane == sub + k * GQ, part, packed)
+            stats = jnp.where(line == i, jnp.sum(packed, axis=0, keepdims=True), stats)
+        out[p, :rows * GQ, :] = mixed[pl.ds(p * rows, rows)].reshape(rows * GQ, HD).astype(BF16)
+        out[p, rows * GQ:, :] = stats.astype(BF16)
 
 
 def finish_kernel(parts, own, out, flat, fresh_rows):
@@ -187,25 +198,28 @@
         fresh = jnp.sum(own[i, :GQ, :] * own[i, GQ:GQ + 1, :], axis=1, keepdims=True) / math.sqrt(HD)
         fresh_rows[i:i + 1, :] = jnp.sum(jnp.where(diagonal, fresh, 0.0), axis=0, keepdims=True)
     fresh = fresh_rows[0:rows, :]
-    stats = [parts[p, rows * GQ:rows * GQ + rows, :] for p in range(peers)]
+    lines = [parts[p, rows * GQ:, :].astype(F32)[0:rows] for p in range(peers)]
+    tops = [x + pltpu.roll(x, HD - GQ, axis=1) for x in lines]
+    sums = [pltpu.roll(x, HD - 2 * GQ, axis=1) for x in tops]
     top = fresh
     for p in range(peers):
-        top = jnp.maximum(top, stats[p])
+        top = jnp.maximum(top, tops[p])
     latest = jnp.exp(fresh - top)
     below = latest
-    factors = []
+    factors = [jnp.exp(x - top) for x in tops]
     for p in range(peers):
-        factor = jnp.exp(stats[p] - top)
-        below = below + factor * pltpu.roll(stats[p], HD - GQ, axis=1)
-        factors.append(factor)
+        below = below + factors[p] * sums[p]
+
+    def column(value, i):
+        return jnp.sum(jnp.where(diagonal, value[i:i + 1, :], 0.0), axis=1, keepdims=True)
+
+    above = [column(latest, i) * own[i, GQ + 1:GQ + 2, :] for i in range(rows)]
+    for p in range(peers):
+        values = parts[p, :rows * GQ, :].astype(F32)
+        for i in range(rows):
+            above[i] = above[i] + column(factors[p], i) * values[i * GQ:(i + 1) * GQ]
     for i in range(rows):
-        def column(value):
-            return jnp.sum(jnp.where(diagonal, value[i:i + 1, :], 0.0), axis=1, keepdims=True)
-
-        above = column(latest) * own[i, GQ + 1:GQ + 2, :]
-        for p in range(peers):
-            above = above + column(factors[p]) * parts[p, i * GQ:(i + 1) * GQ, :]
-        result = above / column(below)
+        result = above[i] / column(below, i)
         for g in range(GQ):
             flat[i:i + 1, g * HD:(g + 1) * HD] = result[g:g + 1, :]
     attended = flat[0:rows, :].astype(BF16)
@@ -219,13 +233,17 @@
         flat[p * rows:(p + 1) * rows, :] = blocks[p].astype(F32)
 
 
+def four(own, near, far, cross):
+    return (own[...].astype(F32) + near[...].astype(F32)) + (far[...].astype(F32) + cross[...].astype(F32))
+
+
 def attention_out_kernel(attended, weight, out, flat):
     stacked(attended, flat)
     out[...] = jnp.dot(flat[...].astype(BF16), weight[...], preferred_element_type=F32)
 
 
 def mixing_kernel(own, near, far, cross, hidden, gain, request, weight, out, middle, turned):
-    total = hidden[...].astype(F32) + ((own[...] + near[...]) + (far[...] + cross[...]))
+    total = hidden[...].astype(F32) + four(own, near, far, cross)
     inner = total.astype(BF16)
     middle[...] = inner
     n = request.shape[1]
@@ -268,28 +286,32 @@
     pattern = iota((block, HD), 1) == lax.rem(iota((block, HD), 0), rows)
     squares = jnp.sum(jnp.where(pattern, sums, 0.0), axis=1, keepdims=True)
     scale = jnp.sqrt(squares / D + EPS)
-    keep_row = jnp.exp(-decay[...])
+    keep = jnp.exp(-decay[...])
+    span = range(heads)
+    mixing = [total[block * h:block * (h + 1), :] / scale for h in span]
+    below = [1.0 + jnp.exp(-m) for m in mixing]
+    silu = [m / b for m, b in zip(mixing, below)]
+    gates = [1.0 / b[3 * rows:] for b in below]
+    columns = [v[:2 * rows].T for v in silu]
+    for h in span:
+        mixed[h] = silu[h]
+        turned[h] = columns[h]
+    inner = [jnp.sum(v[:rows] * v[rows:2 * rows], axis=1, keepdims=True) for v in silu]
+    for j in range(rows):
+        for h in span:
+            read = jnp.sum(columns[h][:, j:j + 1] * states[j, h], axis=0, keepdims=True)
+            flat[j:j + 1, h * HD:(h + 1) * HD] = read
     read_squares = jnp.zeros((rows, 1), F32)
-    for h in range(heads):
-        mixing = total[block * h:block * (h + 1), :] / scale
-        below = 1.0 + jnp.exp(-mixing)
-        mixed[h] = mixing / below
-        gate = 1.0 / below[3 * rows:, :]
-        query, key, value = (mixed[h, k * rows:(k + 1) * rows, :] for k in range(3))
-        turned[h] = mixed[h, :2 * rows, :].T
-        inner = jnp.sum(query * key, axis=1, keepdims=True)
-        keep = keep_row[:, h:h + 1]
-        for j in range(rows):
-            read = jnp.sum(turned[h, :, j:j + 1] * states[j, h], axis=0, keepdims=True)
-            flat[j:j + 1, h * HD:(h + 1) * HD] = keep * read + inner[j:j + 1, :] * value[j:j + 1, :]
-        read = flat[0:rows, h * HD:(h + 1) * HD]
+    for h in span:
+        at = slice(h * HD, (h + 1) * HD)
+        read = keep[:, h:h + 1] * flat[0:rows, at] + inner[h] * silu[h][2 * rows:3 * rows]
         read_squares = read_squares + jnp.sum(read * read, axis=1, keepdims=True)
-        flat[0:rows, h * HD:(h + 1) * HD] = read * gain[h:h + 1, :] * gate
+        flat[0:rows, at] = read * gain[h:h + 1, :] * gates[h]
     size = heads * HD
     gated = flat[0:rows, 0:size].astype(BF16)
-    upper = read_squares.astype(BF16).astype(F32)
+    upper, lower = halves(read_squares)
     lane = iota((rows, HD), 1)
-    tail = jnp.where(lane == 0, upper, jnp.where(lane == 1, read_squares - upper, 0.0)).astype(BF16)
+    tail = jnp.where(lane == 0, upper, jnp.where(lane == 1, lower, 0.0)).astype(BF16)
     for p in range(out.shape[0]):
         out[p, :, :size] = gated
         out[p, :, size:] = tail
@@ -317,10 +339,19 @@
     out[n:n + 1, 0:n] = squares
 
 
+def pair_kernel(own, near, out):
+    n = own.shape[0] - 8
+    total = own[...] + near[...]
+    out[0:n, :] = total[0:n].astype(BF16)
+    upper, lower = halves(total[n:n + 1])
+    line = iota((out.shape[0] - n, out.shape[1]), 0)
+    out[n:, :] = jnp.where(line == 0, upper, jnp.where(line == 1, lower, 0.0)).astype(BF16)
+
+
 def last_kernel(own, near, far, cross, middle, out):
     n = middle.shape[0]
-    total = (own[...] + near[...]) + (far[...] + cross[...])
-    squares = as_column(total[n:n + 1, 0:n])
+    total = four(own, near, far, cross)
+    squares = as_column(total[n:n + 1, 0:n] + total[n + 1:n + 2, 0:n])
     scale = 1.0 / jnp.sqrt(squares / (LH * HD) + EPS)
     out[...] = (middle[...].astype(F32) + total[0:n, :] * scale).astype(BF16)
 
@@ -329,9 +360,12 @@
     return lax.all_to_all(blocks, "kv", 0, 0, tiled=True)
 
 
-def head_parts(value):
+def other_core(value):
+    return lax.ppermute(value, "head", [(i, i ^ 1) for i in range(lax.axis_size("head"))])
+
+
+def along_z(value):
     size = lax.axis_size("head")
-    value = value + lax.ppermute(value, "head", [(i, i ^ 1) for i in range(size)])
     near = lax.ppermute(value, "head", [(i, i ^ 2) for i in range(size)])
     far = lax.ppermute(value, "head", [(i, (3 - i // 2) * 2 + i % 2) for i in range(size)])
     cross = lax.ppermute(value, "head", [(i, i ^ 4) for i in range(size)])
@@ -372,32 +406,35 @@
     values = cache_values.reshape(slots, CH, HD)
     plan = stretch_counts[None, :], tail_tokens[None, :], slot_stretch[None, :]
 
-    parts = kernel_call(
+    parts, info = kernel_call(
         project_kernel,
-        S((peers, rows, width + HD), F32),
+        (S((peers, rows, width + HD), F32), S((2, slots), jnp.int32)),
         [HBM] * 6, 8 * MIB, 2 * requests * features * width, 2 * features * width,
         [
             pltpu.VMEM((requests, features), BF16),
             pltpu.VMEM((chunks, HD), F32),
             pltpu.VMEM((features, width), BF16),
-            pltpu.SemaphoreType.DMA((2 + chunks,)),
+            pltpu.VMEM((1, requests), jnp.int32),
+            pltpu.VMEM((1, requests), jnp.int32),
+            pltpu.VMEM((1, slots), jnp.int32),
+            pltpu.SemaphoreType.DMA((5 + chunks,)),
         ],
     )(
         in_hbm(hidden_in), in_hbm(attn_gain.reshape(chunks, HD)), in_hbm(attn_weight),
         *(in_hbm(row) for row in plan),
     )
-    queries, own, info = kernel_call(
+    queries, own = kernel_call(
         normalise_kernel,
-        (S((peers, rows, GQ, HD), BF16), S((rows, GQ + 2, HD), F32), S((2, slots), jnp.int32)),
-        [VMEM] * 4 + [HBM] * 2, 8 * MIB, 0, 8 * peers * rows * width,
+        (S((peers, rows, GQ, HD), BF16), S((rows, GQ + 2, HD), F32)),
+        [VMEM] + [HBM] * 2, 8 * MIB, 0, 8 * peers * rows * width,
     )(
-        exchange(parts), *plan, in_hbm(keys), in_hbm(values)
+        exchange(parts), in_hbm(keys), in_hbm(values)
     )
     queries = exchange(queries).reshape(requests, GQ, HD)
     tiles = [pltpu.VMEM((slots, GQ, HD), F32)] * 3 + [pltpu.VMEM((requests + 1, GQ, HD), F32)] * 3
     partial = kernel_call(
         attention_kernel,
-        S((peers, rows * (GQ + 2), HD), F32),
+        S((peers, rows * GQ + 16, HD), BF16),
         [VMEM, VMEM, VMEM, SMEM], 24 * MIB, 4 * slots * GQ * CH * HD, 4 * slots * CH * HD, tiles,
     )(queries, keys, values, info)
     attended = kernel_call(
@@ -418,7 +455,7 @@
         (S((peers, height, HD), BF16), S((requests, features), BF16)),
         [VMEM] * 8, 16 * MIB, 2 * requests * features * lin_width, 2 * features * lin_width,
         [pltpu.VMEM((peers, 4 * rows, HD), F32)],
-    )(*head_parts(first), hidden_in, lin_gain.reshape(chunks, HD), request, lin_weight)
+    )(*along_z((first + other_core(first)).astype(BF16)), hidden_in, lin_gain.reshape(chunks, HD), request, lin_weight)
     decay = decay_rate[None, :]
     gated, turned, mixed = kernel_call(
         lightning_kernel,
@@ -436,6 +473,9 @@
         [VMEM] * 3, 8 * MIB, 2 * requests * size * features, 2 * size * features,
         [pltpu.VMEM((requests, size + HD), F32)],
     )(exchange(gated), request, lin_out_weight)
+    pair = kernel_call(
+        pair_kernel, S((requests + 16, features), BF16), [VMEM] * 2, 4 * MIB, 0, 16 * requests * features,
+    )(second, other_core(second))
     renewed = kernel_call(
         renew_kernel, S(states.shape, F32), [VMEM] * 4, 8 * MIB, 0, 8 * rows * size * HD,
     )(turned, mixed, decay, states)
@@ -443,7 +483,7 @@
         last_kernel,
         S((requests, features), BF16),
         [VMEM] * 5, 4 * MIB, 0, 16 * requests * features,
-    )(*head_parts(second), middle)
+    )(*along_z(pair), middle)
     return hidden_out, renewed
 
 

time: 112 us -> 105 us (0.938)
  waiting for transfers between devices: 11.1 us -> 8.7 us
  local copies, waits for them, and re-layouts: 2.02 us -> 0.05 us
  blocking collectives: 77 us -> 75.8 us
    ppermute x8, waiting for transfers between devices: 11.1 us -> 8.7 us  [the longest x2 4.8 us: along_z(): lax.ppermute(value, 'head', [(i, (3 - i // 2) * 2 + i % 2) for i in range...]
    unnamed x28 -> x22, local copies, waits for them, and re-layouts: 2.02 us -> 0.05 us
    all_to_all x6, blocking collectives: 77 us -> 75.8 us  [exchange(): return lax.all_to_all(blocks, 'kv', 0, 0, tiled=True)]
    pallas_call x2 -> x3, Pallas kernels: 4.78 us -> 4.89 us  [the longest x1 3.17 us: per_device(): kernel_call(attention_kernel, S((peers, rows * GQ + 16, HD), BF16), [VMEM...]
  transfers between devices with their start and end apart: 8 -> 8, of which waited for: 8 -> 6; matrix products, arithmetic and copies ran while one was open for 0% -> 0% of each run, Pallas kernels for 2% -> 2%
where the time goes in v3:
time: 105 us
  blocking collectives  75.8 us (72%)
  Pallas kernels  10.9 us (10%)
  starting transfers between devices  8.72 us (8%)
  waiting for transfers between devices  8.7 us (8%)
    all_to_all x6, blocking collectives, exchange(): return lax.all_to_all(blocks, 'kv', 0, 0, tiled=True)  75.8 us
    ppermute x2, starting transfers between devices, along_z(): cross = lax.ppermute(value, 'head', [(i, i ^ 4) for i in range(size)])  5.92 us
    ppermute x2, waiting for transfers between devices, along_z(): lax.ppermute(value, 'head', [(i, (3 - i // 2) * 2 + i % 2) for i in range...  4.8 us
    pallas_call x1, Pallas kernels, per_device(): kernel_call(attention_kernel, S((peers, rows * GQ + 16, HD), BF16), [VMEM...  3.17 us
    ppermute x2, waiting for transfers between devices, other_core(): lax.ppermute(value, 'head', [(i, i ^ 1) for i in range(lax.axis_size('hea...  2.59 us
  transfers between devices with their start and end apart: 8, of which 6 were waited for; matrix products, arithmetic and copies ran while one was open for 0% of the time, Pallas kernels for 2%

profile of v3, /device:TPU:0, one launch (start us, length us, event | category | flops | bytes accessed | tf_op | source)
XLA Modules:
  0.0 105.0 jit_solution(4555382678459397518)
XLA Ops:
  0.6 1.7 %shard_map.167 = (f32[16,4,1408]{2,1,0:T(4,128)S(1)}, s32[2,64]{1,0:T(2,128)S(1)}) custom-call(bf16[64,384]{1,0:T(8,128)(2,1)} %hidden.1, f32[3,128]{1,0:T(4,128)} %bitcast.22, bf16[384,1280]{1,0:T(8,128)(2,1)} %weight_hbm.1, s32[1,64]{1,0:T(1,128)} %bitcast.23, s32[1,64]{1,0:T(1,128)} %bitcast.24, s32[1,64]{1,0:T(1,128)} %bitcast.25), custom_call_target="tpu_custom_call" | custom-call | flops 62914560 | bytes 983040 | tf_op jit(solution)/shard_map/pallas_call | solution.py:409
  2.3 16.7 %all_to_all.30.parts = f32[16,4,1408]{2,1,0:T(4,128)S(1)} all-to-all(f32[16,4,1408]{2,1,0:T(4,128)S(1)} %get-tuple-element.11), channel_id=1, replica_groups=mesh['kv'=16,'head'=8] {'kv'}, dimensions={0} | all-to-all | bytes 720896 | tf_op jit(solution)/shard_map/all_to_all | solution.py:360
  19.0 0.0 copy-start
  19.0 0.0 copy-start.1
  19.0 0.1 shard_map.168
  19.1 11.1 %all_to_all.31 = bf16[16,4,8,128]{3,2,1,0:T(8,128)(2,1)S(1)} all-to-all(bf16[16,4,8,128]{3,2,1,0:T(8,128)(2,1)S(1)} %get-tuple-element.12), channel_id=1, replica_groups=mesh['kv'=16,'head'=8] {'kv'}, dimensions={0} | all-to-all | bytes 262144 | tf_op jit(solution)/shard_map/all_to_all | solution.py:360
  30.3 0.0 copy-done
  30.3 0.0 copy-done.1
  30.3 0.0 copy-start.4
  30.3 0.0 copy-start.3
  30.3 0.0 copy-start.6
  30.3 0.0 copy-start.8
  30.3 0.0 copy-start.9
  30.3 3.2 %shard_map.169 = bf16[16,48,128]{2,1,0:T(8,128)(2,1)S(1)} custom-call(bf16[64,8,128]{2,1,0:T(8,128)(2,1)S(1)} %bitcast.15, bf16[64,256,128]{2,1,0:T(8,128)(2,1)S(1)} %bitcast.12, bf16[64,256,128]{2,1,0:T(8,128)(2,1)S(1)} %bitcast.14, s32[2,64]{1,0:T(2,128)S(1)} %get-tuple-element.13.info), custom_call_target="tpu_custom_call" | custom-call | flops 67108864 | bytes 8388608 | tf_op jit(solution)/shard_map/pallas_call | solution.py:435
  33.5 11.4 %all_to_all.32.parts = bf16[16,48,128]{2,1,0:T(8,128)(2,1)S(1)} all-to-all(bf16[16,48,128]{2,1,0:T(8,128)(2,1)S(1)} %shard_map.169), channel_id=1, replica_groups=mesh['kv'=16,'head'=8] {'kv'}, dimensions={0} | all-to-all | bytes 393216 | tf_op jit(solution)/shard_map/all_to_all | solution.py:360
  44.9 0.0 copy-start.2
  44.9 0.0 copy-start.7
  44.9 0.0 copy-start.10
  44.9 0.3 shard_map.170
  45.2 11.1 %all_to_all.33.attended = bf16[16,4,1024]{2,1,0:T(4,128)(2,1)S(1)} all-to-all(bf16[16,4,1024]{2,1,0:T(4,128)(2,1)S(1)} %shard_map.170), channel_id=1, replica_groups=mesh['kv'=16,'head'=8] {'kv'}, dimensions={0} | all-to-all | bytes 262144 | tf_op jit(solution)/shard_map/all_to_all | solution.py:360
  56.3 0.0 copy-done.4
  56.3 0.3 shard_map.171
  56.6 0.1 collective-permute-start
  56.7 1.3 %collective-permute-done = f32[64,384]{1,0:T(8,128)S(1)} collective-permute-done((f32[64,384]{1,0:T(8,128)S(1)}, f32[64,384]{1,0:T(8,128)S(1)}, u32[]{:S(2)}, u32[]{:S(2)}) %collective-permute-start) | collective-permute-done | bytes 98336 | tf_op jit(solution)/shard_map/ppermute | solution.py:364
  58.0 4.0 %collective-permute-start.3 = (bf16[64,384]{1,0:T(8,128)(2,1)S(1)}, bf16[64,384]{1,0:T(8,128)(2,1)S(1)}, u32[]{:S(2)}, u32[]{:S(2)}) collective-permute-start(bf16[64,384]{1,0:T(8,128)(2,1)S(1)} %add_convert_fusion.own), channel_id=1, source_target_pairs={{0,4},{1,5},{2,6},{3,7},{4,0},{5,1},{6,2},{7,3},{8,12},{9,13},{10,... | collective-permute-start | bytes 147464 | tf_op jit(solution)/shard_map/ppermute | solution.py:371
  61.9 0.7 collective-permute-start.2
  62.7 0.3 collective-permute-start.1
  63.0 1.1 %collective-permute-done.3.cross = bf16[64,384]{1,0:T(8,128)(2,1)S(1)} collective-permute-done((bf16[64,384]{1,0:T(8,128)(2,1)S(1)}, bf16[64,384]{1,0:T(8,128)(2,1)S(1)}, u32[]{:S(2)}, u32[]{:S(2)}) %collective-permute-start.3) | collective-permute-done | bytes 49184 | tf_op jit(solution)/shard_map/ppermute | solution.py:371
  64.0 3.2 %collective-permute-done.2.far = bf16[64,384]{1,0:T(8,128)(2,1)S(1)} collective-permute-done((bf16[64,384]{1,0:T(8,128)(2,1)S(1)}, bf16[64,384]{1,0:T(8,128)(2,1)S(1)}, u32[]{:S(2)}, u32[]{:S(2)}) %collective-permute-start.2) | collective-permute-done | bytes 49184 | tf_op jit(solution)/shard_map/ppermute | solution.py:370
  67.2 0.0 collective-permute-done.1.near
  67.3 0.0 copy-done.3
  67.3 0.0 copy-done.6
  67.3 0.0 copy-done.8
  67.3 0.0 copy-done.9
  67.3 0.0 copy-start.5
  67.3 0.9 shard_map.172
  68.2 14.2 %all_to_all.34.parts = bf16[16,144,128]{2,1,0:T(8,128)(2,1)S(1)} all-to-all(bf16[16,144,128]{2,1,0:T(8,128)(2,1)S(1)} %get-tuple-element.15), channel_id=1, replica_groups=mesh['kv'=16,'head'=8] {'kv'}, dimensions={0} | all-to-all | bytes 1179648 | tf_op jit(solution)/shard_map/all_to_all | solution.py:360
  82.4 0.0 copy-done.2
  82.4 0.0 copy-done.7
  82.4 0.0 copy-done.10
  82.5 1.3 %shard_map.173 = (bf16[16,4,1152]{2,1,0:T(4,128)(2,1)S(1)}, f32[8,128,8]{2,1,0:T(8,128)S(1)}, f32[8,16,128]{2,1,0:T(8,128)S(1)}) custom-call(bf16[16,144,128]{2,1,0:T(8,128)(2,1)S(1)} %all_to_all.34.parts, f32[1,8]{1,0:T(1,128)S(1)} %bitcast.20, f32[4,8,128,128]{3,2,1,0:T(8,128)S(1)} %copy-done.2, f32[8,128]{1,0:T(8,128)S(1)} %bitcast.16), custom_call_target="tpu_custom_call" | custom-call | bytes 4194304 | tf_op jit(solution)/shard_map/pallas_call | solution.py:460
  83.8 11.2 %all_to_all.35.blocks = bf16[16,4,1152]{2,1,0:T(4,128)(2,1)S(1)} all-to-all(bf16[16,4,1152]{2,1,0:T(4,128)(2,1)S(1)} %get-tuple-element.16), channel_id=1, replica_groups=mesh['kv'=16,'head'=8] {'kv'}, dimensions={0} | all-to-all | bytes 294912 | tf_op jit(solution)/shard_map/all_to_all | solution.py:360
  95.0 0.0 copy-done.5
  95.0 0.4 shard_map.174.own
  95.4 0.1 collective-permute-start.4
  95.5 1.3 %collective-permute-done.4.near = f32[72,384]{1,0:T(8,128)S(1)} collective-permute-done((f32[72,384]{1,0:T(8,128)S(1)}, f32[72,384]{1,0:T(8,128)S(1)}, u32[]{:S(2)}, u32[]{:S(2)}) %collective-permute-start.4) | collective-permute-done | bytes 110624 | tf_op jit(solution)/shard_map/ppermute | solution.py:364
  96.8 2.0 %collective-permute-start.7 = (bf16[80,384]{1,0:T(8,128)(2,1)S(1)}, bf16[80,384]{1,0:T(8,128)(2,1)S(1)}, u32[]{:S(2)}, u32[]{:S(2)}) collective-permute-start(bf16[80,384]{1,0:T(8,128)(2,1)S(1)} %shard_map.175.own), channel_id=1, source_target_pairs={{0,4},{1,5},{2,6},{3,7},{4,0},{5,1},{6,2},{7,3},{8,12},{9,13},{10,... | collective-permute-start | bytes 184328 | tf_op jit(solution)/shard_map/ppermute | solution.py:371
  98.8 1.1 %collective-permute-start.6 = (bf16[80,384]{1,0:T(8,128)(2,1)S(1)}, bf16[80,384]{1,0:T(8,128)(2,1)S(1)}, u32[]{:S(2)}, u32[]{:S(2)}) collective-permute-start(bf16[80,384]{1,0:T(8,128)(2,1)S(1)} %shard_map.175.own), channel_id=1, source_target_pairs={{0,6},{1,7},{2,4},{3,5},{4,2},{5,3},{6,0},{7,1},{8,14},{9,15},{10,... | collective-permute-start | bytes 184328 | tf_op jit(solution)/shard_map/ppermute | solution.py:370
  99.9 0.5 collective-permute-start.5
  100.4 2.0 %shard_map.177 = f32[4,8,128,128]{3,2,1,0:T(8,128)} custom-call(f32[8,128,8]{2,1,0:T(8,128)S(1)} %get-tuple-element.18.turned, f32[8,16,128]{2,1,0:T(8,128)S(1)} %get-tuple-element.19.mixed, f32[1,8]{1,0:T(1,128)S(1)} %bitcast.21, f32[4,8,128,128]{3,2,1,0:T(8,128)S(1)} %copy-done.2), custom_call_target="tpu_custom_call" | custom-call | bytes 4194304 | tf_op jit(solution)/shard_map/pallas_call | solution.py:479
  102.4 0.3 collective-permute-done.7.cross
  102.7 1.6 %collective-permute-done.6.far = bf16[80,384]{1,0:T(8,128)(2,1)S(1)} collective-permute-done((bf16[80,384]{1,0:T(8,128)(2,1)S(1)}, bf16[80,384]{1,0:T(8,128)(2,1)S(1)}, u32[]{:S(2)}, u32[]{:S(2)}) %collective-permute-start.6) | collective-permute-done | bytes 61472 | tf_op jit(solution)/shard_map/ppermute | solution.py:370
  104.2 0.0 collective-permute-done.5.near
  104.2 0.7 shard_map.176
  (2 shorter events, 0.0 us)
Async XLA Ops:
  19.0 11.3 %copy-start = (bf16[64,1,256,128]{3,2,1,0:T(8,128)(2,1)S(1)}, bf16[64,1,256,128]{3,2,1,0:T(8,128)(2,1)}, u32[]{:S(2)}) copy-start(bf16[64,1,256,128]{3,2,1,0:T(8,128)(2,1)} %param.20) | copy-start | bytes 12582916
  19.0 11.3 %copy-start.1 = (bf16[64,1,256,128]{3,2,1,0:T(8,128)(2,1)S(1)}, bf16[64,1,256,128]{3,2,1,0:T(8,128)(2,1)}, u32[]{:S(2)}) copy-start(bf16[64,1,256,128]{3,2,1,0:T(8,128)(2,1)} %param.21) | copy-start | bytes 12582916
  30.3 26.1 %copy-start.4 = (bf16[1024,384]{1,0:T(8,128)(2,1)S(1)}, bf16[1024,384]{1,0:T(8,128)(2,1)}, u32[]{:S(2)}) copy-start(bf16[1024,384]{1,0:T(8,128)(2,1)} %weight.3) | copy-start | bytes 2359300
  30.3 37.0 %copy-start.3 = (bf16[384,4096]{1,0:T(8,128)(2,1)S(1)}, bf16[384,4096]{1,0:T(8,128)(2,1)}, u32[]{:S(2)}) copy-start(bf16[384,4096]{1,0:T(8,128)(2,1)} %weight.4) | copy-start | bytes 9437188
  30.3 37.0 %copy-start.6 = (bf16[64,384]{1,0:T(8,128)(2,1)S(1)}, bf16[64,384]{1,0:T(8,128)(2,1)}, u32[]{:S(2)}) copy-start(bf16[64,384]{1,0:T(8,128)(2,1)} %hidden.1) | copy-start | bytes 147460
  30.3 37.0 %copy-start.8 = (f32[384]{0:T(512)S(1)}, f32[384]{0:T(512)}, u32[]{:S(2)}) copy-start(f32[384]{0:T(512)} %param.25) | copy-start | bytes 4612
  30.3 37.0 %copy-start.9 = (s32[64]{0:T(128)S(1)}, s32[64]{0:T(128)}, u32[]{:S(2)}) copy-start(s32[64]{0:T(128)} %param.31) | copy-start | bytes 772
  44.9 37.5 %copy-start.2 = (f32[4,8,128,128]{3,2,1,0:T(8,128)S(1)}, f32[4,8,128,128]{3,2,1,0:T(8,128)}, u32[]{:S(2)}) copy-start(f32[4,8,128,128]{3,2,1,0:T(8,128)} %states.3) | copy-start | bytes 6291460
  44.9 37.5 %copy-start.7 = (f32[1024]{0:T(1024)S(1)}, f32[1024]{0:T(1024)}, u32[]{:S(2)}) copy-start(f32[1024]{0:T(1024)} %param.29) | copy-start | bytes 12292
  44.9 37.5 %copy-start.10 = (f32[8]{0:T(128)S(1)}, f32[8]{0:T(128)}, u32[]{:S(2)}) copy-start(f32[8]{0:T(128)} %param.27) | copy-start | bytes 100
  56.6 1.4 %collective-permute-start = (f32[64,384]{1,0:T(8,128)S(1)}, f32[64,384]{1,0:T(8,128)S(1)}, u32[]{:S(2)}, u32[]{:S(2)}) collective-permute-start(f32[64,384]{1,0:T(8,128)S(1)} %shard_map.171), channel_id=1, source_target_pairs={{0,1},{1,0},{2,3},{3,2},{4,5},{5,4},{6,7},{7,6},{8,9},{9,8},{10,11... | collective-permute-start | bytes 294920 | tf_op jit(solution)/shard_map/ppermute | solution.py:364
  58.0 6.0 %collective-permute-start.3 = (bf16[64,384]{1,0:T(8,128)(2,1)S(1)}, bf16[64,384]{1,0:T(8,128)(2,1)S(1)}, u32[]{:S(2)}, u32[]{:S(2)}) collective-permute-start(bf16[64,384]{1,0:T(8,128)(2,1)S(1)} %add_convert_fusion.own), channel_id=1, source_target_pairs={{0,4},{1,5},{2,6},{3,7},{4,0},{5,1},{6,2},{7,3},{8,12},{9,13},{10,... | collective-permute-start | bytes 147464 | tf_op jit(solution)/shard_map/ppermute | solution.py:371
  61.9 5.3 %collective-permute-start.2 = (bf16[64,384]{1,0:T(8,128)(2,1)S(1)}, bf16[64,384]{1,0:T(8,128)(2,1)S(1)}, u32[]{:S(2)}, u32[]{:S(2)}) collective-permute-start(bf16[64,384]{1,0:T(8,128)(2,1)S(1)} %add_convert_fusion.own), channel_id=1, source_target_pairs={{0,6},{1,7},{2,4},{3,5},{4,2},{5,3},{6,0},{7,1},{8,14},{9,15},{10,... | collective-permute-start | bytes 147464 | tf_op jit(solution)/shard_map/ppermute | solution.py:370
  62.7 4.6 %collective-permute-start.1 = (bf16[64,384]{1,0:T(8,128)(2,1)S(1)}, bf16[64,384]{1,0:T(8,128)(2,1)S(1)}, u32[]{:S(2)}, u32[]{:S(2)}) collective-permute-start(bf16[64,384]{1,0:T(8,128)(2,1)S(1)} %add_convert_fusion.own), channel_id=1, source_target_pairs={{0,2},{1,3},{2,0},{3,1},{4,6},{5,7},{6,4},{7,5},{8,10},{9,11},{10,... | collective-permute-start | bytes 147464 | tf_op jit(solution)/shard_map/ppermute | solution.py:369
  67.3 27.7 %copy-start.5 = (bf16[1024,384]{1,0:T(8,128)(2,1)S(1)}, bf16[1024,384]{1,0:T(8,128)(2,1)}, u32[]{:S(2)}) copy-start(bf16[1024,384]{1,0:T(8,128)(2,1)} %weight.5) | copy-start | bytes 2359300
  95.4 1.4 %collective-permute-start.4 = (f32[72,384]{1,0:T(8,128)S(1)}, f32[72,384]{1,0:T(8,128)S(1)}, u32[]{:S(2)}, u32[]{:S(2)}) collective-permute-start(f32[72,384]{1,0:T(8,128)S(1)} %shard_map.174.own), channel_id=1, source_target_pairs={{0,1},{1,0},{2,3},{3,2},{4,5},{5,4},{6,7},{7,6},{8,9},{9,8},{10,11... | collective-permute-start | bytes 331784 | tf_op jit(solution)/shard_map/ppermute | solution.py:364
  96.8 5.8 %collective-permute-start.7 = (bf16[80,384]{1,0:T(8,128)(2,1)S(1)}, bf16[80,384]{1,0:T(8,128)(2,1)S(1)}, u32[]{:S(2)}, u32[]{:S(2)}) collective-permute-start(bf16[80,384]{1,0:T(8,128)(2,1)S(1)} %shard_map.175.own), channel_id=1, source_target_pairs={{0,4},{1,5},{2,6},{3,7},{4,0},{5,1},{6,2},{7,3},{8,12},{9,13},{10,... | collective-permute-start | bytes 184328 | tf_op jit(solution)/shard_map/ppermute | solution.py:371
  98.8 5.4 %collective-permute-start.6 = (bf16[80,384]{1,0:T(8,128)(2,1)S(1)}, bf16[80,384]{1,0:T(8,128)(2,1)S(1)}, u32[]{:S(2)}, u32[]{:S(2)}) collective-permute-start(bf16[80,384]{1,0:T(8,128)(2,1)S(1)} %shard_map.175.own), channel_id=1, source_target_pairs={{0,6},{1,7},{2,4},{3,5},{4,2},{5,3},{6,0},{7,1},{8,14},{9,15},{10,... | collective-permute-start | bytes 184328 | tf_op jit(solution)/shard_map/ppermute | solution.py:370
  99.9 4.4 %collective-permute-start.5 = (bf16[80,384]{1,0:T(8,128)(2,1)S(1)}, bf16[80,384]{1,0:T(8,128)(2,1)S(1)}, u32[]{:S(2)}, u32[]{:S(2)}) collective-permute-start(bf16[80,384]{1,0:T(8,128)(2,1)S(1)} %shard_map.175.own), channel_id=1, source_target_pairs={{0,2},{1,3},{2,0},{3,1},{4,6},{5,7},{6,4},{7,5},{8,10},{9,11},{10,... | collective-permute-start | bytes 184328 | tf_op jit(solution)/shard_map/ppermute | solution.py:369

commit v4 on v3

--- a/solution.py
+++ b/solution.py
@@ -19,6 +19,7 @@
 F32 = jnp.float32
 BF16 = jnp.bfloat16
 MIB = 1 << 20
+LINES = 16
 
 
 def iota(shape, dim):
@@ -125,15 +126,15 @@
         out[p] = queries
 
 
-def attention_kernel(queries, keys, values, info, out, slot_max, slot_sum, slot_value, best, summed, mixed):
-    slots = keys.shape[0]
-    rows = REQ // out.shape[0]
+def attention_kernel(queries, keys, values, info, own, out, slot_max, slot_sum, slot_value, best, summed, mixed):
+    slots, rows = keys.shape[0], own.shape[0]
     best[...] = jnp.full(best.shape, NEGATIVE, F32)
     summed[...] = jnp.zeros(summed.shape, F32)
     mixed[...] = jnp.zeros(mixed.shape, F32)
     token = iota((GQ, CH), 1)
     scale = 1.0 / math.sqrt(HD)
     batch = 32
+    mine = lax.axis_index("kv") * rows
 
     @pl.loop(0, slots, step=batch)
     def _(base):
@@ -161,8 +162,20 @@
             slot_sum[s] = jnp.broadcast_to(total, (GQ, HD))
             slot_value[s] = mix
 
+    fresh = [
+        jnp.broadcast_to(
+            jnp.sum(own[i, :GQ, :] * own[i, GQ:GQ + 1, :], axis=1, keepdims=True) / math.sqrt(HD), (GQ, HD)
+        )
+        for i in range(rows)
+    ]
+    for i in range(rows):
+        best[mine + i] = jnp.maximum(best[mine + i], fresh[i])
     upper, lower = halves(best[...])
     best[...] = upper + lower
+    for i in range(rows):
+        factor = jnp.exp(fresh[i] - best[mine + i])
+        summed[mine + i] = factor
+        mixed[mine + i] = factor * own[i, GQ + 1:GQ + 2, :]
     step = 8
 
     @pl.loop(0, slots, step=step)
@@ -175,56 +188,69 @@
             mixed[r] = mixed[r] + factor * slot_value[s]
 
     lane, sub = iota((GQ, HD), 1), iota((GQ, HD), 0)
-    line = iota((2 * GQ, HD), 0)
-
-    @pl.loop(0, out.shape[0])
-    def _(p):
-        stats = jnp.zeros((2 * GQ, HD), F32)
-        for i in range(rows):
-            r = p * rows + i
-            packed = jnp.zeros((GQ, HD), F32)
+    line = iota((LINES, HD), 0)
+    stats = jnp.zeros((LINES, HD), F32)
+    for i in range(LINES):
+        packed = jnp.zeros((GQ, HD), F32)
+        for c in range(REQ // LINES):
+            r = c * LINES + i
             for k, part in enumerate(halves(best[r]) + halves(summed[r])):
-                packed = jnp.where(lane == sub + k * GQ, part, packed)
-            stats = jnp.where(line == i, jnp.sum(packed, axis=0, keepdims=True), stats)
-        out[p, :rows * GQ, :] = mixed[pl.ds(p * rows, rows)].reshape(rows * GQ, HD).astype(BF16)
-        out[p, rows * GQ:, :] = stats.astype(BF16)
-
-
-def finish_kernel(parts, own, out, flat, fresh_rows):
-    peers, rows = parts.shape[0], own.shape[0]
-    lane, sub = iota((GQ, HD), 1), iota((GQ, HD), 0)
-    diagonal = lane == sub
-    for i in range(rows):
-        fresh = jnp.sum(own[i, :GQ, :] * own[i, GQ:GQ + 1, :], axis=1, keepdims=True) / math.sqrt(HD)
-        fresh_rows[i:i + 1, :] = jnp.sum(jnp.where(diagonal, fresh, 0.0), axis=0, keepdims=True)
-    fresh = fresh_rows[0:rows, :]
-    lines = [parts[p, rows * GQ:, :].astype(F32)[0:rows] for p in range(peers)]
+                packed = jnp.where(lane == sub + (4 * c + k) * GQ, part, packed)
+        stats = jnp.where(line == i, jnp.sum(packed, axis=0, keepdims=True), stats)
+    out[:REQ * GQ, :] = mixed[0:REQ].reshape(REQ * GQ, HD).astype(BF16)
+    out[REQ * GQ:, :] = stats.astype(BF16)
+
+
+def merge_weights(parts):
+    lines = [part[REQ * GQ:, :].astype(F32) for part in parts]
     tops = [x + pltpu.roll(x, HD - GQ, axis=1) for x in lines]
     sums = [pltpu.roll(x, HD - 2 * GQ, axis=1) for x in tops]
-    top = fresh
-    for p in range(peers):
-        top = jnp.maximum(top, tops[p])
-    latest = jnp.exp(fresh - top)
-    below = latest
+    top = jnp.maximum(jnp.maximum(tops[0], tops[1]), jnp.maximum(tops[2], tops[3]))
     factors = [jnp.exp(x - top) for x in tops]
-    for p in range(peers):
-        below = below + factors[p] * sums[p]
-
-    def column(value, i):
-        return jnp.sum(jnp.where(diagonal, value[i:i + 1, :], 0.0), axis=1, keepdims=True)
-
-    above = [column(latest, i) * own[i, GQ + 1:GQ + 2, :] for i in range(rows)]
-    for p in range(peers):
-        values = parts[p, :rows * GQ, :].astype(F32)
-        for i in range(rows):
-            above[i] = above[i] + column(factors[p], i) * values[i * GQ:(i + 1) * GQ]
-    for i in range(rows):
-        result = above[i] / column(below, i)
-        for g in range(GQ):
-            flat[i:i + 1, g * HD:(g + 1) * HD] = result[g:g + 1, :]
-    attended = flat[0:rows, :].astype(BF16)
-    for p in range(out.shape[0]):
-        out[p] = attended
+    terms = [f * x for f, x in zip(factors, sums)]
+    return top, factors, (terms[0] + terms[1]) + (terms[2] + terms[3])
+
+
+def weighted(parts, factors, store):
+    columns = [f.T for f in factors]
+    for r in range(0, REQ, 2):
+        c, i = r // LINES, r % LINES
+        blocks = [part[r * GQ:(r + 2) * GQ, :].astype(F32) for part in parts]
+        pair = []
+        for u in range(2):
+            at = slice(4 * c * GQ, (4 * c + 1) * GQ)
+            terms = [t[at, i + u:i + u + 1] * b[u * GQ:(u + 1) * GQ] for t, b in zip(columns, blocks)]
+            pair.append((terms[0] + terms[1]) + (terms[2] + terms[3]))
+        store(r, jnp.concatenate(pair, axis=0))
+
+
+def merge_kernel(own, near, far, cross, out):
+    parts = own, near, far, cross
+    top, factors, total = merge_weights(parts)
+
+    def store(r, value):
+        out[r * GQ:(r + 2) * GQ, :] = value.astype(BF16)
+
+    weighted(parts, factors, store)
+    place = lax.rem(iota((LINES, HD), 1), 4 * GQ)
+    packed = jnp.zeros((LINES, HD), F32)
+    for k, part in enumerate(halves(top) + halves(total)):
+        moved = part if k == 0 else pltpu.roll(part, k * GQ, axis=1)
+        packed = jnp.where((place >= k * GQ) & (place < (k + 1) * GQ), moved, packed)
+    out[REQ * GQ:, :] = packed.astype(BF16)
+
+
+def attention_out_kernel(own, near, far, cross, weight, out, tall, flat):
+    parts = own, near, far, cross
+    _, factors, total = merge_weights(parts)
+
+    def store(r, value):
+        tall[r * GQ:(r + 2) * GQ, :] = value
+
+    weighted(parts, [f / total for f in factors], store)
+    for g in range(GQ):
+        flat[:, g * HD:(g + 1) * HD] = tall[pl.ds(g, REQ, stride=GQ), :].astype(BF16)
+    out[...] = jnp.dot(flat[...], weight[...], preferred_element_type=F32)
 
 
 def stacked(blocks, flat):
@@ -235,11 +261,6 @@
 
 def four(own, near, far, cross):
     return (own[...].astype(F32) + near[...].astype(F32)) + (far[...].astype(F32) + cross[...].astype(F32))
-
-
-def attention_out_kernel(attended, weight, out, flat):
-    stacked(attended, flat)
-    out[...] = jnp.dot(flat[...].astype(BF16), weight[...], preferred_element_type=F32)
 
 
 def mixing_kernel(own, near, far, cross, hidden, gain, request, weight, out, middle, turned):
@@ -364,12 +385,16 @@
     return lax.ppermute(value, "head", [(i, i ^ 1) for i in range(lax.axis_size("head"))])
 
 
-def along_z(value):
-    size = lax.axis_size("head")
-    near = lax.ppermute(value, "head", [(i, i ^ 2) for i in range(size)])
-    far = lax.ppermute(value, "head", [(i, (3 - i // 2) * 2 + i % 2) for i in range(size)])
-    cross = lax.ppermute(value, "head", [(i, i ^ 4) for i in range(size)])
-    return value, near, far, cross
+def along(value, axis, stride):
+    size = lax.axis_size(axis)
+
+    def place(i):
+        return i // stride % 4
+
+    near = [(i, i ^ stride) for i in range(size)]
+    far = [(i, i + (3 - 2 * place(i)) * stride) for i in range(size)]
+    cross = [(i, i ^ (2 * stride)) for i in range(size)]
+    return (value, *(lax.ppermute(value, axis, pairs) for pairs in (near, far, cross)))
 
 
 def per_device(
@@ -432,30 +457,27 @@
     )
     queries = exchange(queries).reshape(requests, GQ, HD)
     tiles = [pltpu.VMEM((slots, GQ, HD), F32)] * 3 + [pltpu.VMEM((requests + 1, GQ, HD), F32)] * 3
-    partial = kernel_call(
-        attention_kernel,
-        S((peers, rows * GQ + 16, HD), BF16),
-        [VMEM, VMEM, VMEM, SMEM], 24 * MIB, 4 * slots * GQ * CH * HD, 4 * slots * CH * HD, tiles,
-    )(queries, keys, values, info)
-    attended = kernel_call(
-        finish_kernel,
-        S((peers, rows, GQ * HD), BF16),
-        [VMEM, VMEM], 8 * MIB, 0, 8 * peers * rows * GQ * HD,
-        [pltpu.VMEM((8, GQ * HD), F32), pltpu.VMEM((8, HD), F32)],
-    )(exchange(partial), own)
+    partial = S((requests * GQ + LINES, HD), BF16)
+    part = kernel_call(
+        attention_kernel, partial,
+        [VMEM, VMEM, VMEM, SMEM, VMEM], 24 * MIB, 4 * slots * GQ * CH * HD, 4 * slots * CH * HD, tiles,
+    )(queries, keys, values, info, own)
+    part = kernel_call(
+        merge_kernel, partial, [VMEM] * 4, 8 * MIB, 0, 10 * requests * GQ * HD,
+    )(*along(part, "kv", 1))
     first = kernel_call(
         attention_out_kernel,
         S((requests, features), F32),
-        [VMEM, VMEM], 8 * MIB, 2 * requests * GQ * HD * features, 2 * GQ * HD * features,
-        [pltpu.VMEM((requests, GQ * HD), F32)],
-    )(exchange(attended), attn_out_weight)
+        [VMEM] * 5, 8 * MIB, 2 * requests * GQ * HD * features, 2 * GQ * HD * features,
+        [pltpu.VMEM((requests * GQ, HD), F32), pltpu.VMEM((requests, GQ * HD), BF16)],
+    )(*along(part, "kv", 4), attn_out_weight)
     height = rows * (lin_width // HD) + 16
     mixing, middle = kernel_call(
         mixing_kernel,
         (S((peers, height, HD), BF16), S((requests, features), BF16)),
         [VMEM] * 8, 16 * MIB, 2 * requests * features * lin_width, 2 * features * lin_width,
         [pltpu.VMEM((peers, 4 * rows, HD), F32)],
-    )(*along_z((first + other_core(first)).astype(BF16)), hidden_in, lin_gain.reshape(chunks, HD), request, lin_weight)
+    )(*along((first + other_core(first)).astype(BF16), "head", 2), hidden_in, lin_gain.reshape(chunks, HD), request, lin_weight)
     decay = decay_rate[None, :]
     gated, turned, mixed = kernel_call(
         lightning_kernel,
@@ -483,7 +505,7 @@
         last_kernel,
         S((requests, features), BF16),
         [VMEM] * 5, 4 * MIB, 0, 16 * requests * features,
-    )(*along_z(pair), middle)
+    )(*along(pair, "head", 2), middle)
     return hidden_out, renewed
 
 

time: 105 us -> 101 us (0.962)
  blocking collectives: 75.8 us -> 53.8 us
  waiting for transfers between devices: 8.7 us -> 17.9 us
  starting transfers between devices: 8.72 us -> 15.9 us
    all_to_all x6 -> x4, blocking collectives: 75.8 us -> 53.8 us  [exchange(): return lax.all_to_all(blocks, 'kv', 0, 0, tiled=True)]
    ppermute x6 -> x12, waiting for transfers between devices: 6.11 us -> 15.3 us  [along(): lax.ppermute(value, axis, pairs)]
    ppermute x6 -> x12, starting transfers between devices: 8.54 us -> 15.7 us  [along(): lax.ppermute(value, axis, pairs)]
  transfers between devices with their start and end apart: 8 -> 14, of which waited for: 6 -> 11; matrix products, arithmetic and copies ran while one was open for 0% -> 0% of each run, Pallas kernels for 2% -> 2%
where the time goes in v4:
time: 101 us; the launch traced here: 100 us
  blocking collectives  53.8 us (53%)
  waiting for transfers between devices  17.9 us (18%)
  starting transfers between devices  15.9 us (16%)
  Pallas kernels  11.9 us (12%)
    all_to_all x4, blocking collectives, exchange(): return lax.all_to_all(blocks, 'kv', 0, 0, tiled=True)  53.8 us
    ppermute x12, starting transfers between devices, along(): lax.ppermute(value, axis, pairs)  15.7 us
    ppermute x12, waiting for transfers between devices, along(): lax.ppermute(value, axis, pairs)  15.3 us
    pallas_call x1, Pallas kernels, per_device(): kernel_call(attention_kernel, partial, [VMEM, VMEM, VMEM, SMEM, VMEM], 24...  3.06 us
    ppermute x2, waiting for transfers between devices, other_core(): lax.ppermute(value, 'head', [(i, i ^ 1) for i in range(lax.axis_size('hea...  2.59 us
  transfers between devices with their start and end apart: 14, of which 11 were waited for; matrix products, arithmetic and copies ran while one was open for 0% of the time, Pallas kernels for 2%

profile of v4, /device:TPU:0, one launch (start us, length us, event | category | flops | bytes accessed | tf_op | source)
XLA Modules:
  0.0 100.3 jit_solution(13104150347425171448)
XLA Ops:
  0.6 1.7 %shard_map.167 = (f32[16,4,1408]{2,1,0:T(4,128)S(1)}, s32[2,64]{1,0:T(2,128)S(1)}) custom-call(bf16[64,384]{1,0:T(8,128)(2,1)} %hidden.1, f32[3,128]{1,0:T(4,128)} %bitcast.22, bf16[384,1280]{1,0:T(8,128)(2,1)} %weight_hbm.1, s32[1,64]{1,0:T(1,128)} %bitcast.23, s32[1,64]{1,0:T(1,128)} %bitcast.24, s32[1,64]{1,0:T(1,128)} %bitcast.25), custom_call_target="tpu_custom_call" | custom-call | flops 62914560 | bytes 983040 | tf_op jit(solution)/shard_map/pallas_call | solution.py:434
  2.3 16.7 %all_to_all.20.parts = f32[16,4,1408]{2,1,0:T(4,128)S(1)} all-to-all(f32[16,4,1408]{2,1,0:T(4,128)S(1)} %get-tuple-element.11), channel_id=1, replica_groups=mesh['kv'=16,'head'=8] {'kv'}, dimensions={0} | all-to-all | bytes 720896 | tf_op jit(solution)/shard_map/all_to_all | solution.py:381
  19.0 0.0 copy-start
  19.0 0.0 copy-start.1
  19.0 0.1 shard_map.168
  19.1 11.1 %all_to_all.21 = bf16[16,4,8,128]{3,2,1,0:T(8,128)(2,1)S(1)} all-to-all(bf16[16,4,8,128]{3,2,1,0:T(8,128)(2,1)S(1)} %get-tuple-element.12), channel_id=1, replica_groups=mesh['kv'=16,'head'=8] {'kv'}, dimensions={0} | all-to-all | bytes 262144 | tf_op jit(solution)/shard_map/all_to_all | solution.py:381
  30.3 0.0 copy-done
  30.3 0.0 copy-done.1
  30.3 0.0 copy-start.4
  30.3 0.0 copy-start.3
  30.3 0.0 copy-start.6
  30.3 0.0 copy-start.8
  30.3 0.0 copy-start.9
  30.3 3.1 %shard_map.169.own = bf16[528,128]{1,0:T(8,128)(2,1)S(1)} custom-call(bf16[64,8,128]{2,1,0:T(8,128)(2,1)S(1)} %bitcast.15, bf16[64,256,128]{2,1,0:T(8,128)(2,1)S(1)} %bitcast.12, bf16[64,256,128]{2,1,0:T(8,128)(2,1)S(1)} %bitcast.14, s32[2,64]{1,0:T(2,128)S(1)} %get-tuple-element.13.info, f32[4,10,128]{2,1,0:T(8,128)S(1)} %get-tuple-element.14.own), custom_call_target="tpu_custom_call" | custom-call | flops 67108864 | bytes 8388608 | tf_op jit(solution)/shard_map/pallas_call | solution.py:461
  33.4 1.3 %collective-permute-start.2 = (bf16[528,128]{1,0:T(8,128)(2,1)S(1)}, bf16[528,128]{1,0:T(8,128)(2,1)S(1)}, u32[]{:S(2)}, u32[]{:S(2)}) collective-permute-start(bf16[528,128]{1,0:T(8,128)(2,1)S(1)} %shard_map.169.own), channel_id=1, source_target_pairs={{0,16},{8,24},{16,0},{24,8},{32,48},{40,56},{48,32},{56,40},{64,80... | collective-permute-start | bytes 405512 | tf_op jit(solution)/shard_map/ppermute | solution.py:397
  34.7 2.0 %collective-permute-start.1 = (bf16[528,128]{1,0:T(8,128)(2,1)S(1)}, bf16[528,128]{1,0:T(8,128)(2,1)S(1)}, u32[]{:S(2)}, u32[]{:S(2)}) collective-permute-start(bf16[528,128]{1,0:T(8,128)(2,1)S(1)} %shard_map.169.own), channel_id=1, source_target_pairs={{0,24},{8,16},{16,8},{24,0},{32,56},{40,48},{48,40},{56,32},{64,88... | collective-permute-start | bytes 405512 | tf_op jit(solution)/shard_map/ppermute | solution.py:397
  36.7 0.3 collective-permute-start
  36.9 3.1 %collective-permute-done.2.cross = bf16[528,128]{1,0:T(8,128)(2,1)S(1)} collective-permute-done((bf16[528,128]{1,0:T(8,128)(2,1)S(1)}, bf16[528,128]{1,0:T(8,128)(2,1)S(1)}, u32[]{:S(2)}, u32[]{:S(2)}) %collective-permute-start.2) | collective-permute-done | bytes 135200 | tf_op jit(solution)/shard_map/ppermute | solution.py:397
  40.0 1.4 %collective-permute-done.1.far = bf16[528,128]{1,0:T(8,128)(2,1)S(1)} collective-permute-done((bf16[528,128]{1,0:T(8,128)(2,1)S(1)}, bf16[528,128]{1,0:T(8,128)(2,1)S(1)}, u32[]{:S(2)}, u32[]{:S(2)}) %collective-permute-start.1) | collective-permute-done | bytes 135200 | tf_op jit(solution)/shard_map/ppermute | solution.py:397
  41.4 0.3 collective-permute-done.near
  41.7 0.6 shard_map.170.own
  42.3 0.0 copy-start.2
  42.4 0.0 copy-start.7
  42.4 0.0 copy-start.10
  42.4 1.1 %collective-permute-start.5 = (bf16[528,128]{1,0:T(8,128)(2,1)S(1)}, bf16[528,128]{1,0:T(8,128)(2,1)S(1)}, u32[]{:S(2)}, u32[]{:S(2)}) collective-permute-start(bf16[528,128]{1,0:T(8,128)(2,1)S(1)} %shard_map.170.own), channel_id=1, source_target_pairs={{0,64},{8,72},{16,80},{24,88},{32,96},{40,104},{48,112},{56,120},{... | collective-permute-start | bytes 405512 | tf_op jit(solution)/shard_map/ppermute | solution.py:397
  43.5 1.9 %collective-permute-start.4 = (bf16[528,128]{1,0:T(8,128)(2,1)S(1)}, bf16[528,128]{1,0:T(8,128)(2,1)S(1)}, u32[]{:S(2)}, u32[]{:S(2)}) collective-permute-start(bf16[528,128]{1,0:T(8,128)(2,1)S(1)} %shard_map.170.own), channel_id=1, source_target_pairs={{0,96},{8,104},{16,112},{24,120},{32,64},{40,72},{48,80},{56,88},{... | collective-permute-start | bytes 405512 | tf_op jit(solution)/shard_map/ppermute | solution.py:397
  45.4 0.6 collective-permute-start.3
  45.9 3.1 %collective-permute-done.5.cross = bf16[528,128]{1,0:T(8,128)(2,1)S(1)} collective-permute-done((bf16[528,128]{1,0:T(8,128)(2,1)S(1)}, bf16[528,128]{1,0:T(8,128)(2,1)S(1)}, u32[]{:S(2)}, u32[]{:S(2)}) %collective-permute-start.5) | collective-permute-done | bytes 135200 | tf_op jit(solution)/shard_map/ppermute | solution.py:397
  49.1 1.4 %collective-permute-done.4.far = bf16[528,128]{1,0:T(8,128)(2,1)S(1)} collective-permute-done((bf16[528,128]{1,0:T(8,128)(2,1)S(1)}, bf16[528,128]{1,0:T(8,128)(2,1)S(1)}, u32[]{:S(2)}, u32[]{:S(2)}) %collective-permute-start.4) | collective-permute-done | bytes 135200 | tf_op jit(solution)/shard_map/ppermute | solution.py:397
  50.4 0.0 collective-permute-done.3.near
  50.4 0.0 copy-done.4
  50.4 0.9 shard_map.171
  51.4 0.1 collective-permute-start.6
  51.5 1.3 %collective-permute-done.6 = f32[64,384]{1,0:T(8,128)S(1)} collective-permute-done((f32[64,384]{1,0:T(8,128)S(1)}, f32[64,384]{1,0:T(8,128)S(1)}, u32[]{:S(2)}, u32[]{:S(2)}) %collective-permute-start.6) | collective-permute-done | bytes 98336 | tf_op jit(solution)/shard_map/ppermute | solution.py:385
  52.8 4.0 %collective-permute-start.9 = (bf16[64,384]{1,0:T(8,128)(2,1)S(1)}, bf16[64,384]{1,0:T(8,128)(2,1)S(1)}, u32[]{:S(2)}, u32[]{:S(2)}) collective-permute-start(bf16[64,384]{1,0:T(8,128)(2,1)S(1)} %add_convert_fusion.own), channel_id=1, source_target_pairs={{0,4},{1,5},{2,6},{3,7},{4,0},{5,1},{6,2},{7,3},{8,12},{9,13},{10,... | collective-permute-start | bytes 147464 | tf_op jit(solution)/shard_map/ppermute | solution.py:397
  56.7 0.7 collective-permute-start.8
  57.4 0.3 collective-permute-start.7
  57.8 1.1 %collective-permute-done.9.cross = bf16[64,384]{1,0:T(8,128)(2,1)S(1)} collective-permute-done((bf16[64,384]{1,0:T(8,128)(2,1)S(1)}, bf16[64,384]{1,0:T(8,128)(2,1)S(1)}, u32[]{:S(2)}, u32[]{:S(2)}) %collective-permute-start.9) | collective-permute-done | bytes 49184 | tf_op jit(solution)/shard_map/ppermute | solution.py:397
  58.8 3.2 %collective-permute-done.8.far = bf16[64,384]{1,0:T(8,128)(2,1)S(1)} collective-permute-done((bf16[64,384]{1,0:T(8,128)(2,1)S(1)}, bf16[64,384]{1,0:T(8,128)(2,1)S(1)}, u32[]{:S(2)}, u32[]{:S(2)}) %collective-permute-start.8) | collective-permute-done | bytes 49184 | tf_op jit(solution)/shard_map/ppermute | solution.py:397
  62.0 0.0 collective-permute-done.7.near
  62.0 0.0 copy-done.3
  62.0 0.0 copy-done.6
  62.1 0.0 copy-done.8
  62.1 0.0 copy-done.9
  62.1 0.0 copy-start.5
  62.1 0.9 shard_map.172
  63.0 14.8 %all_to_all.22.parts = bf16[16,144,128]{2,1,0:T(8,128)(2,1)S(1)} all-to-all(bf16[16,144,128]{2,1,0:T(8,128)(2,1)S(1)} %get-tuple-element.15), channel_id=1, replica_groups=mesh['kv'=16,'head'=8] {'kv'}, dimensions={0} | all-to-all | bytes 1179648 | tf_op jit(solution)/shard_map/all_to_all | solution.py:381
  77.8 0.0 copy-done.2
  77.8 0.0 copy-done.7
  77.8 0.0 copy-done.10
  77.8 1.3 %shard_map.173 = (bf16[16,4,1152]{2,1,0:T(4,128)(2,1)S(1)}, f32[8,128,8]{2,1,0:T(8,128)S(1)}, f32[8,16,128]{2,1,0:T(8,128)S(1)}) custom-call(bf16[16,144,128]{2,1,0:T(8,128)(2,1)S(1)} %all_to_all.22.parts, f32[1,8]{1,0:T(1,128)S(1)} %bitcast.20, f32[4,8,128,128]{3,2,1,0:T(8,128)S(1)} %copy-done.2, f32[8,128]{1,0:T(8,128)S(1)} %bitcast.16), custom_call_target="tpu_custom_call" | custom-call | bytes 4194304 | tf_op jit(solution)/shard_map/pallas_call | solution.py:482
  79.1 11.2 %all_to_all.23.blocks = bf16[16,4,1152]{2,1,0:T(4,128)(2,1)S(1)} all-to-all(bf16[16,4,1152]{2,1,0:T(4,128)(2,1)S(1)} %get-tuple-element.16), channel_id=1, replica_groups=mesh['kv'=16,'head'=8] {'kv'}, dimensions={0} | all-to-all | bytes 294912 | tf_op jit(solution)/shard_map/all_to_all | solution.py:381
  90.4 0.0 copy-done.5
  90.4 0.4 shard_map.174.own
  90.8 0.1 collective-permute-start.10
  90.8 1.3 %collective-permute-done.10.near = f32[72,384]{1,0:T(8,128)S(1)} collective-permute-done((f32[72,384]{1,0:T(8,128)S(1)}, f32[72,384]{1,0:T(8,128)S(1)}, u32[]{:S(2)}, u32[]{:S(2)}) %collective-permute-start.10) | collective-permute-done | bytes 110624 | tf_op jit(solution)/shard_map/ppermute | solution.py:385
  92.2 2.0 %collective-permute-start.13 = (bf16[80,384]{1,0:T(8,128)(2,1)S(1)}, bf16[80,384]{1,0:T(8,128)(2,1)S(1)}, u32[]{:S(2)}, u32[]{:S(2)}) collective-permute-start(bf16[80,384]{1,0:T(8,128)(2,1)S(1)} %shard_map.175.own), channel_id=1, source_target_pairs={{0,4},{1,5},{2,6},{3,7},{4,0},{5,1},{6,2},{7,3},{8,12},{9,13},{10,... | collective-permute-start | bytes 184328 | tf_op jit(solution)/shard_map/ppermute | solution.py:397
  94.1 1.1 %collective-permute-start.12 = (bf16[80,384]{1,0:T(8,128)(2,1)S(1)}, bf16[80,384]{1,0:T(8,128)(2,1)S(1)}, u32[]{:S(2)}, u32[]{:S(2)}) collective-permute-start(bf16[80,384]{1,0:T(8,128)(2,1)S(1)} %shard_map.175.own), channel_id=1, source_target_pairs={{0,6},{1,7},{2,4},{3,5},{4,2},{5,3},{6,0},{7,1},{8,14},{9,15},{10,... | collective-permute-start | bytes 184328 | tf_op jit(solution)/shard_map/ppermute | solution.py:397
  95.2 0.5 collective-permute-start.11
  95.8 2.0 %shard_map.177 = f32[4,8,128,128]{3,2,1,0:T(8,128)} custom-call(f32[8,128,8]{2,1,0:T(8,128)S(1)} %get-tuple-element.18.turned, f32[8,16,128]{2,1,0:T(8,128)S(1)} %get-tuple-element.19.mixed, f32[1,8]{1,0:T(1,128)S(1)} %bitcast.21, f32[4,8,128,128]{3,2,1,0:T(8,128)S(1)} %copy-done.2), custom_call_target="tpu_custom_call" | custom-call | bytes 4194304 | tf_op jit(solution)/shard_map/pallas_call | solution.py:501
  97.8 0.3 collective-permute-done.13.cross
  98.0 1.6 %collective-permute-done.12.far = bf16[80,384]{1,0:T(8,128)(2,1)S(1)} collective-permute-done((bf16[80,384]{1,0:T(8,128)(2,1)S(1)}, bf16[80,384]{1,0:T(8,128)(2,1)S(1)}, u32[]{:S(2)}, u32[]{:S(2)}) %collective-permute-start.12) | collective-permute-done | bytes 61472 | tf_op jit(solution)/shard_map/ppermute | solution.py:397
  99.6 0.0 collective-permute-done.11.near
  99.6 0.7 shard_map.176
  (2 shorter events, 0.0 us)
Async XLA Ops:
  19.0 11.3 %copy-start = (bf16[64,1,256,128]{3,2,1,0:T(8,128)(2,1)S(1)}, bf16[64,1,256,128]{3,2,1,0:T(8,128)(2,1)}, u32[]{:S(2)}) copy-start(bf16[64,1,256,128]{3,2,1,0:T(8,128)(2,1)} %param.20) | copy-start | bytes 12582916
  19.0 11.3 %copy-start.1 = (bf16[64,1,256,128]{3,2,1,0:T(8,128)(2,1)S(1)}, bf16[64,1,256,128]{3,2,1,0:T(8,128)(2,1)}, u32[]{:S(2)}) copy-start(bf16[64,1,256,128]{3,2,1,0:T(8,128)(2,1)} %param.21) | copy-start | bytes 12582916
  30.3 20.2 %copy-start.4 = (bf16[1024,384]{1,0:T(8,128)(2,1)S(1)}, bf16[1024,384]{1,0:T(8,128)(2,1)}, u32[]{:S(2)}) copy-start(bf16[1024,384]{1,0:T(8,128)(2,1)} %weight.3) | copy-start | bytes 2359300
  30.3 31.8 %copy-start.3 = (bf16[384,4096]{1,0:T(8,128)(2,1)S(1)}, bf16[384,4096]{1,0:T(8,128)(2,1)}, u32[]{:S(2)}) copy-start(bf16[384,4096]{1,0:T(8,128)(2,1)} %weight.4) | copy-start | bytes 9437188
  30.3 31.8 %copy-start.6 = (bf16[64,384]{1,0:T(8,128)(2,1)S(1)}, bf16[64,384]{1,0:T(8,128)(2,1)}, u32[]{:S(2)}) copy-start(bf16[64,384]{1,0:T(8,128)(2,1)} %hidden.1) | copy-start | bytes 147460
  30.3 31.8 %copy-start.8 = (f32[384]{0:T(512)S(1)}, f32[384]{0:T(512)}, u32[]{:S(2)}) copy-start(f32[384]{0:T(512)} %param.25) | copy-start | bytes 4612
  30.3 31.8 %copy-start.9 = (s32[64]{0:T(128)S(1)}, s32[64]{0:T(128)}, u32[]{:S(2)}) copy-start(s32[64]{0:T(128)} %param.31) | copy-start | bytes 772
  33.4 6.7 %collective-permute-start.2 = (bf16[528,128]{1,0:T(8,128)(2,1)S(1)}, bf16[528,128]{1,0:T(8,128)(2,1)S(1)}, u32[]{:S(2)}, u32[]{:S(2)}) collective-permute-start(bf16[528,128]{1,0:T(8,128)(2,1)S(1)} %shard_map.169.own), channel_id=1, source_target_pairs={{0,16},{8,24},{16,0},{24,8},{32,48},{40,56},{48,32},{56,40},{64,80... | collective-permute-start | bytes 405512 | tf_op jit(solution)/shard_map/ppermute | solution.py:397
  34.7 6.8 %collective-permute-start.1 = (bf16[528,128]{1,0:T(8,128)(2,1)S(1)}, bf16[528,128]{1,0:T(8,128)(2,1)S(1)}, u32[]{:S(2)}, u32[]{:S(2)}) collective-permute-start(bf16[528,128]{1,0:T(8,128)(2,1)S(1)} %shard_map.169.own), channel_id=1, source_target_pairs={{0,24},{8,16},{16,8},{24,0},{32,56},{40,48},{48,40},{56,32},{64,88... | collective-permute-start | bytes 405512 | tf_op jit(solution)/shard_map/ppermute | solution.py:397
  36.7 5.0 %collective-permute-start = (bf16[528,128]{1,0:T(8,128)(2,1)S(1)}, bf16[528,128]{1,0:T(8,128)(2,1)S(1)}, u32[]{:S(2)}, u32[]{:S(2)}) collective-permute-start(bf16[528,128]{1,0:T(8,128)(2,1)S(1)} %shard_map.169.own), channel_id=1, source_target_pairs={{0,8},{8,0},{16,24},{24,16},{32,40},{40,32},{48,56},{56,48},{64,72... | collective-permute-start | bytes 405512 | tf_op jit(solution)/shard_map/ppermute | solution.py:397
  42.3 35.4 %copy-start.2 = (f32[4,8,128,128]{3,2,1,0:T(8,128)S(1)}, f32[4,8,128,128]{3,2,1,0:T(8,128)}, u32[]{:S(2)}) copy-start(f32[4,8,128,128]{3,2,1,0:T(8,128)} %states.3) | copy-start | bytes 6291460
  42.4 35.4 %copy-start.7 = (f32[1024]{0:T(1024)S(1)}, f32[1024]{0:T(1024)}, u32[]{:S(2)}) copy-start(f32[1024]{0:T(1024)} %param.29) | copy-start | bytes 12292
  42.4 35.4 %copy-start.10 = (f32[8]{0:T(128)S(1)}, f32[8]{0:T(128)}, u32[]{:S(2)}) copy-start(f32[8]{0:T(128)} %param.27) | copy-start | bytes 100
  42.4 6.7 %collective-permute-start.5 = (bf16[528,128]{1,0:T(8,128)(2,1)S(1)}, bf16[528,128]{1,0:T(8,128)(2,1)S(1)}, u32[]{:S(2)}, u32[]{:S(2)}) collective-permute-start(bf16[528,128]{1,0:T(8,128)(2,1)S(1)} %shard_map.170.own), channel_id=1, source_target_pairs={{0,64},{8,72},{16,80},{24,88},{32,96},{40,104},{48,112},{56,120},{... | collective-permute-start | bytes 405512 | tf_op jit(solution)/shard_map/ppermute | solution.py:397
  43.5 7.0 %collective-permute-start.4 = (bf16[528,128]{1,0:T(8,128)(2,1)S(1)}, bf16[528,128]{1,0:T(8,128)(2,1)S(1)}, u32[]{:S(2)}, u32[]{:S(2)}) collective-permute-start(bf16[528,128]{1,0:T(8,128)(2,1)S(1)} %shard_map.170.own), channel_id=1, source_target_pairs={{0,96},{8,104},{16,112},{24,120},{32,64},{40,72},{48,80},{56,88},{... | collective-permute-start | bytes 405512 | tf_op jit(solution)/shard_map/ppermute | solution.py:397
  45.4 5.0 %collective-permute-start.3 = (bf16[528,128]{1,0:T(8,128)(2,1)S(1)}, bf16[528,128]{1,0:T(8,128)(2,1)S(1)}, u32[]{:S(2)}, u32[]{:S(2)}) collective-permute-start(bf16[528,128]{1,0:T(8,128)(2,1)S(1)} %shard_map.170.own), channel_id=1, source_target_pairs={{0,32},{8,40},{16,48},{24,56},{32,0},{40,8},{48,16},{56,24},{64,96... | collective-permute-start | bytes 405512 | tf_op jit(solution)/shard_map/ppermute | solution.py:397
  51.4 1.4 %collective-permute-start.6 = (f32[64,384]{1,0:T(8,128)S(1)}, f32[64,384]{1,0:T(8,128)S(1)}, u32[]{:S(2)}, u32[]{:S(2)}) collective-permute-start(f32[64,384]{1,0:T(8,128)S(1)} %shard_map.171), channel_id=1, source_target_pairs={{0,1},{1,0},{2,3},{3,2},{4,5},{5,4},{6,7},{7,6},{8,9},{9,8},{10,11... | collective-permute-start | bytes 294920 | tf_op jit(solution)/shard_map/ppermute | solution.py:385
  52.8 6.0 %collective-permute-start.9 = (bf16[64,384]{1,0:T(8,128)(2,1)S(1)}, bf16[64,384]{1,0:T(8,128)(2,1)S(1)}, u32[]{:S(2)}, u32[]{:S(2)}) collective-permute-start(bf16[64,384]{1,0:T(8,128)(2,1)S(1)} %add_convert_fusion.own), channel_id=1, source_target_pairs={{0,4},{1,5},{2,6},{3,7},{4,0},{5,1},{6,2},{7,3},{8,12},{9,13},{10,... | collective-permute-start | bytes 147464 | tf_op jit(solution)/shard_map/ppermute | solution.py:397
  56.7 5.3 %collective-permute-start.8 = (bf16[64,384]{1,0:T(8,128)(2,1)S(1)}, bf16[64,384]{1,0:T(8,128)(2,1)S(1)}, u32[]{:S(2)}, u32[]{:S(2)}) collective-permute-start(bf16[64,384]{1,0:T(8,128)(2,1)S(1)} %add_convert_fusion.own), channel_id=1, source_target_pairs={{0,6},{1,7},{2,4},{3,5},{4,2},{5,3},{6,0},{7,1},{8,14},{9,15},{10,... | collective-permute-start | bytes 147464 | tf_op jit(solution)/shard_map/ppermute | solution.py:397
  57.4 4.6 %collective-permute-start.7 = (bf16[64,384]{1,0:T(8,128)(2,1)S(1)}, bf16[64,384]{1,0:T(8,128)(2,1)S(1)}, u32[]{:S(2)}, u32[]{:S(2)}) collective-permute-start(bf16[64,384]{1,0:T(8,128)(2,1)S(1)} %add_convert_fusion.own), channel_id=1, source_target_pairs={{0,2},{1,3},{2,0},{3,1},{4,6},{5,7},{6,4},{7,5},{8,10},{9,11},{10,... | collective-permute-start | bytes 147464 | tf_op jit(solution)/shard_map/ppermute | solution.py:397
  62.1 28.3 %copy-start.5 = (bf16[1024,384]{1,0:T(8,128)(2,1)S(1)}, bf16[1024,384]{1,0:T(8,128)(2,1)}, u32[]{:S(2)}) copy-start(bf16[1024,384]{1,0:T(8,128)(2,1)} %weight.5) | copy-start | bytes 2359300
  90.8 1.4 %collective-permute-start.10 = (f32[72,384]{1,0:T(8,128)S(1)}, f32[72,384]{1,0:T(8,128)S(1)}, u32[]{:S(2)}, u32[]{:S(2)}) collective-permute-start(f32[72,384]{1,0:T(8,128)S(1)} %shard_map.174.own), channel_id=1, source_target_pairs={{0,1},{1,0},{2,3},{3,2},{4,5},{5,4},{6,7},{7,6},{8,9},{9,8},{10,11... | collective-permute-start | bytes 331784 | tf_op jit(solution)/shard_map/ppermute | solution.py:385
  92.2 5.8 %collective-permute-start.13 = (bf16[80,384]{1,0:T(8,128)(2,1)S(1)}, bf16[80,384]{1,0:T(8,128)(2,1)S(1)}, u32[]{:S(2)}, u32[]{:S(2)}) collective-permute-start(bf16[80,384]{1,0:T(8,128)(2,1)S(1)} %shard_map.175.own), channel_id=1, source_target_pairs={{0,4},{1,5},{2,6},{3,7},{4,0},{5,1},{6,2},{7,3},{8,12},{9,13},{10,... | collective-permute-start | bytes 184328 | tf_op jit(solution)/shard_map/ppermute | solution.py:397
  94.1 5.4 %collective-permute-start.12 = (bf16[80,384]{1,0:T(8,128)(2,1)S(1)}, bf16[80,384]{1,0:T(8,128)(2,1)S(1)}, u32[]{:S(2)}, u32[]{:S(2)}) collective-permute-start(bf16[80,384]{1,0:T(8,128)(2,1)S(1)} %shard_map.175.own), channel_id=1, source_target_pairs={{0,6},{1,7},{2,4},{3,5},{4,2},{5,3},{6,0},{7,1},{8,14},{9,15},{10,... | collective-permute-start | bytes 184328 | tf_op jit(solution)/shard_map/ppermute | solution.py:397
  95.2 4.4 %collective-permute-start.11 = (bf16[80,384]{1,0:T(8,128)(2,1)S(1)}, bf16[80,384]{1,0:T(8,128)(2,1)S(1)}, u32[]{:S(2)}, u32[]{:S(2)}) collective-permute-start(bf16[80,384]{1,0:T(8,128)(2,1)S(1)} %shard_map.175.own), channel_id=1, source_target_pairs={{0,2},{1,3},{2,0},{3,1},{4,6},{5,7},{6,4},{7,5},{8,10},{9,11},{10,... | collective-permute-start | bytes 184328 | tf_op jit(solution)/shard_map/ppermute | solution.py:397

commit v5 on v4

--- a/solution.py
+++ b/solution.py
@@ -121,7 +121,7 @@
     projected = (total[:, :width] / jnp.sqrt(mean + EPS)).astype(BF16).astype(F32)
     for g in range(own.shape[1]):
         own[:, g, :] = projected[:, g * HD:(g + 1) * HD]
-    queries = own[:, :GQ, :].astype(BF16)
+    queries = own[:, :GQ, :].reshape(own.shape[0] * GQ, HD).astype(BF16)
     for p in range(out.shape[0]):
         out[p] = queries
 
@@ -133,7 +133,7 @@
     mixed[...] = jnp.zeros(mixed.shape, F32)
     token = iota((GQ, CH), 1)
     scale = 1.0 / math.sqrt(HD)
-    batch = 32
+    batch = 64
     mine = lax.axis_index("kv") * rows
 
     @pl.loop(0, slots, step=batch)
@@ -263,53 +263,44 @@
     return (own[...].astype(F32) + near[...].astype(F32)) + (far[...].astype(F32) + cross[...].astype(F32))
 
 
-def mixing_kernel(own, near, far, cross, hidden, gain, request, weight, out, middle, turned):
+def mixing_kernel(own, near, far, cross, hidden, gain, request, weight, out, middle):
     total = hidden[...].astype(F32) + four(own, near, far, cross)
     inner = total.astype(BF16)
     middle[...] = inner
     n = request.shape[1]
     pick = (as_column(request[...]) == iota((n, n), 1)).astype(F32).astype(BF16)
     ordered = jnp.dot(pick, inner, preferred_element_type=F32)
-    squares = jnp.sum(ordered * ordered, axis=1, keepdims=True)
-    upper = squares.astype(BF16).astype(F32)
+    upper, lower = halves(jnp.sum(ordered * ordered, axis=1, keepdims=True))
+    lane = iota((n, HD), 1)
+    tail = jnp.where(lane == 0, upper, jnp.where(lane == 1, lower, 0.0))
     scaled = jnp.concatenate(
         [(ordered[:, c * HD:(c + 1) * HD] * gain[c:c + 1, :]).astype(BF16) for c in range(gain.shape[0])], axis=1
     )
-    groups, height, _ = out.shape
-    rows = n // groups
+    groups, rows, _ = out.shape
     width = weight.shape[1]
-    used = rows * (width // HD)
-    step = 4
-    for c in range(0, width // HD, step):
-        y = jnp.dot(scaled, weight[:, c * HD:(c + step) * HD], preferred_element_type=F32)
+    step = 4 * HD
+    for c in range(0, width, step):
+        y = jnp.dot(scaled, weight[:, c:c + step], preferred_element_type=F32)
         for p in range(groups):
-            for k in range(step):
-                turned[p, k * rows:(k + 1) * rows, :] = y[p * rows:(p + 1) * rows, k * HD:(k + 1) * HD]
-        for p in range(groups):
-            out[p, c * rows:(c + step) * rows, :] = turned[p].astype(BF16)
-    lane, sub = iota((rows, HD), 1), iota((rows, HD), 0)
+            out[p, :, c:c + step] = y[p * rows:(p + 1) * rows].astype(BF16)
     for p in range(groups):
-        at = slice(p * rows, (p + 1) * rows)
-        both = jnp.where(lane == sub, upper[at], 0.0) + jnp.where(lane == sub + rows, (squares - upper)[at], 0.0)
-        line = jnp.sum(both, axis=0, keepdims=True)
-        out[p, used:, :] = jnp.where(iota((height - used, HD), 0) == 0, line, 0.0).astype(BF16)
-
-
-def lightning_kernel(parts, decay, states, gain, out, turned, mixed, flat):
+        out[p, :, width:] = tail[p * rows:(p + 1) * rows].astype(BF16)
+
+
+def lightning_kernel(parts, decay, states, gain, out, turned, mixed, flat, wide):
     rows, heads = states.shape[0], states.shape[1]
-    used = 4 * rows * heads
     total = parts[0].astype(F32)
     for p in range(1, parts.shape[0]):
         total = total + parts[p].astype(F32)
-    line = total[used:used + 1, :]
-    sums = line + pltpu.roll(line, HD - rows, axis=1)
-    block = 4 * rows
-    pattern = iota((block, HD), 1) == lax.rem(iota((block, HD), 0), rows)
-    squares = jnp.sum(jnp.where(pattern, sums, 0.0), axis=1, keepdims=True)
-    scale = jnp.sqrt(squares / D + EPS)
+    width = 4 * heads * HD
+    scale = jnp.sqrt((total[:, width:width + 1] + total[:, width + 1:width + 2]) / D + EPS)
+    wide[0:rows, :] = total[:, :width] / scale
+    for h in range(heads):
+        for k in range(4):
+            mixed[h, k * rows:(k + 1) * rows, :] = wide[0:rows, (4 * h + k) * HD:(4 * h + k + 1) * HD]
     keep = jnp.exp(-decay[...])
     span = range(heads)
-    mixing = [total[block * h:block * (h + 1), :] / scale for h in span]
+    mixing = [mixed[h] for h in span]
     below = [1.0 + jnp.exp(-m) for m in mixing]
     silu = [m / b for m, b in zip(mixing, below)]
     gates = [1.0 / b[3 * rows:] for b in below]
@@ -450,7 +441,7 @@
     )
     queries, own = kernel_call(
         normalise_kernel,
-        (S((peers, rows, GQ, HD), BF16), S((rows, GQ + 2, HD), F32)),
+        (S((peers, rows * GQ, HD), BF16), S((rows, GQ + 2, HD), F32)),
         [VMEM] + [HBM] * 2, 8 * MIB, 0, 8 * peers * rows * width,
     )(
         exchange(parts), in_hbm(keys), in_hbm(values)
@@ -471,12 +462,10 @@
         [VMEM] * 5, 8 * MIB, 2 * requests * GQ * HD * features, 2 * GQ * HD * features,
         [pltpu.VMEM((requests * GQ, HD), F32), pltpu.VMEM((requests, GQ * HD), BF16)],
     )(*along(part, "kv", 4), attn_out_weight)
-    height = rows * (lin_width // HD) + 16
     mixing, middle = kernel_call(
         mixing_kernel,
-        (S((peers, height, HD), BF16), S((requests, features), BF16)),
+        (S((peers, rows, lin_width + HD), BF16), S((requests, features), BF16)),
         [VMEM] * 8, 16 * MIB, 2 * requests * features * lin_width, 2 * features * lin_width,
-        [pltpu.VMEM((peers, 4 * rows, HD), F32)],
     )(*along((first + other_core(first)).astype(BF16), "head", 2), hidden_in, lin_gain.reshape(chunks, HD), request, lin_weight)
     decay = decay_rate[None, :]
     gated, turned, mixed = kernel_call(
@@ -487,7 +476,7 @@
             S((heads, 4 * rows, HD), F32),
         ),
         [VMEM] * 4, 16 * MIB, 0, 8 * rows * size * HD,
-        [pltpu.VMEM((8, size), F32)],
+        [pltpu.VMEM((8, size), F32), pltpu.VMEM((8, lin_width), F32)],
     )(exchange(mixing), decay, states, out_gain.reshape(heads, HD))
     second = kernel_call(
         lightning_out_kernel,

time: 101 us -> 99.9 us (0.989)
  no operation moved by 1% of the time
where the time goes in v5:
time: 99.9 us; the launch traced here: 99.7 us
  blocking collectives  53.3 us (53%)
  waiting for transfers between devices  18 us (18%)
  starting transfers between devices  15.9 us (16%)
  Pallas kernels  11.7 us (12%)
    all_to_all x4, blocking collectives, exchange(): return lax.all_to_all(blocks, 'kv', 0, 0, tiled=True)  53.3 us
    ppermute x12, starting transfers between devices, along(): lax.ppermute(value, axis, pairs)  15.7 us
    ppermute x12, waiting for transfers between devices, along(): lax.ppermute(value, axis, pairs)  15.4 us
    pallas_call x1, Pallas kernels, per_device(): kernel_call(attention_kernel, partial, [VMEM, VMEM, VMEM, SMEM, VMEM], 24...  2.92 us
    ppermute x2, waiting for transfers between devices, other_core(): lax.ppermute(value, 'head', [(i, i ^ 1) for i in range(lax.axis_size('hea...  2.59 us
  transfers between devices with their start and end apart: 14, of which 11 were waited for; matrix products, arithmetic and copies ran while one was open for 0% of the time, Pallas kernels for 2%

profile of v5, /device:TPU:0, one launch (start us, length us, event | category | flops | bytes accessed | tf_op | source)
XLA Modules:
  0.0 99.7 jit_solution(17699260413801975323)
XLA Ops:
  0.6 1.7 %shard_map.167 = (f32[16,4,1408]{2,1,0:T(4,128)S(1)}, s32[2,64]{1,0:T(2,128)S(1)}) custom-call(bf16[64,384]{1,0:T(8,128)(2,1)} %hidden.1, f32[3,128]{1,0:T(4,128)} %bitcast.22, bf16[384,1280]{1,0:T(8,128)(2,1)} %weight_hbm.1, s32[1,64]{1,0:T(1,128)} %bitcast.23, s32[1,64]{1,0:T(1,128)} %bitcast.24, s32[1,64]{1,0:T(1,128)} %bitcast.25), custom_call_target="tpu_custom_call" | custom-call | flops 62914560 | bytes 983040 | tf_op jit(solution)/shard_map/pallas_call | solution.py:425
  2.3 16.7 %all_to_all.20.parts = f32[16,4,1408]{2,1,0:T(4,128)S(1)} all-to-all(f32[16,4,1408]{2,1,0:T(4,128)S(1)} %get-tuple-element.11), channel_id=1, replica_groups=mesh['kv'=16,'head'=8] {'kv'}, dimensions={0} | all-to-all | bytes 720896 | tf_op jit(solution)/shard_map/all_to_all | solution.py:372
  19.0 0.0 copy-start
  19.0 0.0 copy-start.1
  19.0 0.1 shard_map.168
  19.1 11.1 %all_to_all.21 = bf16[16,32,128]{2,1,0:T(8,128)(2,1)S(1)} all-to-all(bf16[16,32,128]{2,1,0:T(8,128)(2,1)S(1)} %get-tuple-element.12), channel_id=1, replica_groups=mesh['kv'=16,'head'=8] {'kv'}, dimensions={0} | all-to-all | bytes 262144 | tf_op jit(solution)/shard_map/all_to_all | solution.py:372
  30.3 0.0 copy-done
  30.3 0.0 copy-done.1
  30.3 0.0 copy-start.4
  30.3 0.0 copy-start.3
  30.3 0.0 copy-start.6
  30.3 0.0 copy-start.8
  30.3 0.0 copy-start.9
  30.3 2.9 %shard_map.169.own = bf16[528,128]{1,0:T(8,128)(2,1)S(1)} custom-call(bf16[64,8,128]{2,1,0:T(8,128)(2,1)S(1)} %bitcast.15, bf16[64,256,128]{2,1,0:T(8,128)(2,1)S(1)} %bitcast.12, bf16[64,256,128]{2,1,0:T(8,128)(2,1)S(1)} %bitcast.14, s32[2,64]{1,0:T(2,128)S(1)} %get-tuple-element.13.info, f32[4,10,128]{2,1,0:T(8,128)S(1)} %get-tuple-element.14.own), custom_call_target="tpu_custom_call" | custom-call | flops 67108864 | bytes 8388608 | tf_op jit(solution)/shard_map/pallas_call | solution.py:452
  33.2 1.3 %collective-permute-start.2 = (bf16[528,128]{1,0:T(8,128)(2,1)S(1)}, bf16[528,128]{1,0:T(8,128)(2,1)S(1)}, u32[]{:S(2)}, u32[]{:S(2)}) collective-permute-start(bf16[528,128]{1,0:T(8,128)(2,1)S(1)} %shard_map.169.own), channel_id=1, source_target_pairs={{0,16},{8,24},{16,0},{24,8},{32,48},{40,56},{48,32},{56,40},{64,80... | collective-permute-start | bytes 405512 | tf_op jit(solution)/shard_map/ppermute | solution.py:388
  34.5 2.0 %collective-permute-start.1 = (bf16[528,128]{1,0:T(8,128)(2,1)S(1)}, bf16[528,128]{1,0:T(8,128)(2,1)S(1)}, u32[]{:S(2)}, u32[]{:S(2)}) collective-permute-start(bf16[528,128]{1,0:T(8,128)(2,1)S(1)} %shard_map.169.own), channel_id=1, source_target_pairs={{0,24},{8,16},{16,8},{24,0},{32,56},{40,48},{48,40},{56,32},{64,88... | collective-permute-start | bytes 405512 | tf_op jit(solution)/shard_map/ppermute | solution.py:388
  36.6 0.2 collective-permute-start
  36.8 3.1 %collective-permute-done.2.cross = bf16[528,128]{1,0:T(8,128)(2,1)S(1)} collective-permute-done((bf16[528,128]{1,0:T(8,128)(2,1)S(1)}, bf16[528,128]{1,0:T(8,128)(2,1)S(1)}, u32[]{:S(2)}, u32[]{:S(2)}) %collective-permute-start.2) | collective-permute-done | bytes 135200 | tf_op jit(solution)/shard_map/ppermute | solution.py:388
  39.9 1.4 %collective-permute-done.1.far = bf16[528,128]{1,0:T(8,128)(2,1)S(1)} collective-permute-done((bf16[528,128]{1,0:T(8,128)(2,1)S(1)}, bf16[528,128]{1,0:T(8,128)(2,1)S(1)}, u32[]{:S(2)}, u32[]{:S(2)}) %collective-permute-start.1) | collective-permute-done | bytes 135200 | tf_op jit(solution)/shard_map/ppermute | solution.py:388
  41.3 0.3 collective-permute-done.near
  41.6 0.6 shard_map.170.own
  42.2 0.0 copy-start.2
  42.2 0.0 copy-start.7
  42.2 0.0 copy-start.10
  42.3 1.1 %collective-permute-start.5 = (bf16[528,128]{1,0:T(8,128)(2,1)S(1)}, bf16[528,128]{1,0:T(8,128)(2,1)S(1)}, u32[]{:S(2)}, u32[]{:S(2)}) collective-permute-start(bf16[528,128]{1,0:T(8,128)(2,1)S(1)} %shard_map.170.own), channel_id=1, source_target_pairs={{0,64},{8,72},{16,80},{24,88},{32,96},{40,104},{48,112},{56,120},{... | collective-permute-start | bytes 405512 | tf_op jit(solution)/shard_map/ppermute | solution.py:388
  43.3 1.9 %collective-permute-start.4 = (bf16[528,128]{1,0:T(8,128)(2,1)S(1)}, bf16[528,128]{1,0:T(8,128)(2,1)S(1)}, u32[]{:S(2)}, u32[]{:S(2)}) collective-permute-start(bf16[528,128]{1,0:T(8,128)(2,1)S(1)} %shard_map.170.own), channel_id=1, source_target_pairs={{0,96},{8,104},{16,112},{24,120},{32,64},{40,72},{48,80},{56,88},{... | collective-permute-start | bytes 405512 | tf_op jit(solution)/shard_map/ppermute | solution.py:388
  45.3 0.6 collective-permute-start.3
  45.8 3.1 %collective-permute-done.5.cross = bf16[528,128]{1,0:T(8,128)(2,1)S(1)} collective-permute-done((bf16[528,128]{1,0:T(8,128)(2,1)S(1)}, bf16[528,128]{1,0:T(8,128)(2,1)S(1)}, u32[]{:S(2)}, u32[]{:S(2)}) %collective-permute-start.5) | collective-permute-done | bytes 135200 | tf_op jit(solution)/shard_map/ppermute | solution.py:388
  48.9 1.4 %collective-permute-done.4.far = bf16[528,128]{1,0:T(8,128)(2,1)S(1)} collective-permute-done((bf16[528,128]{1,0:T(8,128)(2,1)S(1)}, bf16[528,128]{1,0:T(8,128)(2,1)S(1)}, u32[]{:S(2)}, u32[]{:S(2)}) %collective-permute-start.4) | collective-permute-done | bytes 135200 | tf_op jit(solution)/shard_map/ppermute | solution.py:388
  50.3 0.0 collective-permute-done.3.near
  50.3 0.0 copy-done.4
  50.3 0.9 shard_map.171
  51.2 0.1 collective-permute-start.6
  51.3 1.3 %collective-permute-done.6 = f32[64,384]{1,0:T(8,128)S(1)} collective-permute-done((f32[64,384]{1,0:T(8,128)S(1)}, f32[64,384]{1,0:T(8,128)S(1)}, u32[]{:S(2)}, u32[]{:S(2)}) %collective-permute-start.6) | collective-permute-done | bytes 98336 | tf_op jit(solution)/shard_map/ppermute | solution.py:376
  52.6 4.0 %collective-permute-start.9 = (bf16[64,384]{1,0:T(8,128)(2,1)S(1)}, bf16[64,384]{1,0:T(8,128)(2,1)S(1)}, u32[]{:S(2)}, u32[]{:S(2)}) collective-permute-start(bf16[64,384]{1,0:T(8,128)(2,1)S(1)} %add_convert_fusion.own), channel_id=1, source_target_pairs={{0,4},{1,5},{2,6},{3,7},{4,0},{5,1},{6,2},{7,3},{8,12},{9,13},{10,... | collective-permute-start | bytes 147464 | tf_op jit(solution)/shard_map/ppermute | solution.py:388
  56.6 0.7 collective-permute-start.8
  57.3 0.3 collective-permute-start.7
  57.6 1.1 %collective-permute-done.9.cross = bf16[64,384]{1,0:T(8,128)(2,1)S(1)} collective-permute-done((bf16[64,384]{1,0:T(8,128)(2,1)S(1)}, bf16[64,384]{1,0:T(8,128)(2,1)S(1)}, u32[]{:S(2)}, u32[]{:S(2)}) %collective-permute-start.9) | collective-permute-done | bytes 49184 | tf_op jit(solution)/shard_map/ppermute | solution.py:388
  58.7 3.2 %collective-permute-done.8.far = bf16[64,384]{1,0:T(8,128)(2,1)S(1)} collective-permute-done((bf16[64,384]{1,0:T(8,128)(2,1)S(1)}, bf16[64,384]{1,0:T(8,128)(2,1)S(1)}, u32[]{:S(2)}, u32[]{:S(2)}) %collective-permute-start.8) | collective-permute-done | bytes 49184 | tf_op jit(solution)/shard_map/ppermute | solution.py:388
  61.9 0.0 collective-permute-done.7.near
  61.9 0.0 copy-done.3
  61.9 0.0 copy-done.6
  61.9 0.0 copy-done.8
  61.9 0.0 copy-done.9
  61.9 0.0 copy-start.5
  62.0 0.9 shard_map.172
  62.8 14.4 %all_to_all.22.parts = bf16[16,4,4224]{2,1,0:T(4,128)(2,1)S(1)} all-to-all(bf16[16,4,4224]{2,1,0:T(4,128)(2,1)S(1)} %get-tuple-element.15), channel_id=1, replica_groups=mesh['kv'=16,'head'=8] {'kv'}, dimensions={0} | all-to-all | bytes 1081344 | tf_op jit(solution)/shard_map/all_to_all | solution.py:372
  77.2 0.0 copy-done.2
  77.2 0.0 copy-done.7
  77.2 0.0 copy-done.10
  77.3 1.3 %shard_map.173 = (bf16[16,4,1152]{2,1,0:T(4,128)(2,1)S(1)}, f32[8,128,8]{2,1,0:T(8,128)S(1)}, f32[8,16,128]{2,1,0:T(8,128)S(1)}) custom-call(bf16[16,4,4224]{2,1,0:T(4,128)(2,1)S(1)} %all_to_all.22.parts, f32[1,8]{1,0:T(1,128)S(1)} %bitcast.20, f32[4,8,128,128]{3,2,1,0:T(8,128)S(1)} %copy-done.2, f32[8,128]{1,0:T(8,128)S(1)} %bitcast.16), custom_call_target="tpu_custom_call" | custom-call | bytes 4194304 | tf_op jit(solution)/shard_map/pallas_call | solution.py:471
  78.6 11.1 %all_to_all.23.blocks = bf16[16,4,1152]{2,1,0:T(4,128)(2,1)S(1)} all-to-all(bf16[16,4,1152]{2,1,0:T(4,128)(2,1)S(1)} %get-tuple-element.16), channel_id=1, replica_groups=mesh['kv'=16,'head'=8] {'kv'}, dimensions={0} | all-to-all | bytes 294912 | tf_op jit(solution)/shard_map/all_to_all | solution.py:372
  89.7 0.0 copy-done.5
  89.7 0.4 shard_map.174.own
  90.1 0.1 collective-permute-start.10
  90.2 1.3 %collective-permute-done.10.near = f32[72,384]{1,0:T(8,128)S(1)} collective-permute-done((f32[72,384]{1,0:T(8,128)S(1)}, f32[72,384]{1,0:T(8,128)S(1)}, u32[]{:S(2)}, u32[]{:S(2)}) %collective-permute-start.10) | collective-permute-done | bytes 110624 | tf_op jit(solution)/shard_map/ppermute | solution.py:376
  91.5 2.0 %collective-permute-start.13 = (bf16[80,384]{1,0:T(8,128)(2,1)S(1)}, bf16[80,384]{1,0:T(8,128)(2,1)S(1)}, u32[]{:S(2)}, u32[]{:S(2)}) collective-permute-start(bf16[80,384]{1,0:T(8,128)(2,1)S(1)} %shard_map.175.own), channel_id=1, source_target_pairs={{0,4},{1,5},{2,6},{3,7},{4,0},{5,1},{6,2},{7,3},{8,12},{9,13},{10,... | collective-permute-start | bytes 184328 | tf_op jit(solution)/shard_map/ppermute | solution.py:388
  93.5 1.0 %collective-permute-start.12 = (bf16[80,384]{1,0:T(8,128)(2,1)S(1)}, bf16[80,384]{1,0:T(8,128)(2,1)S(1)}, u32[]{:S(2)}, u32[]{:S(2)}) collective-permute-start(bf16[80,384]{1,0:T(8,128)(2,1)S(1)} %shard_map.175.own), channel_id=1, source_target_pairs={{0,6},{1,7},{2,4},{3,5},{4,2},{5,3},{6,0},{7,1},{8,14},{9,15},{10,... | collective-permute-start | bytes 184328 | tf_op jit(solution)/shard_map/ppermute | solution.py:388
  94.5 0.6 collective-permute-start.11
  95.1 2.0 %shard_map.177 = f32[4,8,128,128]{3,2,1,0:T(8,128)} custom-call(f32[8,128,8]{2,1,0:T(8,128)S(1)} %get-tuple-element.18.turned, f32[8,16,128]{2,1,0:T(8,128)S(1)} %get-tuple-element.19.mixed, f32[1,8]{1,0:T(1,128)S(1)} %bitcast.21, f32[4,8,128,128]{3,2,1,0:T(8,128)S(1)} %copy-done.2), custom_call_target="tpu_custom_call" | custom-call | bytes 4194304 | tf_op jit(solution)/shard_map/pallas_call | solution.py:490
  97.1 0.3 collective-permute-done.13.cross
  97.3 1.6 %collective-permute-done.12.far = bf16[80,384]{1,0:T(8,128)(2,1)S(1)} collective-permute-done((bf16[80,384]{1,0:T(8,128)(2,1)S(1)}, bf16[80,384]{1,0:T(8,128)(2,1)S(1)}, u32[]{:S(2)}, u32[]{:S(2)}) %collective-permute-start.12) | collective-permute-done | bytes 61472 | tf_op jit(solution)/shard_map/ppermute | solution.py:388
  98.9 0.0 collective-permute-done.11.near
  98.9 0.7 shard_map.176
  (2 shorter events, 0.0 us)
Async XLA Ops:
  19.0 11.3 %copy-start = (bf16[64,1,256,128]{3,2,1,0:T(8,128)(2,1)S(1)}, bf16[64,1,256,128]{3,2,1,0:T(8,128)(2,1)}, u32[]{:S(2)}) copy-start(bf16[64,1,256,128]{3,2,1,0:T(8,128)(2,1)} %param.20) | copy-start | bytes 12582916
  19.0 11.3 %copy-start.1 = (bf16[64,1,256,128]{3,2,1,0:T(8,128)(2,1)S(1)}, bf16[64,1,256,128]{3,2,1,0:T(8,128)(2,1)}, u32[]{:S(2)}) copy-start(bf16[64,1,256,128]{3,2,1,0:T(8,128)(2,1)} %param.21) | copy-start | bytes 12582916
  30.3 20.0 %copy-start.4 = (bf16[1024,384]{1,0:T(8,128)(2,1)S(1)}, bf16[1024,384]{1,0:T(8,128)(2,1)}, u32[]{:S(2)}) copy-start(bf16[1024,384]{1,0:T(8,128)(2,1)} %weight.3) | copy-start | bytes 2359300
  30.3 31.6 %copy-start.3 = (bf16[384,4096]{1,0:T(8,128)(2,1)S(1)}, bf16[384,4096]{1,0:T(8,128)(2,1)}, u32[]{:S(2)}) copy-start(bf16[384,4096]{1,0:T(8,128)(2,1)} %weight.4) | copy-start | bytes 9437188
  30.3 31.6 %copy-start.6 = (bf16[64,384]{1,0:T(8,128)(2,1)S(1)}, bf16[64,384]{1,0:T(8,128)(2,1)}, u32[]{:S(2)}) copy-start(bf16[64,384]{1,0:T(8,128)(2,1)} %hidden.1) | copy-start | bytes 147460
  30.3 31.6 %copy-start.8 = (f32[384]{0:T(512)S(1)}, f32[384]{0:T(512)}, u32[]{:S(2)}) copy-start(f32[384]{0:T(512)} %param.25) | copy-start | bytes 4612
  30.3 31.6 %copy-start.9 = (s32[64]{0:T(128)S(1)}, s32[64]{0:T(128)}, u32[]{:S(2)}) copy-start(s32[64]{0:T(128)} %param.31) | copy-start | bytes 772
  33.2 6.7 %collective-permute-start.2 = (bf16[528,128]{1,0:T(8,128)(2,1)S(1)}, bf16[528,128]{1,0:T(8,128)(2,1)S(1)}, u32[]{:S(2)}, u32[]{:S(2)}) collective-permute-start(bf16[528,128]{1,0:T(8,128)(2,1)S(1)} %shard_map.169.own), channel_id=1, source_target_pairs={{0,16},{8,24},{16,0},{24,8},{32,48},{40,56},{48,32},{56,40},{64,80... | collective-permute-start | bytes 405512 | tf_op jit(solution)/shard_map/ppermute | solution.py:388
  34.5 6.8 %collective-permute-start.1 = (bf16[528,128]{1,0:T(8,128)(2,1)S(1)}, bf16[528,128]{1,0:T(8,128)(2,1)S(1)}, u32[]{:S(2)}, u32[]{:S(2)}) collective-permute-start(bf16[528,128]{1,0:T(8,128)(2,1)S(1)} %shard_map.169.own), channel_id=1, source_target_pairs={{0,24},{8,16},{16,8},{24,0},{32,56},{40,48},{48,40},{56,32},{64,88... | collective-permute-start | bytes 405512 | tf_op jit(solution)/shard_map/ppermute | solution.py:388
  36.6 5.0 %collective-permute-start = (bf16[528,128]{1,0:T(8,128)(2,1)S(1)}, bf16[528,128]{1,0:T(8,128)(2,1)S(1)}, u32[]{:S(2)}, u32[]{:S(2)}) collective-permute-start(bf16[528,128]{1,0:T(8,128)(2,1)S(1)} %shard_map.169.own), channel_id=1, source_target_pairs={{0,8},{8,0},{16,24},{24,16},{32,40},{40,32},{48,56},{56,48},{64,72... | collective-permute-start | bytes 405512 | tf_op jit(solution)/shard_map/ppermute | solution.py:388
  42.2 35.0 %copy-start.2 = (f32[4,8,128,128]{3,2,1,0:T(8,128)S(1)}, f32[4,8,128,128]{3,2,1,0:T(8,128)}, u32[]{:S(2)}) copy-start(f32[4,8,128,128]{3,2,1,0:T(8,128)} %states.3) | copy-start | bytes 6291460
  42.2 35.0 %copy-start.7 = (f32[1024]{0:T(1024)S(1)}, f32[1024]{0:T(1024)}, u32[]{:S(2)}) copy-start(f32[1024]{0:T(1024)} %param.29) | copy-start | bytes 12292
  42.2 35.0 %copy-start.10 = (f32[8]{0:T(128)S(1)}, f32[8]{0:T(128)}, u32[]{:S(2)}) copy-start(f32[8]{0:T(128)} %param.27) | copy-start | bytes 100
  42.3 6.7 %collective-permute-start.5 = (bf16[528,128]{1,0:T(8,128)(2,1)S(1)}, bf16[528,128]{1,0:T(8,128)(2,1)S(1)}, u32[]{:S(2)}, u32[]{:S(2)}) collective-permute-start(bf16[528,128]{1,0:T(8,128)(2,1)S(1)} %shard_map.170.own), channel_id=1, source_target_pairs={{0,64},{8,72},{16,80},{24,88},{32,96},{40,104},{48,112},{56,120},{... | collective-permute-start | bytes 405512 | tf_op jit(solution)/shard_map/ppermute | solution.py:388
  43.3 7.0 %collective-permute-start.4 = (bf16[528,128]{1,0:T(8,128)(2,1)S(1)}, bf16[528,128]{1,0:T(8,128)(2,1)S(1)}, u32[]{:S(2)}, u32[]{:S(2)}) collective-permute-start(bf16[528,128]{1,0:T(8,128)(2,1)S(1)} %shard_map.170.own), channel_id=1, source_target_pairs={{0,96},{8,104},{16,112},{24,120},{32,64},{40,72},{48,80},{56,88},{... | collective-permute-start | bytes 405512 | tf_op jit(solution)/shard_map/ppermute | solution.py:388
  45.3 5.0 %collective-permute-start.3 = (bf16[528,128]{1,0:T(8,128)(2,1)S(1)}, bf16[528,128]{1,0:T(8,128)(2,1)S(1)}, u32[]{:S(2)}, u32[]{:S(2)}) collective-permute-start(bf16[528,128]{1,0:T(8,128)(2,1)S(1)} %shard_map.170.own), channel_id=1, source_target_pairs={{0,32},{8,40},{16,48},{24,56},{32,0},{40,8},{48,16},{56,24},{64,96... | collective-permute-start | bytes 405512 | tf_op jit(solution)/shard_map/ppermute | solution.py:388
  51.2 1.4 %collective-permute-start.6 = (f32[64,384]{1,0:T(8,128)S(1)}, f32[64,384]{1,0:T(8,128)S(1)}, u32[]{:S(2)}, u32[]{:S(2)}) collective-permute-start(f32[64,384]{1,0:T(8,128)S(1)} %shard_map.171), channel_id=1, source_target_pairs={{0,1},{1,0},{2,3},{3,2},{4,5},{5,4},{6,7},{7,6},{8,9},{9,8},{10,11... | collective-permute-start | bytes 294920 | tf_op jit(solution)/shard_map/ppermute | solution.py:376
  52.6 6.0 %collective-permute-start.9 = (bf16[64,384]{1,0:T(8,128)(2,1)S(1)}, bf16[64,384]{1,0:T(8,128)(2,1)S(1)}, u32[]{:S(2)}, u32[]{:S(2)}) collective-permute-start(bf16[64,384]{1,0:T(8,128)(2,1)S(1)} %add_convert_fusion.own), channel_id=1, source_target_pairs={{0,4},{1,5},{2,6},{3,7},{4,0},{5,1},{6,2},{7,3},{8,12},{9,13},{10,... | collective-permute-start | bytes 147464 | tf_op jit(solution)/shard_map/ppermute | solution.py:388
  56.6 5.3 %collective-permute-start.8 = (bf16[64,384]{1,0:T(8,128)(2,1)S(1)}, bf16[64,384]{1,0:T(8,128)(2,1)S(1)}, u32[]{:S(2)}, u32[]{:S(2)}) collective-permute-start(bf16[64,384]{1,0:T(8,128)(2,1)S(1)} %add_convert_fusion.own), channel_id=1, source_target_pairs={{0,6},{1,7},{2,4},{3,5},{4,2},{5,3},{6,0},{7,1},{8,14},{9,15},{10,... | collective-permute-start | bytes 147464 | tf_op jit(solution)/shard_map/ppermute | solution.py:388
  57.3 4.6 %collective-permute-start.7 = (bf16[64,384]{1,0:T(8,128)(2,1)S(1)}, bf16[64,384]{1,0:T(8,128)(2,1)S(1)}, u32[]{:S(2)}, u32[]{:S(2)}) collective-permute-start(bf16[64,384]{1,0:T(8,128)(2,1)S(1)} %add_convert_fusion.own), channel_id=1, source_target_pairs={{0,2},{1,3},{2,0},{3,1},{4,6},{5,7},{6,4},{7,5},{8,10},{9,11},{10,... | collective-permute-start | bytes 147464 | tf_op jit(solution)/shard_map/ppermute | solution.py:388
  61.9 27.8 %copy-start.5 = (bf16[1024,384]{1,0:T(8,128)(2,1)S(1)}, bf16[1024,384]{1,0:T(8,128)(2,1)}, u32[]{:S(2)}) copy-start(bf16[1024,384]{1,0:T(8,128)(2,1)} %weight.5) | copy-start | bytes 2359300
  90.1 1.4 %collective-permute-start.10 = (f32[72,384]{1,0:T(8,128)S(1)}, f32[72,384]{1,0:T(8,128)S(1)}, u32[]{:S(2)}, u32[]{:S(2)}) collective-permute-start(f32[72,384]{1,0:T(8,128)S(1)} %shard_map.174.own), channel_id=1, source_target_pairs={{0,1},{1,0},{2,3},{3,2},{4,5},{5,4},{6,7},{7,6},{8,9},{9,8},{10,11... | collective-permute-start | bytes 331784 | tf_op jit(solution)/shard_map/ppermute | solution.py:376
  91.5 5.8 %collective-permute-start.13 = (bf16[80,384]{1,0:T(8,128)(2,1)S(1)}, bf16[80,384]{1,0:T(8,128)(2,1)S(1)}, u32[]{:S(2)}, u32[]{:S(2)}) collective-permute-start(bf16[80,384]{1,0:T(8,128)(2,1)S(1)} %shard_map.175.own), channel_id=1, source_target_pairs={{0,4},{1,5},{2,6},{3,7},{4,0},{5,1},{6,2},{7,3},{8,12},{9,13},{10,... | collective-permute-start | bytes 184328 | tf_op jit(solution)/shard_map/ppermute | solution.py:388
  93.5 5.4 %collective-permute-start.12 = (bf16[80,384]{1,0:T(8,128)(2,1)S(1)}, bf16[80,384]{1,0:T(8,128)(2,1)S(1)}, u32[]{:S(2)}, u32[]{:S(2)}) collective-permute-start(bf16[80,384]{1,0:T(8,128)(2,1)S(1)} %shard_map.175.own), channel_id=1, source_target_pairs={{0,6},{1,7},{2,4},{3,5},{4,2},{5,3},{6,0},{7,1},{8,14},{9,15},{10,... | collective-permute-start | bytes 184328 | tf_op jit(solution)/shard_map/ppermute | solution.py:388
  94.5 4.4 %collective-permute-start.11 = (bf16[80,384]{1,0:T(8,128)(2,1)S(1)}, bf16[80,384]{1,0:T(8,128)(2,1)S(1)}, u32[]{:S(2)}, u32[]{:S(2)}) collective-permute-start(bf16[80,384]{1,0:T(8,128)(2,1)S(1)} %shard_map.175.own), channel_id=1, source_target_pairs={{0,2},{1,3},{2,0},{3,1},{4,6},{5,7},{6,4},{7,5},{8,10},{9,11},{10,... | collective-permute-start | bytes 184328 | tf_op jit(solution)/shard_map/ppermute | solution.py:388

commit v6 on v5

--- a/solution.py
+++ b/solution.py
@@ -38,12 +38,12 @@
     return jnp.sum(jnp.where(eye, column, jnp.zeros_like(column)), axis=0, keepdims=True)
 
 
-def kernel_call(body, outs, ins, limit, flops, moved, scratch=()):
+def kernel_call(body, outs, ins, limit, flops, moved, scratch=(), space=pltpu.VMEM):
     return pl.pallas_call(
         body,
         out_shape=outs,
         in_specs=ins,
-        out_specs=jax.tree.map(lambda _: pl.BlockSpec(memory_space=pltpu.VMEM), outs),
+        out_specs=jax.tree.map(lambda _: pl.BlockSpec(memory_space=space), outs),
         scratch_shapes=scratch,
         compiler_params=pltpu.CompilerParams(vmem_limit_bytes=limit),
         cost_estimate=pl.CostEstimate(flops=flops, bytes_accessed=moved, transcendentals=0),
@@ -133,34 +133,27 @@
     mixed[...] = jnp.zeros(mixed.shape, F32)
     token = iota((GQ, CH), 1)
     scale = 1.0 / math.sqrt(HD)
-    batch = 64
     mine = lax.axis_index("kv") * rows
-
-    @pl.loop(0, slots, step=batch)
-    def _(base):
-        span = [base + u for u in range(batch)]
-        owners = [info[0, s] for s in span]
-        scores = [
-            lax.dot_general(
-                queries[jnp.minimum(r, REQ - 1)], keys[s], (((1,), (1,)), ((), ())),
-                preferred_element_type=F32,
-            ) * scale
-            for r, s in zip(owners, span)
-        ]
-        live = [token < info[1, s] for s in span]
-        scores = [jnp.where(m, x, NEGATIVE) for m, x in zip(live, scores)]
-        tops = [jnp.max(x, axis=1, keepdims=True) for x in scores]
-        weights = [jnp.where(m, jnp.exp(x - t), 0.0) for m, x, t in zip(live, scores, tops)]
-        totals = [jnp.sum(w, axis=1, keepdims=True) for w in weights]
-        mixes = [
-            jnp.dot(w.astype(BF16), values[s], preferred_element_type=F32) for w, s in zip(weights, span)
-        ]
-        for r, s, top, total, mix in zip(owners, span, tops, totals, mixes):
-            wide = jnp.broadcast_to(top, (GQ, HD))
-            best[r] = jnp.maximum(best[r], wide)
-            slot_max[s] = wide
-            slot_sum[s] = jnp.broadcast_to(total, (GQ, HD))
-            slot_value[s] = mix
+    span = range(slots)
+    owners = [info[0, s] for s in span]
+    scores = [
+        lax.dot_general(
+            queries[jnp.minimum(r, REQ - 1)], keys[s], (((1,), (1,)), ((), ())), preferred_element_type=F32
+        ) * scale
+        for r, s in zip(owners, span)
+    ]
+    live = [token < info[1, s] for s in span]
+    scores = [jnp.where(m, x, NEGATIVE) for m, x in zip(live, scores)]
+    tops = [jnp.max(x, axis=1, keepdims=True) for x in scores]
+    weights = [jnp.where(m, jnp.exp(x - t), 0.0) for m, x, t in zip(live, scores, tops)]
+    totals = [jnp.sum(w, axis=1, keepdims=True) for w in weights]
+    mixes = [jnp.dot(w.astype(BF16), values[s], preferred_element_type=F32) for w, s in zip(weights, span)]
+    for r, s, top, total, mix in zip(owners, span, tops, totals, mixes):
+        wide = jnp.broadcast_to(top, (GQ, HD))
+        best[r] = jnp.maximum(best[r], wide)
+        slot_max[s] = wide
+        slot_sum[s] = jnp.broadcast_to(total, (GQ, HD))
+        slot_value[s] = mix
 
     fresh = [
         jnp.broadcast_to(
@@ -176,16 +169,10 @@
         factor = jnp.exp(fresh[i] - best[mine + i])
         summed[mine + i] = factor
         mixed[mine + i] = factor * own[i, GQ + 1:GQ + 2, :]
-    step = 8
-
-    @pl.loop(0, slots, step=step)
-    def _(base):
-        for u in range(step):
-            s = base + u
-            r = info[0, s]
-            factor = jnp.exp(slot_max[s] - best[r])
-            summed[r] = summed[r] + factor * slot_sum[s]
-            mixed[r] = mixed[r] + factor * slot_value[s]
+    for r, s in zip(owners, span):
+        factor = jnp.exp(slot_max[s] - best[r])
+        summed[r] = summed[r] + factor * slot_sum[s]
+        mixed[r] = mixed[r] + factor * slot_value[s]
 
     lane, sub = iota((GQ, HD), 1), iota((GQ, HD), 0)
     line = iota((LINES, HD), 0)
@@ -304,14 +291,15 @@
     below = [1.0 + jnp.exp(-m) for m in mixing]
     silu = [m / b for m, b in zip(mixing, below)]
     gates = [1.0 / b[3 * rows:] for b in below]
-    columns = [v[:2 * rows].T for v in silu]
+    columns = jnp.concatenate([v[:2 * rows] for v in silu], axis=0).T
+    turned[...] = columns
     for h in span:
         mixed[h] = silu[h]
-        turned[h] = columns[h]
     inner = [jnp.sum(v[:rows] * v[rows:2 * rows], axis=1, keepdims=True) for v in silu]
     for j in range(rows):
         for h in span:
-            read = jnp.sum(columns[h][:, j:j + 1] * states[j, h], axis=0, keepdims=True)
+            at = 2 * rows * h + j
+            read = jnp.sum(columns[:, at:at + 1] * states[j, h], axis=0, keepdims=True)
             flat[j:j + 1, h * HD:(h + 1) * HD] = read
     read_squares = jnp.zeros((rows, 1), F32)
     for h in span:
@@ -329,14 +317,18 @@
         out[p, :, size:] = tail
 
 
-def renew_kernel(turned, mixed, decay, states, renewed):
+def renew_kernel(turned, mixed, decay, states, renewed, block, sems):
     rows, heads = states.shape[0], states.shape[1]
-    keep_row = jnp.exp(-decay[...])
-    for h in range(heads):
-        keep = keep_row[:, h:h + 1]
-        for j in range(rows):
+    keep = jnp.exp(-decay[...])
+    copies = [pltpu.make_async_copy(block.at[j], renewed.at[j], sems.at[j]) for j in range(rows)]
+    for j in range(rows):
+        for h in range(heads):
             value = mixed[h, 2 * rows + j:2 * rows + j + 1, :]
-            renewed[j, h] = keep * states[j, h] + turned[h, :, rows + j:rows + j + 1] * value
+            at = 2 * rows * h + rows + j
+            block[j, h] = keep[:, h:h + 1] * states[j, h] + turned[:, at:at + 1] * value
+        copies[j].start()
+    for copy in copies:
+        copy.wait()
 
 
 def lightning_out_kernel(blocks, request, weight, out, flat):
@@ -472,7 +464,7 @@
         lightning_kernel,
         (
             S((peers, rows, size + HD), BF16),
-            S((heads, HD, 2 * rows), F32),
+            S((HD, 2 * rows * heads), F32),
             S((heads, 4 * rows, HD), F32),
         ),
         [VMEM] * 4, 16 * MIB, 0, 8 * rows * size * HD,
@@ -489,6 +481,7 @@
     )(second, other_core(second))
     renewed = kernel_call(
         renew_kernel, S(states.shape, F32), [VMEM] * 4, 8 * MIB, 0, 8 * rows * size * HD,
+        [pltpu.VMEM(states.shape, F32), pltpu.SemaphoreType.DMA((rows,))], pltpu.HBM,
     )(turned, mixed, decay, states)
     hidden_out = kernel_call(
         last_kernel,

time: 99.9 us -> 99.6 us (level)
  no operation moved by 1% of the time
where the time goes in v6:
time: 99.6 us; the launch traced here: 99.4 us
  blocking collectives  53.3 us (54%)
  waiting for transfers between devices  18.3 us (18%)
  starting transfers between devices  15.9 us (16%)
  Pallas kernels  11 us (11%)
    all_to_all x4, blocking collectives, exchange(): return lax.all_to_all(blocks, 'kv', 0, 0, tiled=True)  53.3 us
    ppermute x12, waiting for transfers between devices, along(): lax.ppermute(value, axis, pairs)  15.7 us
    ppermute x12, starting transfers between devices, along(): lax.ppermute(value, axis, pairs)  15.7 us
    pallas_call x1, Pallas kernels, per_device(): kernel_call(attention_kernel, partial, [VMEM, VMEM, VMEM, SMEM, VMEM], 24...  2.63 us
    ppermute x2, waiting for transfers between devices, other_core(): lax.ppermute(value, 'head', [(i, i ^ 1) for i in range(lax.axis_size('hea...  2.59 us
  transfers between devices with their start and end apart: 14, of which 11 were waited for; matrix products, arithmetic and copies ran while one was open for 0% of the time, Pallas kernels for 2%

profile of v6, /device:TPU:0, one launch (start us, length us, event | category | flops | bytes accessed | tf_op | source)
XLA Modules:
  0.0 99.4 jit_solution(7532041581774708872)
XLA Ops:
  0.6 1.7 %shard_map.167 = (f32[16,4,1408]{2,1,0:T(4,128)S(1)}, s32[2,64]{1,0:T(2,128)S(1)}) custom-call(bf16[64,384]{1,0:T(8,128)(2,1)} %hidden.1, f32[3,128]{1,0:T(4,128)} %bitcast.22, bf16[384,1280]{1,0:T(8,128)(2,1)} %weight_hbm.1, s32[1,64]{1,0:T(1,128)} %bitcast.23, s32[1,64]{1,0:T(1,128)} %bitcast.24, s32[1,64]{1,0:T(1,128)} %bitcast.25), custom_call_target="tpu_custom_call" | custom-call | flops 62914560 | bytes 983040 | tf_op jit(solution)/shard_map/pallas_call | solution.py:417
  2.3 16.7 %all_to_all.20.parts = f32[16,4,1408]{2,1,0:T(4,128)S(1)} all-to-all(f32[16,4,1408]{2,1,0:T(4,128)S(1)} %get-tuple-element.11), channel_id=1, replica_groups=mesh['kv'=16,'head'=8] {'kv'}, dimensions={0} | all-to-all | bytes 720896 | tf_op jit(solution)/shard_map/all_to_all | solution.py:364
  19.0 0.0 copy-start
  19.0 0.0 copy-start.1
  19.0 0.1 shard_map.168
  19.1 11.1 %all_to_all.21 = bf16[16,32,128]{2,1,0:T(8,128)(2,1)S(1)} all-to-all(bf16[16,32,128]{2,1,0:T(8,128)(2,1)S(1)} %get-tuple-element.12), channel_id=1, replica_groups=mesh['kv'=16,'head'=8] {'kv'}, dimensions={0} | all-to-all | bytes 262144 | tf_op jit(solution)/shard_map/all_to_all | solution.py:364
  30.3 0.0 copy-done
  30.3 0.0 copy-done.1
  30.3 0.0 copy-start.4
  30.3 0.0 copy-start.3
  30.3 0.0 copy-start.6
  30.3 0.0 copy-start.8
  30.3 0.0 copy-start.9
  30.3 2.6 %shard_map.169.own = bf16[528,128]{1,0:T(8,128)(2,1)S(1)} custom-call(bf16[64,8,128]{2,1,0:T(8,128)(2,1)S(1)} %bitcast.15, bf16[64,256,128]{2,1,0:T(8,128)(2,1)S(1)} %bitcast.12, bf16[64,256,128]{2,1,0:T(8,128)(2,1)S(1)} %bitcast.14, s32[2,64]{1,0:T(2,128)S(1)} %get-tuple-element.13.info, f32[4,10,128]{2,1,0:T(8,128)S(1)} %get-tuple-element.14.own), custom_call_target="tpu_custom_call" | custom-call | flops 67108864 | bytes 8388608 | tf_op jit(solution)/shard_map/pallas_call | solution.py:444
  33.0 1.3 %collective-permute-start.2 = (bf16[528,128]{1,0:T(8,128)(2,1)S(1)}, bf16[528,128]{1,0:T(8,128)(2,1)S(1)}, u32[]{:S(2)}, u32[]{:S(2)}) collective-permute-start(bf16[528,128]{1,0:T(8,128)(2,1)S(1)} %shard_map.169.own), channel_id=1, source_target_pairs={{0,16},{8,24},{16,0},{24,8},{32,48},{40,56},{48,32},{56,40},{64,80... | collective-permute-start | bytes 405512 | tf_op jit(solution)/shard_map/ppermute | solution.py:380
  34.2 2.0 %collective-permute-start.1 = (bf16[528,128]{1,0:T(8,128)(2,1)S(1)}, bf16[528,128]{1,0:T(8,128)(2,1)S(1)}, u32[]{:S(2)}, u32[]{:S(2)}) collective-permute-start(bf16[528,128]{1,0:T(8,128)(2,1)S(1)} %shard_map.169.own), channel_id=1, source_target_pairs={{0,24},{8,16},{16,8},{24,0},{32,56},{40,48},{48,40},{56,32},{64,88... | collective-permute-start | bytes 405512 | tf_op jit(solution)/shard_map/ppermute | solution.py:380
  36.3 0.3 collective-permute-start
  36.5 3.1 %collective-permute-done.2.cross = bf16[528,128]{1,0:T(8,128)(2,1)S(1)} collective-permute-done((bf16[528,128]{1,0:T(8,128)(2,1)S(1)}, bf16[528,128]{1,0:T(8,128)(2,1)S(1)}, u32[]{:S(2)}, u32[]{:S(2)}) %collective-permute-start.2) | collective-permute-done | bytes 135200 | tf_op jit(solution)/shard_map/ppermute | solution.py:380
  39.6 1.4 %collective-permute-done.1.far = bf16[528,128]{1,0:T(8,128)(2,1)S(1)} collective-permute-done((bf16[528,128]{1,0:T(8,128)(2,1)S(1)}, bf16[528,128]{1,0:T(8,128)(2,1)S(1)}, u32[]{:S(2)}, u32[]{:S(2)}) %collective-permute-start.1) | collective-permute-done | bytes 135200 | tf_op jit(solution)/shard_map/ppermute | solution.py:380
  41.0 0.3 collective-permute-done.near
  41.3 0.6 shard_map.170.own
  41.9 0.0 copy-start.2
  41.9 0.0 copy-start.7
  42.0 0.0 copy-start.10
  42.0 1.1 %collective-permute-start.5 = (bf16[528,128]{1,0:T(8,128)(2,1)S(1)}, bf16[528,128]{1,0:T(8,128)(2,1)S(1)}, u32[]{:S(2)}, u32[]{:S(2)}) collective-permute-start(bf16[528,128]{1,0:T(8,128)(2,1)S(1)} %shard_map.170.own), channel_id=1, source_target_pairs={{0,64},{8,72},{16,80},{24,88},{32,96},{40,104},{48,112},{56,120},{... | collective-permute-start | bytes 405512 | tf_op jit(solution)/shard_map/ppermute | solution.py:380
  43.1 1.9 %collective-permute-start.4 = (bf16[528,128]{1,0:T(8,128)(2,1)S(1)}, bf16[528,128]{1,0:T(8,128)(2,1)S(1)}, u32[]{:S(2)}, u32[]{:S(2)}) collective-permute-start(bf16[528,128]{1,0:T(8,128)(2,1)S(1)} %shard_map.170.own), channel_id=1, source_target_pairs={{0,96},{8,104},{16,112},{24,120},{32,64},{40,72},{48,80},{56,88},{... | collective-permute-start | bytes 405512 | tf_op jit(solution)/shard_map/ppermute | solution.py:380
  45.0 0.6 collective-permute-start.3
  45.5 3.1 %collective-permute-done.5.cross = bf16[528,128]{1,0:T(8,128)(2,1)S(1)} collective-permute-done((bf16[528,128]{1,0:T(8,128)(2,1)S(1)}, bf16[528,128]{1,0:T(8,128)(2,1)S(1)}, u32[]{:S(2)}, u32[]{:S(2)}) %collective-permute-start.5) | collective-permute-done | bytes 135200 | tf_op jit(solution)/shard_map/ppermute | solution.py:380
  48.6 1.4 %collective-permute-done.4.far = bf16[528,128]{1,0:T(8,128)(2,1)S(1)} collective-permute-done((bf16[528,128]{1,0:T(8,128)(2,1)S(1)}, bf16[528,128]{1,0:T(8,128)(2,1)S(1)}, u32[]{:S(2)}, u32[]{:S(2)}) %collective-permute-start.4) | collective-permute-done | bytes 135200 | tf_op jit(solution)/shard_map/ppermute | solution.py:380
  50.0 0.0 collective-permute-done.3.near
  50.0 0.0 copy-done.4
  50.0 0.9 shard_map.171
  51.0 0.1 collective-permute-start.6
  51.1 1.3 %collective-permute-done.6 = f32[64,384]{1,0:T(8,128)S(1)} collective-permute-done((f32[64,384]{1,0:T(8,128)S(1)}, f32[64,384]{1,0:T(8,128)S(1)}, u32[]{:S(2)}, u32[]{:S(2)}) %collective-permute-start.6) | collective-permute-done | bytes 98336 | tf_op jit(solution)/shard_map/ppermute | solution.py:368
  52.4 4.0 %collective-permute-start.9 = (bf16[64,384]{1,0:T(8,128)(2,1)S(1)}, bf16[64,384]{1,0:T(8,128)(2,1)S(1)}, u32[]{:S(2)}, u32[]{:S(2)}) collective-permute-start(bf16[64,384]{1,0:T(8,128)(2,1)S(1)} %add_convert_fusion.own), channel_id=1, source_target_pairs={{0,4},{1,5},{2,6},{3,7},{4,0},{5,1},{6,2},{7,3},{8,12},{9,13},{10,... | collective-permute-start | bytes 147464 | tf_op jit(solution)/shard_map/ppermute | solution.py:380
  56.3 0.7 collective-permute-start.8
  57.0 0.3 collective-permute-start.7
  57.3 1.0 %collective-permute-done.9.cross = bf16[64,384]{1,0:T(8,128)(2,1)S(1)} collective-permute-done((bf16[64,384]{1,0:T(8,128)(2,1)S(1)}, bf16[64,384]{1,0:T(8,128)(2,1)S(1)}, u32[]{:S(2)}, u32[]{:S(2)}) %collective-permute-start.9) | collective-permute-done | bytes 49184 | tf_op jit(solution)/shard_map/ppermute | solution.py:380
  58.4 3.2 %collective-permute-done.8.far = bf16[64,384]{1,0:T(8,128)(2,1)S(1)} collective-permute-done((bf16[64,384]{1,0:T(8,128)(2,1)S(1)}, bf16[64,384]{1,0:T(8,128)(2,1)S(1)}, u32[]{:S(2)}, u32[]{:S(2)}) %collective-permute-start.8) | collective-permute-done | bytes 49184 | tf_op jit(solution)/shard_map/ppermute | solution.py:380
  61.6 0.0 collective-permute-done.7.near
  61.6 0.0 copy-done.3
  61.6 0.0 copy-done.6
  61.6 0.0 copy-done.8
  61.6 0.0 copy-done.9
  61.7 0.0 copy-start.5
  61.7 0.9 shard_map.172
  62.5 14.4 %all_to_all.22.parts = bf16[16,4,4224]{2,1,0:T(4,128)(2,1)S(1)} all-to-all(bf16[16,4,4224]{2,1,0:T(4,128)(2,1)S(1)} %get-tuple-element.15), channel_id=1, replica_groups=mesh['kv'=16,'head'=8] {'kv'}, dimensions={0} | all-to-all | bytes 1081344 | tf_op jit(solution)/shard_map/all_to_all | solution.py:364
  77.0 0.0 copy-done.2
  77.0 0.0 copy-done.7
  77.0 0.0 copy-done.10
  77.0 1.3 %shard_map.173 = (bf16[16,4,1152]{2,1,0:T(4,128)(2,1)S(1)}, f32[128,64]{1,0:T(8,128)S(1)}, f32[8,16,128]{2,1,0:T(8,128)S(1)}) custom-call(bf16[16,4,4224]{2,1,0:T(4,128)(2,1)S(1)} %all_to_all.22.parts, f32[1,8]{1,0:T(1,128)S(1)} %bitcast.20, f32[4,8,128,128]{3,2,1,0:T(8,128)S(1)} %copy-done.2, f32[8,128]{1,0:T(8,128)S(1)} %bitcast.16), custom_call_target="tpu_custom_call" | custom-call | bytes 4194304 | tf_op jit(solution)/shard_map/pallas_call | solution.py:463
  78.3 11.1 %all_to_all.23.blocks = bf16[16,4,1152]{2,1,0:T(4,128)(2,1)S(1)} all-to-all(bf16[16,4,1152]{2,1,0:T(4,128)(2,1)S(1)} %get-tuple-element.16), channel_id=1, replica_groups=mesh['kv'=16,'head'=8] {'kv'}, dimensions={0} | all-to-all | bytes 294912 | tf_op jit(solution)/shard_map/all_to_all | solution.py:364
  89.4 0.0 copy-done.5
  89.4 0.4 shard_map.174.own
  89.8 0.1 collective-permute-start.10
  89.9 1.3 %collective-permute-done.10.near = f32[72,384]{1,0:T(8,128)S(1)} collective-permute-done((f32[72,384]{1,0:T(8,128)S(1)}, f32[72,384]{1,0:T(8,128)S(1)}, u32[]{:S(2)}, u32[]{:S(2)}) %collective-permute-start.10) | collective-permute-done | bytes 110624 | tf_op jit(solution)/shard_map/ppermute | solution.py:368
  91.2 1.9 %collective-permute-start.13 = (bf16[80,384]{1,0:T(8,128)(2,1)S(1)}, bf16[80,384]{1,0:T(8,128)(2,1)S(1)}, u32[]{:S(2)}, u32[]{:S(2)}) collective-permute-start(bf16[80,384]{1,0:T(8,128)(2,1)S(1)} %shard_map.175.own), channel_id=1, source_target_pairs={{0,4},{1,5},{2,6},{3,7},{4,0},{5,1},{6,2},{7,3},{8,12},{9,13},{10,... | collective-permute-start | bytes 184328 | tf_op jit(solution)/shard_map/ppermute | solution.py:380
  93.2 1.0 %collective-permute-start.12 = (bf16[80,384]{1,0:T(8,128)(2,1)S(1)}, bf16[80,384]{1,0:T(8,128)(2,1)S(1)}, u32[]{:S(2)}, u32[]{:S(2)}) collective-permute-start(bf16[80,384]{1,0:T(8,128)(2,1)S(1)} %shard_map.175.own), channel_id=1, source_target_pairs={{0,6},{1,7},{2,4},{3,5},{4,2},{5,3},{6,0},{7,1},{8,14},{9,15},{10,... | collective-permute-start | bytes 184328 | tf_op jit(solution)/shard_map/ppermute | solution.py:380
  94.2 0.6 collective-permute-start.11
  94.8 1.6 %shard_map.177 = f32[4,8,128,128]{3,2,1,0:T(8,128)} custom-call(f32[128,64]{1,0:T(8,128)S(1)} %get-tuple-element.18.turned, f32[8,16,128]{2,1,0:T(8,128)S(1)} %get-tuple-element.19.mixed, f32[1,8]{1,0:T(1,128)S(1)} %bitcast.21, f32[4,8,128,128]{3,2,1,0:T(8,128)S(1)} %copy-done.2), custom_call_target="tpu_custom_call" | custom-call | bytes 4194304 | tf_op jit(solution)/shard_map/pallas_call | solution.py:482
  96.4 0.7 collective-permute-done.13.cross
  97.1 1.6 %collective-permute-done.12.far = bf16[80,384]{1,0:T(8,128)(2,1)S(1)} collective-permute-done((bf16[80,384]{1,0:T(8,128)(2,1)S(1)}, bf16[80,384]{1,0:T(8,128)(2,1)S(1)}, u32[]{:S(2)}, u32[]{:S(2)}) %collective-permute-start.12) | collective-permute-done | bytes 61472 | tf_op jit(solution)/shard_map/ppermute | solution.py:380
  98.6 0.0 collective-permute-done.11.near
  98.6 0.7 shard_map.176
  (2 shorter events, 0.0 us)
Async XLA Ops:
  19.0 11.3 %copy-start = (bf16[64,1,256,128]{3,2,1,0:T(8,128)(2,1)S(1)}, bf16[64,1,256,128]{3,2,1,0:T(8,128)(2,1)}, u32[]{:S(2)}) copy-start(bf16[64,1,256,128]{3,2,1,0:T(8,128)(2,1)} %param.20) | copy-start | bytes 12582916
  19.0 11.3 %copy-start.1 = (bf16[64,1,256,128]{3,2,1,0:T(8,128)(2,1)S(1)}, bf16[64,1,256,128]{3,2,1,0:T(8,128)(2,1)}, u32[]{:S(2)}) copy-start(bf16[64,1,256,128]{3,2,1,0:T(8,128)(2,1)} %param.21) | copy-start | bytes 12582916
  30.3 19.8 %copy-start.4 = (bf16[1024,384]{1,0:T(8,128)(2,1)S(1)}, bf16[1024,384]{1,0:T(8,128)(2,1)}, u32[]{:S(2)}) copy-start(bf16[1024,384]{1,0:T(8,128)(2,1)} %weight.3) | copy-start | bytes 2359300
  30.3 31.4 %copy-start.3 = (bf16[384,4096]{1,0:T(8,128)(2,1)S(1)}, bf16[384,4096]{1,0:T(8,128)(2,1)}, u32[]{:S(2)}) copy-start(bf16[384,4096]{1,0:T(8,128)(2,1)} %weight.4) | copy-start | bytes 9437188
  30.3 31.4 %copy-start.6 = (bf16[64,384]{1,0:T(8,128)(2,1)S(1)}, bf16[64,384]{1,0:T(8,128)(2,1)}, u32[]{:S(2)}) copy-start(bf16[64,384]{1,0:T(8,128)(2,1)} %hidden.1) | copy-start | bytes 147460
  30.3 31.4 %copy-start.8 = (f32[384]{0:T(512)S(1)}, f32[384]{0:T(512)}, u32[]{:S(2)}) copy-start(f32[384]{0:T(512)} %param.25) | copy-start | bytes 4612
  30.3 31.3 %copy-start.9 = (s32[64]{0:T(128)S(1)}, s32[64]{0:T(128)}, u32[]{:S(2)}) copy-start(s32[64]{0:T(128)} %param.31) | copy-start | bytes 772
  33.0 6.7 %collective-permute-start.2 = (bf16[528,128]{1,0:T(8,128)(2,1)S(1)}, bf16[528,128]{1,0:T(8,128)(2,1)S(1)}, u32[]{:S(2)}, u32[]{:S(2)}) collective-permute-start(bf16[528,128]{1,0:T(8,128)(2,1)S(1)} %shard_map.169.own), channel_id=1, source_target_pairs={{0,16},{8,24},{16,0},{24,8},{32,48},{40,56},{48,32},{56,40},{64,80... | collective-permute-start | bytes 405512 | tf_op jit(solution)/shard_map/ppermute | solution.py:380
  34.2 6.8 %collective-permute-start.1 = (bf16[528,128]{1,0:T(8,128)(2,1)S(1)}, bf16[528,128]{1,0:T(8,128)(2,1)S(1)}, u32[]{:S(2)}, u32[]{:S(2)}) collective-permute-start(bf16[528,128]{1,0:T(8,128)(2,1)S(1)} %shard_map.169.own), channel_id=1, source_target_pairs={{0,24},{8,16},{16,8},{24,0},{32,56},{40,48},{48,40},{56,32},{64,88... | collective-permute-start | bytes 405512 | tf_op jit(solution)/shard_map/ppermute | solution.py:380
  36.3 5.0 %collective-permute-start = (bf16[528,128]{1,0:T(8,128)(2,1)S(1)}, bf16[528,128]{1,0:T(8,128)(2,1)S(1)}, u32[]{:S(2)}, u32[]{:S(2)}) collective-permute-start(bf16[528,128]{1,0:T(8,128)(2,1)S(1)} %shard_map.169.own), channel_id=1, source_target_pairs={{0,8},{8,0},{16,24},{24,16},{32,40},{40,32},{48,56},{56,48},{64,72... | collective-permute-start | bytes 405512 | tf_op jit(solution)/shard_map/ppermute | solution.py:380
  41.9 35.0 %copy-start.2 = (f32[4,8,128,128]{3,2,1,0:T(8,128)S(1)}, f32[4,8,128,128]{3,2,1,0:T(8,128)}, u32[]{:S(2)}) copy-start(f32[4,8,128,128]{3,2,1,0:T(8,128)} %states.3) | copy-start | bytes 6291460
  41.9 35.0 %copy-start.7 = (f32[1024]{0:T(1024)S(1)}, f32[1024]{0:T(1024)}, u32[]{:S(2)}) copy-start(f32[1024]{0:T(1024)} %param.29) | copy-start | bytes 12292
  42.0 35.0 %copy-start.10 = (f32[8]{0:T(128)S(1)}, f32[8]{0:T(128)}, u32[]{:S(2)}) copy-start(f32[8]{0:T(128)} %param.27) | copy-start | bytes 100
  42.0 6.7 %collective-permute-start.5 = (bf16[528,128]{1,0:T(8,128)(2,1)S(1)}, bf16[528,128]{1,0:T(8,128)(2,1)S(1)}, u32[]{:S(2)}, u32[]{:S(2)}) collective-permute-start(bf16[528,128]{1,0:T(8,128)(2,1)S(1)} %shard_map.170.own), channel_id=1, source_target_pairs={{0,64},{8,72},{16,80},{24,88},{32,96},{40,104},{48,112},{56,120},{... | collective-permute-start | bytes 405512 | tf_op jit(solution)/shard_map/ppermute | solution.py:380
  43.1 7.0 %collective-permute-start.4 = (bf16[528,128]{1,0:T(8,128)(2,1)S(1)}, bf16[528,128]{1,0:T(8,128)(2,1)S(1)}, u32[]{:S(2)}, u32[]{:S(2)}) collective-permute-start(bf16[528,128]{1,0:T(8,128)(2,1)S(1)} %shard_map.170.own), channel_id=1, source_target_pairs={{0,96},{8,104},{16,112},{24,120},{32,64},{40,72},{48,80},{56,88},{... | collective-permute-start | bytes 405512 | tf_op jit(solution)/shard_map/ppermute | solution.py:380
  45.0 5.1 %collective-permute-start.3 = (bf16[528,128]{1,0:T(8,128)(2,1)S(1)}, bf16[528,128]{1,0:T(8,128)(2,1)S(1)}, u32[]{:S(2)}, u32[]{:S(2)}) collective-permute-start(bf16[528,128]{1,0:T(8,128)(2,1)S(1)} %shard_map.170.own), channel_id=1, source_target_pairs={{0,32},{8,40},{16,48},{24,56},{32,0},{40,8},{48,16},{56,24},{64,96... | collective-permute-start | bytes 405512 | tf_op jit(solution)/shard_map/ppermute | solution.py:380
  51.0 1.4 %collective-permute-start.6 = (f32[64,384]{1,0:T(8,128)S(1)}, f32[64,384]{1,0:T(8,128)S(1)}, u32[]{:S(2)}, u32[]{:S(2)}) collective-permute-start(f32[64,384]{1,0:T(8,128)S(1)} %shard_map.171), channel_id=1, source_target_pairs={{0,1},{1,0},{2,3},{3,2},{4,5},{5,4},{6,7},{7,6},{8,9},{9,8},{10,11... | collective-permute-start | bytes 294920 | tf_op jit(solution)/shard_map/ppermute | solution.py:368
  52.4 6.0 %collective-permute-start.9 = (bf16[64,384]{1,0:T(8,128)(2,1)S(1)}, bf16[64,384]{1,0:T(8,128)(2,1)S(1)}, u32[]{:S(2)}, u32[]{:S(2)}) collective-permute-start(bf16[64,384]{1,0:T(8,128)(2,1)S(1)} %add_convert_fusion.own), channel_id=1, source_target_pairs={{0,4},{1,5},{2,6},{3,7},{4,0},{5,1},{6,2},{7,3},{8,12},{9,13},{10,... | collective-permute-start | bytes 147464 | tf_op jit(solution)/shard_map/ppermute | solution.py:380
  56.3 5.3 %collective-permute-start.8 = (bf16[64,384]{1,0:T(8,128)(2,1)S(1)}, bf16[64,384]{1,0:T(8,128)(2,1)S(1)}, u32[]{:S(2)}, u32[]{:S(2)}) collective-permute-start(bf16[64,384]{1,0:T(8,128)(2,1)S(1)} %add_convert_fusion.own), channel_id=1, source_target_pairs={{0,6},{1,7},{2,4},{3,5},{4,2},{5,3},{6,0},{7,1},{8,14},{9,15},{10,... | collective-permute-start | bytes 147464 | tf_op jit(solution)/shard_map/ppermute | solution.py:380
  57.0 4.6 %collective-permute-start.7 = (bf16[64,384]{1,0:T(8,128)(2,1)S(1)}, bf16[64,384]{1,0:T(8,128)(2,1)S(1)}, u32[]{:S(2)}, u32[]{:S(2)}) collective-permute-start(bf16[64,384]{1,0:T(8,128)(2,1)S(1)} %add_convert_fusion.own), channel_id=1, source_target_pairs={{0,2},{1,3},{2,0},{3,1},{4,6},{5,7},{6,4},{7,5},{8,10},{9,11},{10,... | collective-permute-start | bytes 147464 | tf_op jit(solution)/shard_map/ppermute | solution.py:380
  61.7 27.8 %copy-start.5 = (bf16[1024,384]{1,0:T(8,128)(2,1)S(1)}, bf16[1024,384]{1,0:T(8,128)(2,1)}, u32[]{:S(2)}) copy-start(bf16[1024,384]{1,0:T(8,128)(2,1)} %weight.5) | copy-start | bytes 2359300
  89.8 1.4 %collective-permute-start.10 = (f32[72,384]{1,0:T(8,128)S(1)}, f32[72,384]{1,0:T(8,128)S(1)}, u32[]{:S(2)}, u32[]{:S(2)}) collective-permute-start(f32[72,384]{1,0:T(8,128)S(1)} %shard_map.174.own), channel_id=1, source_target_pairs={{0,1},{1,0},{2,3},{3,2},{4,5},{5,4},{6,7},{7,6},{8,9},{9,8},{10,11... | collective-permute-start | bytes 331784 | tf_op jit(solution)/shard_map/ppermute | solution.py:368
  91.2 5.8 %collective-permute-start.13 = (bf16[80,384]{1,0:T(8,128)(2,1)S(1)}, bf16[80,384]{1,0:T(8,128)(2,1)S(1)}, u32[]{:S(2)}, u32[]{:S(2)}) collective-permute-start(bf16[80,384]{1,0:T(8,128)(2,1)S(1)} %shard_map.175.own), channel_id=1, source_target_pairs={{0,4},{1,5},{2,6},{3,7},{4,0},{5,1},{6,2},{7,3},{8,12},{9,13},{10,... | collective-permute-start | bytes 184328 | tf_op jit(solution)/shard_map/ppermute | solution.py:380
  93.2 5.4 %collective-permute-start.12 = (bf16[80,384]{1,0:T(8,128)(2,1)S(1)}, bf16[80,384]{1,0:T(8,128)(2,1)S(1)}, u32[]{:S(2)}, u32[]{:S(2)}) collective-permute-start(bf16[80,384]{1,0:T(8,128)(2,1)S(1)} %shard_map.175.own), channel_id=1, source_target_pairs={{0,6},{1,7},{2,4},{3,5},{4,2},{5,3},{6,0},{7,1},{8,14},{9,15},{10,... | collective-permute-start | bytes 184328 | tf_op jit(solution)/shard_map/ppermute | solution.py:380
  94.2 4.4 %collective-permute-start.11 = (bf16[80,384]{1,0:T(8,128)(2,1)S(1)}, bf16[80,384]{1,0:T(8,128)(2,1)S(1)}, u32[]{:S(2)}, u32[]{:S(2)}) collective-permute-start(bf16[80,384]{1,0:T(8,128)(2,1)S(1)} %shard_map.175.own), channel_id=1, source_target_pairs={{0,2},{1,3},{2,0},{3,1},{4,6},{5,7},{6,4},{7,5},{8,10},{9,11},{10,... | collective-permute-start | bytes 184328 | tf_op jit(solution)/shard_map/ppermute | solution.py:380

commit v7 on v6

--- a/solution.py
+++ b/solution.py
@@ -65,8 +65,8 @@
 
 
 def project_kernel(
-    hidden_hbm, gain_hbm, weight_hbm, counts_hbm, tails_hbm, slots_hbm, out, info,
-    hidden, gain, weight, counts, tails, slots, sems,
+    hidden_hbm, gain_hbm, weight_hbm, counts_hbm, tails_hbm, slots_hbm, own, cross, far, near, info,
+    hidden, gain, weight, counts, tails, slots, whole, sems,
 ):
     chunks = gain.shape[0]
     first = [(hidden_hbm, hidden), (gain_hbm, gain)]
@@ -104,36 +104,47 @@
     for c in range(chunks):
         copies[2 + c].wait()
         y = y + jnp.dot(scaled[c], weight[c * HD:(c + 1) * HD, :], preferred_element_type=F32)
-    groups, rows, _ = out.shape
     width = weight.shape[1]
-    wide = jnp.broadcast_to(squares, (x.shape[0], HD))
-    for p in range(groups):
-        out[p, :, :width] = y[p * rows:(p + 1) * rows]
-        out[p, :, width:] = wide[p * rows:(p + 1) * rows]
-
-
-def normalise_kernel(parts, keys, values, out, own):
-    total = parts[0]
-    for p in range(1, parts.shape[0]):
-        total = total + parts[p]
-    width = own.shape[1] * HD
-    mean = total[:, width:width + 1] / D
-    projected = (total[:, :width] / jnp.sqrt(mean + EPS)).astype(BF16).astype(F32)
-    for g in range(own.shape[1]):
-        own[:, g, :] = projected[:, g * HD:(g + 1) * HD]
-    queries = own[:, :GQ, :].reshape(own.shape[0] * GQ, HD).astype(BF16)
-    for p in range(out.shape[0]):
-        out[p] = queries
-
-
-def attention_kernel(queries, keys, values, info, own, out, slot_max, slot_sum, slot_value, best, summed, mixed):
+    whole[:, :width] = y
+    whole[:, width:] = jnp.broadcast_to(squares, (x.shape[0], HD))
+    place = lax.rem(lax.axis_index("kv"), 4)
+    rows = own.shape[0]
+    for k, part in enumerate((own, near, cross, far)):
+        at = pl.multiple_of(jnp.bitwise_xor(place, k) * rows, rows)
+        part[...] = whole[pl.ds(at, rows), :]
+
+
+def sum_kernel(own, near, far, cross, keys, values, out):
+    out[...] = four(own, near, far, cross)
+
+
+def normalise_kernel(one, near, far, cross, out, own, tiles):
+    total = four(one, near, far, cross)
+    columns = own.shape[1]
+    width = columns * HD
+    scale = jnp.sqrt(total[:, width:width + 1] / D + EPS)
+    projected = (total[:, :width] / scale).astype(BF16).astype(F32)
+    for g in range(columns):
+        tiles[:, g, :] = projected[:, g * HD:(g + 1) * HD]
+    out[...] = tiles[:, :GQ, :].astype(BF16)
+    rows = own.shape[0]
+    own[...] = tiles[pl.ds(lax.div(lax.axis_index("kv"), 4) * rows, rows)]
+
+
+def attention_kernel(
+    one, near, far, cross, keys, values, info, own, out, slot_max, slot_sum, slot_value, best, summed, mixed, queries
+):
     slots, rows = keys.shape[0], own.shape[0]
     best[...] = jnp.full(best.shape, NEGATIVE, F32)
     summed[...] = jnp.zeros(summed.shape, F32)
     mixed[...] = jnp.zeros(mixed.shape, F32)
     token = iota((GQ, CH), 1)
     scale = 1.0 / math.sqrt(HD)
-    mine = lax.axis_index("kv") * rows
+    place = lax.rem(lax.axis_index("kv"), 4)
+    quarter = one.shape[0]
+    for k, part in enumerate((one, near, cross, far)):
+        queries[pl.ds(jnp.bitwise_xor(place, k) * quarter, quarter)] = part[...]
+    mine = place * quarter + lax.div(lax.axis_index("kv"), 4) * rows
     span = range(slots)
     owners = [info[0, s] for s in span]
     scores = [
@@ -368,16 +379,20 @@
     return lax.ppermute(value, "head", [(i, i ^ 1) for i in range(lax.axis_size("head"))])
 
 
+def spread(parts, axis, stride):
+    size = lax.axis_size(axis)
+    own, *others = parts
+    return (
+        own,
+        *(
+            lax.ppermute(part, axis, [(i, i ^ (k * stride)) for i in range(size)])
+            for part, k in zip(others, (1, 3, 2))
+        ),
+    )
+
+
 def along(value, axis, stride):
-    size = lax.axis_size(axis)
-
-    def place(i):
-        return i // stride % 4
-
-    near = [(i, i ^ stride) for i in range(size)]
-    far = [(i, i + (3 - 2 * place(i)) * stride) for i in range(size)]
-    cross = [(i, i ^ (2 * stride)) for i in range(size)]
-    return (value, *(lax.ppermute(value, axis, pairs) for pairs in (near, far, cross)))
+    return spread([value] * 4, axis, stride)
 
 
 def per_device(
@@ -414,9 +429,11 @@
     values = cache_values.reshape(slots, CH, HD)
     plan = stretch_counts[None, :], tail_tokens[None, :], slot_stretch[None, :]
 
-    parts, info = kernel_call(
+    quarter = requests // 4
+    block = S((quarter, width + HD), F32)
+    own, cross, far, near, info = kernel_call(
         project_kernel,
-        (S((peers, rows, width + HD), F32), S((2, slots), jnp.int32)),
+        (block, block, block, block, S((2, slots), jnp.int32)),
         [HBM] * 6, 8 * MIB, 2 * requests * features * width, 2 * features * width,
         [
             pltpu.VMEM((requests, features), BF16),
@@ -425,26 +442,29 @@
             pltpu.VMEM((1, requests), jnp.int32),
             pltpu.VMEM((1, requests), jnp.int32),
             pltpu.VMEM((1, slots), jnp.int32),
+            pltpu.VMEM((requests, width + HD), F32),
             pltpu.SemaphoreType.DMA((5 + chunks,)),
         ],
     )(
         in_hbm(hidden_in), in_hbm(attn_gain.reshape(chunks, HD)), in_hbm(attn_weight),
         *(in_hbm(row) for row in plan),
     )
+    parts = kernel_call(
+        sum_kernel, block, [VMEM] * 4 + [HBM] * 2, 8 * MIB, 0, 20 * quarter * width,
+    )(*spread((own, near, far, cross), "kv", 1), in_hbm(keys), in_hbm(values))
     queries, own = kernel_call(
         normalise_kernel,
-        (S((peers, rows * GQ, HD), BF16), S((rows, GQ + 2, HD), F32)),
-        [VMEM] + [HBM] * 2, 8 * MIB, 0, 8 * peers * rows * width,
-    )(
-        exchange(parts), in_hbm(keys), in_hbm(values)
-    )
-    queries = exchange(queries).reshape(requests, GQ, HD)
+        (S((quarter, GQ, HD), BF16), S((rows, GQ + 2, HD), F32)),
+        [VMEM] * 4, 8 * MIB, 0, 20 * quarter * width,
+        [pltpu.VMEM((quarter, GQ + 2, HD), F32)],
+    )(*along(parts, "kv", 4))
     tiles = [pltpu.VMEM((slots, GQ, HD), F32)] * 3 + [pltpu.VMEM((requests + 1, GQ, HD), F32)] * 3
+    tiles.append(pltpu.VMEM((requests, GQ, HD), BF16))
     partial = S((requests * GQ + LINES, HD), BF16)
     part = kernel_call(
         attention_kernel, partial,
-        [VMEM, VMEM, VMEM, SMEM, VMEM], 24 * MIB, 4 * slots * GQ * CH * HD, 4 * slots * CH * HD, tiles,
-    )(queries, keys, values, info, own)
+        [VMEM] * 6 + [SMEM, VMEM], 24 * MIB, 4 * slots * GQ * CH * HD, 4 * slots * CH * HD, tiles,
+    )(*along(queries, "kv", 1), keys, values, info, own)
     part = kernel_call(
         merge_kernel, partial, [VMEM] * 4, 8 * MIB, 0, 10 * requests * GQ * HD,
     )(*along(part, "kv", 1))

time: 99.6 us -> 98 us (0.984)
  blocking collectives: 53.3 us -> 25.9 us
  waiting for transfers between devices: 18.3 us -> 31.8 us
  starting transfers between devices: 15.9 us -> 28.1 us
    all_to_all x4 -> x2, blocking collectives: 53.3 us -> 25.9 us  [exchange(): return lax.all_to_all(blocks, 'kv', 0, 0, tiled=True)]
    ppermute x12 -> x21, waiting for transfers between devices: 15.7 us -> 29.2 us  [spread(): lax.ppermute(part, axis, [(i, i ^ k * stride) for i in range(size)])]
    ppermute x12 -> x21, starting transfers between devices: 15.7 us -> 28 us  [spread(): lax.ppermute(part, axis, [(i, i ^ k * stride) for i in range(size)])]
    pallas_call x3 -> x4, Pallas kernels: 4.45 us -> 4.52 us  [the longest x1 2.62 us: per_device(): kernel_call(attention_kernel, partial, [VMEM] * 6 + [SMEM, VMEM], 24 * MI...]
  transfers between devices with their start and end apart: 14 -> 23, of which waited for: 11 -> 18; matrix products, arithmetic and copies ran while one was open for 0% -> 0% of each run, Pallas kernels for 2% -> 2%
where the time goes in v7:
time: 98 us; the launch traced here: 97.7 us
  waiting for transfers between devices  31.8 us (32%)
  starting transfers between devices  28.1 us (29%)
  blocking collectives  25.9 us (26%)
  Pallas kernels  11 us (11%)
    ppermute x21, waiting for transfers between devices, spread(): lax.ppermute(part, axis, [(i, i ^ k * stride) for i in range(size)])  29.2 us
    ppermute x21, starting transfers between devices, spread(): lax.ppermute(part, axis, [(i, i ^ k * stride) for i in range(size)])  28 us
    all_to_all x2, blocking collectives, exchange(): return lax.all_to_all(blocks, 'kv', 0, 0, tiled=True)  25.9 us
    pallas_call x1, Pallas kernels, per_device(): kernel_call(attention_kernel, partial, [VMEM] * 6 + [SMEM, VMEM], 24 * MI...  2.62 us
    ppermute x2, waiting for transfers between devices, other_core(): lax.ppermute(value, 'head', [(i, i ^ 1) for i in range(lax.axis_size('hea...  2.59 us
  transfers between devices with their start and end apart: 23, of which 18 were waited for; matrix products, arithmetic and copies ran while one was open for 0% of the time, Pallas kernels for 2%

profile of v7, /device:TPU:0, one launch (start us, length us, event | category | flops | bytes accessed | tf_op | source)
XLA Modules:
  0.0 97.7 jit_solution(9750859143333842863)
XLA Ops:
  0.6 1.7 %shard_map.167 = (f32[16,1408]{1,0:T(8,128)S(1)}, f32[16,1408]{1,0:T(8,128)S(1)}, f32[16,1408]{1,0:T(8,128)S(1)}, f32[16,1408]{1,0:T(8,128)S(1)}, s32[2,64]{1,0:T(2,128)S(1)}) custom-call(bf16[64,384]{1,0:T(8,128)(2,1)} %hidden.1, f32[3,128]{1,0:T(4,128)} %bitcast.20, bf16[384,1280]{1,0:T(8,128)(2,1)} %weight_hbm.1, s32[1,64]{1,0:T(1,128)} %bitcast.21, ...), custom_call_target="tpu_custom_call" | custom-call | flops 62914560 | bytes 983040 | tf_op jit(solution)/shard_map/pallas_call | solution.py:434
  2.4 1.7 %collective-permute-start = (f32[16,1408]{1,0:T(8,128)S(1)}, f32[16,1408]{1,0:T(8,128)S(1)}, u32[]{:S(2)}, u32[]{:S(2)}) collective-permute-start(f32[16,1408]{1,0:T(8,128)S(1)} %get-tuple-element.15), channel_id=1, source_target_pairs={{0,8},{8,0},{16,24},{24,16},{32,40},{40,32},{48,56},{56,48},{64,72... | collective-permute-start | bytes 270344 | tf_op jit(solution)/shard_map/ppermute | solution.py:388
  4.0 2.1 %collective-permute-start.1 = (f32[16,1408]{1,0:T(8,128)S(1)}, f32[16,1408]{1,0:T(8,128)S(1)}, u32[]{:S(2)}, u32[]{:S(2)}) collective-permute-start(f32[16,1408]{1,0:T(8,128)S(1)} %get-tuple-element.16), channel_id=1, source_target_pairs={{0,24},{8,16},{16,8},{24,0},{32,56},{40,48},{48,40},{56,32},{64,88... | collective-permute-start | bytes 270344 | tf_op jit(solution)/shard_map/ppermute | solution.py:388
  6.1 0.6 collective-permute-start.2
  6.8 0.2 collective-permute-done.near
  7.0 3.8 %collective-permute-done.1.far = f32[16,1408]{1,0:T(8,128)S(1)} collective-permute-done((f32[16,1408]{1,0:T(8,128)S(1)}, f32[16,1408]{1,0:T(8,128)S(1)}, u32[]{:S(2)}, u32[]{:S(2)}) %collective-permute-start.1) | collective-permute-done | bytes 90144 | tf_op jit(solution)/shard_map/ppermute | solution.py:388
  10.7 1.4 %collective-permute-done.2.cross = f32[16,1408]{1,0:T(8,128)S(1)} collective-permute-done((f32[16,1408]{1,0:T(8,128)S(1)}, f32[16,1408]{1,0:T(8,128)S(1)}, u32[]{:S(2)}, u32[]{:S(2)}) %collective-permute-start.2) | collective-permute-done | bytes 90144 | tf_op jit(solution)/shard_map/ppermute | solution.py:388
  12.2 3.3 %collective-permute-start.5 = (f32[16,1408]{1,0:T(8,128)S(1)}, f32[16,1408]{1,0:T(8,128)S(1)}, u32[]{:S(2)}, u32[]{:S(2)}) collective-permute-start(f32[16,1408]{1,0:T(8,128)S(1)} %shard_map.168.one), channel_id=1, source_target_pairs={{0,64},{8,72},{16,80},{24,88},{32,96},{40,104},{48,112},{56,120},{... | collective-permute-start | bytes 270344 | tf_op jit(solution)/shard_map/ppermute | solution.py:388
  15.5 1.1 %collective-permute-start.4 = (f32[16,1408]{1,0:T(8,128)S(1)}, f32[16,1408]{1,0:T(8,128)S(1)}, u32[]{:S(2)}, u32[]{:S(2)}) collective-permute-start(f32[16,1408]{1,0:T(8,128)S(1)} %shard_map.168.one), channel_id=1, source_target_pairs={{0,96},{8,104},{16,112},{24,120},{32,64},{40,72},{48,80},{56,88},{... | collective-permute-start | bytes 270344 | tf_op jit(solution)/shard_map/ppermute | solution.py:388
  16.5 0.0 collective-permute-start.3
  16.5 1.9 %collective-permute-done.5.cross = f32[16,1408]{1,0:T(8,128)S(1)} collective-permute-done((f32[16,1408]{1,0:T(8,128)S(1)}, f32[16,1408]{1,0:T(8,128)S(1)}, u32[]{:S(2)}, u32[]{:S(2)}) %collective-permute-start.5) | collective-permute-done | bytes 90144 | tf_op jit(solution)/shard_map/ppermute | solution.py:388
  18.4 2.8 %collective-permute-done.4.far = f32[16,1408]{1,0:T(8,128)S(1)} collective-permute-done((f32[16,1408]{1,0:T(8,128)S(1)}, f32[16,1408]{1,0:T(8,128)S(1)}, u32[]{:S(2)}, u32[]{:S(2)}) %collective-permute-start.4) | collective-permute-done | bytes 90144 | tf_op jit(solution)/shard_map/ppermute | solution.py:388
  21.2 0.0 collective-permute-done.3.near
  21.2 0.1 shard_map.169
  21.4 1.2 %collective-permute-start.8 = (bf16[16,8,128]{2,1,0:T(8,128)(2,1)S(1)}, bf16[16,8,128]{2,1,0:T(8,128)(2,1)S(1)}, u32[]{:S(2)}, u32[]{:S(2)}) collective-permute-start(bf16[16,8,128]{2,1,0:T(8,128)(2,1)S(1)} %get-tuple-element.18.one), channel_id=1, source_target_pairs={{0,16},{8,24},{16,0},{24,8},{32,48},{40,56},{48,32},{56,40},{64,80... | collective-permute-start | bytes 98312 | tf_op jit(solution)/shard_map/ppermute | solution.py:388
  22.5 2.2 %collective-permute-start.7 = (bf16[16,8,128]{2,1,0:T(8,128)(2,1)S(1)}, bf16[16,8,128]{2,1,0:T(8,128)(2,1)S(1)}, u32[]{:S(2)}, u32[]{:S(2)}) collective-permute-start(bf16[16,8,128]{2,1,0:T(8,128)(2,1)S(1)} %get-tuple-element.18.one), channel_id=1, source_target_pairs={{0,24},{8,16},{16,8},{24,0},{32,56},{40,48},{48,40},{56,32},{64,88... | collective-permute-start | bytes 98312 | tf_op jit(solution)/shard_map/ppermute | solution.py:388
  24.7 0.2 collective-permute-start.6
  24.9 1.9 %collective-permute-done.8.cross = bf16[16,8,128]{2,1,0:T(8,128)(2,1)S(1)} collective-permute-done((bf16[16,8,128]{2,1,0:T(8,128)(2,1)S(1)}, bf16[16,8,128]{2,1,0:T(8,128)(2,1)S(1)}, u32[]{:S(2)}, u32[]{:S(2)}) %collective-permute-start.8) | collective-permute-done | bytes 32800 | tf_op jit(solution)/shard_map/ppermute | solution.py:388
  26.9 0.8 collective-permute-done.7.far
  27.6 1.0 %collective-permute-done.6.near = bf16[16,8,128]{2,1,0:T(8,128)(2,1)S(1)} collective-permute-done((bf16[16,8,128]{2,1,0:T(8,128)(2,1)S(1)}, bf16[16,8,128]{2,1,0:T(8,128)(2,1)S(1)}, u32[]{:S(2)}, u32[]{:S(2)}) %collective-permute-start.6) | collective-permute-done | bytes 32800 | tf_op jit(solution)/shard_map/ppermute | solution.py:388
  28.6 0.0 copy-start.6
  28.6 0.0 copy-start.8
  28.7 0.0 copy-start.9
  28.7 2.6 %shard_map.170.own = bf16[528,128]{1,0:T(8,128)(2,1)S(1)} custom-call(bf16[16,8,128]{2,1,0:T(8,128)(2,1)S(1)} %get-tuple-element.18.one, bf16[16,8,128]{2,1,0:T(8,128)(2,1)S(1)} %collective-permute-done.6.near, bf16[16,8,128]{2,1,0:T(8,128)(2,1)S(1)} %collective-permute-done.7.far, bf16[16,8,128]{2,1,0:T(8,128)(2,1)S(1)} %collective-permute-done.8.cross, ...), custom_call_target="tpu_custom_call" | custom-call | flops 67108864 | bytes 8388608 | tf_op jit(solution)/shard_map/pallas_call | solution.py:464
  31.3 1.1 %collective-permute-start.11 = (bf16[528,128]{1,0:T(8,128)(2,1)S(1)}, bf16[528,128]{1,0:T(8,128)(2,1)S(1)}, u32[]{:S(2)}, u32[]{:S(2)}) collective-permute-start(bf16[528,128]{1,0:T(8,128)(2,1)S(1)} %shard_map.170.own), channel_id=1, source_target_pairs={{0,16},{8,24},{16,0},{24,8},{32,48},{40,56},{48,32},{56,40},{64,80... | collective-permute-start | bytes 405512 | tf_op jit(solution)/shard_map/ppermute | solution.py:388
  32.4 1.8 %collective-permute-start.10 = (bf16[528,128]{1,0:T(8,128)(2,1)S(1)}, bf16[528,128]{1,0:T(8,128)(2,1)S(1)}, u32[]{:S(2)}, u32[]{:S(2)}) collective-permute-start(bf16[528,128]{1,0:T(8,128)(2,1)S(1)} %shard_map.170.own), channel_id=1, source_target_pairs={{0,24},{8,16},{16,8},{24,0},{32,56},{40,48},{48,40},{56,32},{64,88... | collective-permute-start | bytes 405512 | tf_op jit(solution)/shard_map/ppermute | solution.py:388
  34.3 0.6 collective-permute-start.9
  34.9 3.1 %collective-permute-done.11.cross = bf16[528,128]{1,0:T(8,128)(2,1)S(1)} collective-permute-done((bf16[528,128]{1,0:T(8,128)(2,1)S(1)}, bf16[528,128]{1,0:T(8,128)(2,1)S(1)}, u32[]{:S(2)}, u32[]{:S(2)}) %collective-permute-start.11) | collective-permute-done | bytes 135200 | tf_op jit(solution)/shard_map/ppermute | solution.py:388
  38.0 1.4 %collective-permute-done.10.far = bf16[528,128]{1,0:T(8,128)(2,1)S(1)} collective-permute-done((bf16[528,128]{1,0:T(8,128)(2,1)S(1)}, bf16[528,128]{1,0:T(8,128)(2,1)S(1)}, u32[]{:S(2)}, u32[]{:S(2)}) %collective-permute-start.10) | collective-permute-done | bytes 135200 | tf_op jit(solution)/shard_map/ppermute | solution.py:388
  39.3 0.0 collective-permute-done.9.near
  39.4 0.6 shard_map.171.own
  40.0 0.0 copy-start.2
  40.0 0.0 copy-start.7
  40.0 0.0 copy-start.10
  40.0 1.6 %collective-permute-start.14 = (bf16[528,128]{1,0:T(8,128)(2,1)S(1)}, bf16[528,128]{1,0:T(8,128)(2,1)S(1)}, u32[]{:S(2)}, u32[]{:S(2)}) collective-permute-start(bf16[528,128]{1,0:T(8,128)(2,1)S(1)} %shard_map.171.own), channel_id=1, source_target_pairs={{0,64},{8,72},{16,80},{24,88},{32,96},{40,104},{48,112},{56,120},{... | collective-permute-start | bytes 405512 | tf_op jit(solution)/shard_map/ppermute | solution.py:388
  41.6 1.0 %collective-permute-start.13 = (bf16[528,128]{1,0:T(8,128)(2,1)S(1)}, bf16[528,128]{1,0:T(8,128)(2,1)S(1)}, u32[]{:S(2)}, u32[]{:S(2)}) collective-permute-start(bf16[528,128]{1,0:T(8,128)(2,1)S(1)} %shard_map.171.own), channel_id=1, source_target_pairs={{0,96},{8,104},{16,112},{24,120},{32,64},{40,72},{48,80},{56,88},{... | collective-permute-start | bytes 405512 | tf_op jit(solution)/shard_map/ppermute | solution.py:388
  42.6 1.0 collective-permute-start.12
  43.6 3.0 %collective-permute-done.14.cross = bf16[528,128]{1,0:T(8,128)(2,1)S(1)} collective-permute-done((bf16[528,128]{1,0:T(8,128)(2,1)S(1)}, bf16[528,128]{1,0:T(8,128)(2,1)S(1)}, u32[]{:S(2)}, u32[]{:S(2)}) %collective-permute-start.14) | collective-permute-done | bytes 135200 | tf_op jit(solution)/shard_map/ppermute | solution.py:388
  46.7 1.4 %collective-permute-done.13.far = bf16[528,128]{1,0:T(8,128)(2,1)S(1)} collective-permute-done((bf16[528,128]{1,0:T(8,128)(2,1)S(1)}, bf16[528,128]{1,0:T(8,128)(2,1)S(1)}, u32[]{:S(2)}, u32[]{:S(2)}) %collective-permute-start.13) | collective-permute-done | bytes 135200 | tf_op jit(solution)/shard_map/ppermute | solution.py:388
  48.1 0.0 collective-permute-done.12.near
  48.1 0.9 shard_map.172
  49.0 0.1 collective-permute-start.15
  49.1 1.3 %collective-permute-done.15 = f32[64,384]{1,0:T(8,128)S(1)} collective-permute-done((f32[64,384]{1,0:T(8,128)S(1)}, f32[64,384]{1,0:T(8,128)S(1)}, u32[]{:S(2)}, u32[]{:S(2)}) %collective-permute-start.15) | collective-permute-done | bytes 98336 | tf_op jit(solution)/shard_map/ppermute | solution.py:379
  50.4 4.0 %collective-permute-start.18 = (bf16[64,384]{1,0:T(8,128)(2,1)S(1)}, bf16[64,384]{1,0:T(8,128)(2,1)S(1)}, u32[]{:S(2)}, u32[]{:S(2)}) collective-permute-start(bf16[64,384]{1,0:T(8,128)(2,1)S(1)} %add_convert_fusion.own), channel_id=1, source_target_pairs={{0,4},{1,5},{2,6},{3,7},{4,0},{5,1},{6,2},{7,3},{8,12},{9,13},{10,... | collective-permute-start | bytes 147464 | tf_op jit(solution)/shard_map/ppermute | solution.py:388
  54.4 0.7 collective-permute-start.17
  55.1 0.3 collective-permute-start.16
  55.4 1.1 %collective-permute-done.18.cross = bf16[64,384]{1,0:T(8,128)(2,1)S(1)} collective-permute-done((bf16[64,384]{1,0:T(8,128)(2,1)S(1)}, bf16[64,384]{1,0:T(8,128)(2,1)S(1)}, u32[]{:S(2)}, u32[]{:S(2)}) %collective-permute-start.18) | collective-permute-done | bytes 49184 | tf_op jit(solution)/shard_map/ppermute | solution.py:388
  56.5 3.2 %collective-permute-done.17.far = bf16[64,384]{1,0:T(8,128)(2,1)S(1)} collective-permute-done((bf16[64,384]{1,0:T(8,128)(2,1)S(1)}, bf16[64,384]{1,0:T(8,128)(2,1)S(1)}, u32[]{:S(2)}, u32[]{:S(2)}) %collective-permute-start.17) | collective-permute-done | bytes 49184 | tf_op jit(solution)/shard_map/ppermute | solution.py:388
  59.7 0.0 collective-permute-done.16.near
  59.7 0.0 copy-start.5
  59.7 0.9 shard_map.173
  60.6 14.8 %all_to_all.10.parts = bf16[16,4,4224]{2,1,0:T(4,128)(2,1)S(1)} all-to-all(bf16[16,4,4224]{2,1,0:T(4,128)(2,1)S(1)} %get-tuple-element.21), channel_id=1, replica_groups=mesh['kv'=16,'head'=8] {'kv'}, dimensions={0} | all-to-all | bytes 1081344 | tf_op jit(solution)/shard_map/all_to_all | solution.py:375
  75.4 1.3 %shard_map.174 = (bf16[16,4,1152]{2,1,0:T(4,128)(2,1)S(1)}, f32[128,64]{1,0:T(8,128)S(1)}, f32[8,16,128]{2,1,0:T(8,128)S(1)}) custom-call(bf16[16,4,4224]{2,1,0:T(4,128)(2,1)S(1)} %all_to_all.10.parts, f32[1,8]{1,0:T(1,128)S(1)} %bitcast.18, f32[4,8,128,128]{3,2,1,0:T(8,128)S(1)} %copy-done.2, f32[8,128]{1,0:T(8,128)S(1)} %bitcast.14), custom_call_target="tpu_custom_call" | custom-call | bytes 4194304 | tf_op jit(solution)/shard_map/pallas_call | solution.py:483
  76.7 11.1 %all_to_all.11.blocks = bf16[16,4,1152]{2,1,0:T(4,128)(2,1)S(1)} all-to-all(bf16[16,4,1152]{2,1,0:T(4,128)(2,1)S(1)} %get-tuple-element.22), channel_id=1, replica_groups=mesh['kv'=16,'head'=8] {'kv'}, dimensions={0} | all-to-all | bytes 294912 | tf_op jit(solution)/shard_map/all_to_all | solution.py:375
  87.8 0.4 shard_map.175.own
  88.2 0.1 collective-permute-start.19
  88.3 1.3 %collective-permute-done.19.near = f32[72,384]{1,0:T(8,128)S(1)} collective-permute-done((f32[72,384]{1,0:T(8,128)S(1)}, f32[72,384]{1,0:T(8,128)S(1)}, u32[]{:S(2)}, u32[]{:S(2)}) %collective-permute-start.19) | collective-permute-done | bytes 110624 | tf_op jit(solution)/shard_map/ppermute | solution.py:379
  89.6 1.9 %collective-permute-start.22 = (bf16[80,384]{1,0:T(8,128)(2,1)S(1)}, bf16[80,384]{1,0:T(8,128)(2,1)S(1)}, u32[]{:S(2)}, u32[]{:S(2)}) collective-permute-start(bf16[80,384]{1,0:T(8,128)(2,1)S(1)} %shard_map.176.own), channel_id=1, source_target_pairs={{0,4},{1,5},{2,6},{3,7},{4,0},{5,1},{6,2},{7,3},{8,12},{9,13},{10,... | collective-permute-start | bytes 184328 | tf_op jit(solution)/shard_map/ppermute | solution.py:388
  91.6 1.0 %collective-permute-start.21 = (bf16[80,384]{1,0:T(8,128)(2,1)S(1)}, bf16[80,384]{1,0:T(8,128)(2,1)S(1)}, u32[]{:S(2)}, u32[]{:S(2)}) collective-permute-start(bf16[80,384]{1,0:T(8,128)(2,1)S(1)} %shard_map.176.own), channel_id=1, source_target_pairs={{0,6},{1,7},{2,4},{3,5},{4,2},{5,3},{6,0},{7,1},{8,14},{9,15},{10,... | collective-permute-start | bytes 184328 | tf_op jit(solution)/shard_map/ppermute | solution.py:388
  92.6 0.6 collective-permute-start.20
  93.2 1.6 %shard_map.178 = f32[4,8,128,128]{3,2,1,0:T(8,128)} custom-call(f32[128,64]{1,0:T(8,128)S(1)} %get-tuple-element.24.turned, f32[8,16,128]{2,1,0:T(8,128)S(1)} %get-tuple-element.25.mixed, f32[1,8]{1,0:T(1,128)S(1)} %bitcast.19, f32[4,8,128,128]{3,2,1,0:T(8,128)S(1)} %copy-done.2), custom_call_target="tpu_custom_call" | custom-call | bytes 4194304 | tf_op jit(solution)/shard_map/pallas_call | solution.py:502
  94.8 0.7 collective-permute-done.22.cross
  95.5 1.5 %collective-permute-done.21.far = bf16[80,384]{1,0:T(8,128)(2,1)S(1)} collective-permute-done((bf16[80,384]{1,0:T(8,128)(2,1)S(1)}, bf16[80,384]{1,0:T(8,128)(2,1)S(1)}, u32[]{:S(2)}, u32[]{:S(2)}) %collective-permute-start.21) | collective-permute-done | bytes 61472 | tf_op jit(solution)/shard_map/ppermute | solution.py:388
  97.0 0.7 shard_map.177
  (19 shorter events, 0.1 us)
Async XLA Ops:
  2.4 4.6 %collective-permute-start = (f32[16,1408]{1,0:T(8,128)S(1)}, f32[16,1408]{1,0:T(8,128)S(1)}, u32[]{:S(2)}, u32[]{:S(2)}) collective-permute-start(f32[16,1408]{1,0:T(8,128)S(1)} %get-tuple-element.15), channel_id=1, source_target_pairs={{0,8},{8,0},{16,24},{24,16},{32,40},{40,32},{48,56},{56,48},{64,72... | collective-permute-start | bytes 270344 | tf_op jit(solution)/shard_map/ppermute | solution.py:388
  4.0 6.7 %collective-permute-start.1 = (f32[16,1408]{1,0:T(8,128)S(1)}, f32[16,1408]{1,0:T(8,128)S(1)}, u32[]{:S(2)}, u32[]{:S(2)}) collective-permute-start(f32[16,1408]{1,0:T(8,128)S(1)} %get-tuple-element.16), channel_id=1, source_target_pairs={{0,24},{8,16},{16,8},{24,0},{32,56},{40,48},{48,40},{56,32},{64,88... | collective-permute-start | bytes 270344 | tf_op jit(solution)/shard_map/ppermute | solution.py:388
  6.1 6.0 %collective-permute-start.2 = (f32[16,1408]{1,0:T(8,128)S(1)}, f32[16,1408]{1,0:T(8,128)S(1)}, u32[]{:S(2)}, u32[]{:S(2)}) collective-permute-start(f32[16,1408]{1,0:T(8,128)S(1)} %get-tuple-element.17), channel_id=1, source_target_pairs={{0,16},{8,24},{16,0},{24,8},{32,48},{40,56},{48,32},{56,40},{64,80... | collective-permute-start | bytes 270344 | tf_op jit(solution)/shard_map/ppermute | solution.py:388
  12.2 16.5 %copy-start = (bf16[64,1,256,128]{3,2,1,0:T(8,128)(2,1)S(1)}, bf16[64,1,256,128]{3,2,1,0:T(8,128)(2,1)}, u32[]{:S(2)}) copy-start(bf16[64,1,256,128]{3,2,1,0:T(8,128)(2,1)} %param.20) | copy-start | bytes 12582916
  12.2 16.5 %copy-start.1 = (bf16[64,1,256,128]{3,2,1,0:T(8,128)(2,1)S(1)}, bf16[64,1,256,128]{3,2,1,0:T(8,128)(2,1)}, u32[]{:S(2)}) copy-start(bf16[64,1,256,128]{3,2,1,0:T(8,128)(2,1)} %param.21) | copy-start | bytes 12582916
  12.2 6.2 %collective-permute-start.5 = (f32[16,1408]{1,0:T(8,128)S(1)}, f32[16,1408]{1,0:T(8,128)S(1)}, u32[]{:S(2)}, u32[]{:S(2)}) collective-permute-start(f32[16,1408]{1,0:T(8,128)S(1)} %shard_map.168.one), channel_id=1, source_target_pairs={{0,64},{8,72},{16,80},{24,88},{32,96},{40,104},{48,112},{56,120},{... | collective-permute-start | bytes 270344 | tf_op jit(solution)/shard_map/ppermute | solution.py:388
  15.5 5.7 %collective-permute-start.4 = (f32[16,1408]{1,0:T(8,128)S(1)}, f32[16,1408]{1,0:T(8,128)S(1)}, u32[]{:S(2)}, u32[]{:S(2)}) collective-permute-start(f32[16,1408]{1,0:T(8,128)S(1)} %shard_map.168.one), channel_id=1, source_target_pairs={{0,96},{8,104},{16,112},{24,120},{32,64},{40,72},{48,80},{56,88},{... | collective-permute-start | bytes 270344 | tf_op jit(solution)/shard_map/ppermute | solution.py:388
  16.5 4.7 %collective-permute-start.3 = (f32[16,1408]{1,0:T(8,128)S(1)}, f32[16,1408]{1,0:T(8,128)S(1)}, u32[]{:S(2)}, u32[]{:S(2)}) collective-permute-start(f32[16,1408]{1,0:T(8,128)S(1)} %shard_map.168.one), channel_id=1, source_target_pairs={{0,32},{8,40},{16,48},{24,56},{32,0},{40,8},{48,16},{56,24},{64,96... | collective-permute-start | bytes 270344 | tf_op jit(solution)/shard_map/ppermute | solution.py:388
  21.4 5.5 %collective-permute-start.8 = (bf16[16,8,128]{2,1,0:T(8,128)(2,1)S(1)}, bf16[16,8,128]{2,1,0:T(8,128)(2,1)S(1)}, u32[]{:S(2)}, u32[]{:S(2)}) collective-permute-start(bf16[16,8,128]{2,1,0:T(8,128)(2,1)S(1)} %get-tuple-element.18.one), channel_id=1, source_target_pairs={{0,16},{8,24},{16,0},{24,8},{32,48},{40,56},{48,32},{56,40},{64,80... | collective-permute-start | bytes 98312 | tf_op jit(solution)/shard_map/ppermute | solution.py:388
  22.5 5.1 %collective-permute-start.7 = (bf16[16,8,128]{2,1,0:T(8,128)(2,1)S(1)}, bf16[16,8,128]{2,1,0:T(8,128)(2,1)S(1)}, u32[]{:S(2)}, u32[]{:S(2)}) collective-permute-start(bf16[16,8,128]{2,1,0:T(8,128)(2,1)S(1)} %get-tuple-element.18.one), channel_id=1, source_target_pairs={{0,24},{8,16},{16,8},{24,0},{32,56},{40,48},{48,40},{56,32},{64,88... | collective-permute-start | bytes 98312 | tf_op jit(solution)/shard_map/ppermute | solution.py:388
  24.7 3.9 %collective-permute-start.6 = (bf16[16,8,128]{2,1,0:T(8,128)(2,1)S(1)}, bf16[16,8,128]{2,1,0:T(8,128)(2,1)S(1)}, u32[]{:S(2)}, u32[]{:S(2)}) collective-permute-start(bf16[16,8,128]{2,1,0:T(8,128)(2,1)S(1)} %get-tuple-element.18.one), channel_id=1, source_target_pairs={{0,8},{8,0},{16,24},{24,16},{32,40},{40,32},{48,56},{56,48},{64,72... | collective-permute-start | bytes 98312 | tf_op jit(solution)/shard_map/ppermute | solution.py:388
  28.6 19.5 %copy-start.4 = (bf16[1024,384]{1,0:T(8,128)(2,1)S(1)}, bf16[1024,384]{1,0:T(8,128)(2,1)}, u32[]{:S(2)}) copy-start(bf16[1024,384]{1,0:T(8,128)(2,1)} %weight.3) | copy-start | bytes 2359300
  28.6 31.1 %copy-start.3 = (bf16[384,4096]{1,0:T(8,128)(2,1)S(1)}, bf16[384,4096]{1,0:T(8,128)(2,1)}, u32[]{:S(2)}) copy-start(bf16[384,4096]{1,0:T(8,128)(2,1)} %weight.4) | copy-start | bytes 9437188
  28.6 31.1 %copy-start.6 = (bf16[64,384]{1,0:T(8,128)(2,1)S(1)}, bf16[64,384]{1,0:T(8,128)(2,1)}, u32[]{:S(2)}) copy-start(bf16[64,384]{1,0:T(8,128)(2,1)} %hidden.1) | copy-start | bytes 147460
  28.6 31.1 %copy-start.8 = (f32[384]{0:T(512)S(1)}, f32[384]{0:T(512)}, u32[]{:S(2)}) copy-start(f32[384]{0:T(512)} %param.25) | copy-start | bytes 4612
  28.7 31.1 %copy-start.9 = (s32[64]{0:T(128)S(1)}, s32[64]{0:T(128)}, u32[]{:S(2)}) copy-start(s32[64]{0:T(128)} %param.31) | copy-start | bytes 772
  31.3 6.7 %collective-permute-start.11 = (bf16[528,128]{1,0:T(8,128)(2,1)S(1)}, bf16[528,128]{1,0:T(8,128)(2,1)S(1)}, u32[]{:S(2)}, u32[]{:S(2)}) collective-permute-start(bf16[528,128]{1,0:T(8,128)(2,1)S(1)} %shard_map.170.own), channel_id=1, source_target_pairs={{0,16},{8,24},{16,0},{24,8},{32,48},{40,56},{48,32},{56,40},{64,80... | collective-permute-start | bytes 405512 | tf_op jit(solution)/shard_map/ppermute | solution.py:388
  32.4 6.9 %collective-permute-start.10 = (bf16[528,128]{1,0:T(8,128)(2,1)S(1)}, bf16[528,128]{1,0:T(8,128)(2,1)S(1)}, u32[]{:S(2)}, u32[]{:S(2)}) collective-permute-start(bf16[528,128]{1,0:T(8,128)(2,1)S(1)} %shard_map.170.own), channel_id=1, source_target_pairs={{0,24},{8,16},{16,8},{24,0},{32,56},{40,48},{48,40},{56,32},{64,88... | collective-permute-start | bytes 405512 | tf_op jit(solution)/shard_map/ppermute | solution.py:388
  34.3 5.1 %collective-permute-start.9 = (bf16[528,128]{1,0:T(8,128)(2,1)S(1)}, bf16[528,128]{1,0:T(8,128)(2,1)S(1)}, u32[]{:S(2)}, u32[]{:S(2)}) collective-permute-start(bf16[528,128]{1,0:T(8,128)(2,1)S(1)} %shard_map.170.own), channel_id=1, source_target_pairs={{0,8},{8,0},{16,24},{24,16},{32,40},{40,32},{48,56},{56,48},{64,72... | collective-permute-start | bytes 405512 | tf_op jit(solution)/shard_map/ppermute | solution.py:388
  40.0 35.4 %copy-start.2 = (f32[4,8,128,128]{3,2,1,0:T(8,128)S(1)}, f32[4,8,128,128]{3,2,1,0:T(8,128)}, u32[]{:S(2)}) copy-start(f32[4,8,128,128]{3,2,1,0:T(8,128)} %states.3) | copy-start | bytes 6291460
  40.0 35.4 %copy-start.7 = (f32[1024]{0:T(1024)S(1)}, f32[1024]{0:T(1024)}, u32[]{:S(2)}) copy-start(f32[1024]{0:T(1024)} %param.29) | copy-start | bytes 12292
  40.0 35.3 %copy-start.10 = (f32[8]{0:T(128)S(1)}, f32[8]{0:T(128)}, u32[]{:S(2)}) copy-start(f32[8]{0:T(128)} %param.27) | copy-start | bytes 100
  40.0 6.6 %collective-permute-start.14 = (bf16[528,128]{1,0:T(8,128)(2,1)S(1)}, bf16[528,128]{1,0:T(8,128)(2,1)S(1)}, u32[]{:S(2)}, u32[]{:S(2)}) collective-permute-start(bf16[528,128]{1,0:T(8,128)(2,1)S(1)} %shard_map.171.own), channel_id=1, source_target_pairs={{0,64},{8,72},{16,80},{24,88},{32,96},{40,104},{48,112},{56,120},{... | collective-permute-start | bytes 405512 | tf_op jit(solution)/shard_map/ppermute | solution.py:388
  41.6 6.4 %collective-permute-start.13 = (bf16[528,128]{1,0:T(8,128)(2,1)S(1)}, bf16[528,128]{1,0:T(8,128)(2,1)S(1)}, u32[]{:S(2)}, u32[]{:S(2)}) collective-permute-start(bf16[528,128]{1,0:T(8,128)(2,1)S(1)} %shard_map.171.own), channel_id=1, source_target_pairs={{0,96},{8,104},{16,112},{24,120},{32,64},{40,72},{48,80},{56,88},{... | collective-permute-start | bytes 405512 | tf_op jit(solution)/shard_map/ppermute | solution.py:388
  42.6 5.4 %collective-permute-start.12 = (bf16[528,128]{1,0:T(8,128)(2,1)S(1)}, bf16[528,128]{1,0:T(8,128)(2,1)S(1)}, u32[]{:S(2)}, u32[]{:S(2)}) collective-permute-start(bf16[528,128]{1,0:T(8,128)(2,1)S(1)} %shard_map.171.own), channel_id=1, source_target_pairs={{0,32},{8,40},{16,48},{24,56},{32,0},{40,8},{48,16},{56,24},{64,96... | collective-permute-start | bytes 405512 | tf_op jit(solution)/shard_map/ppermute | solution.py:388
  49.0 1.4 %collective-permute-start.15 = (f32[64,384]{1,0:T(8,128)S(1)}, f32[64,384]{1,0:T(8,128)S(1)}, u32[]{:S(2)}, u32[]{:S(2)}) collective-permute-start(f32[64,384]{1,0:T(8,128)S(1)} %shard_map.172), channel_id=1, source_target_pairs={{0,1},{1,0},{2,3},{3,2},{4,5},{5,4},{6,7},{7,6},{8,9},{9,8},{10,11... | collective-permute-start | bytes 294920 | tf_op jit(solution)/shard_map/ppermute | solution.py:379
  50.4 6.0 %collective-permute-start.18 = (bf16[64,384]{1,0:T(8,128)(2,1)S(1)}, bf16[64,384]{1,0:T(8,128)(2,1)S(1)}, u32[]{:S(2)}, u32[]{:S(2)}) collective-permute-start(bf16[64,384]{1,0:T(8,128)(2,1)S(1)} %add_convert_fusion.own), channel_id=1, source_target_pairs={{0,4},{1,5},{2,6},{3,7},{4,0},{5,1},{6,2},{7,3},{8,12},{9,13},{10,... | collective-permute-start | bytes 147464 | tf_op jit(solution)/shard_map/ppermute | solution.py:388
  54.4 5.3 %collective-permute-start.17 = (bf16[64,384]{1,0:T(8,128)(2,1)S(1)}, bf16[64,384]{1,0:T(8,128)(2,1)S(1)}, u32[]{:S(2)}, u32[]{:S(2)}) collective-permute-start(bf16[64,384]{1,0:T(8,128)(2,1)S(1)} %add_convert_fusion.own), channel_id=1, source_target_pairs={{0,6},{1,7},{2,4},{3,5},{4,2},{5,3},{6,0},{7,1},{8,14},{9,15},{10,... | collective-permute-start | bytes 147464 | tf_op jit(solution)/shard_map/ppermute | solution.py:388
  55.1 4.6 %collective-permute-start.16 = (bf16[64,384]{1,0:T(8,128)(2,1)S(1)}, bf16[64,384]{1,0:T(8,128)(2,1)S(1)}, u32[]{:S(2)}, u32[]{:S(2)}) collective-permute-start(bf16[64,384]{1,0:T(8,128)(2,1)S(1)} %add_convert_fusion.own), channel_id=1, source_target_pairs={{0,2},{1,3},{2,0},{3,1},{4,6},{5,7},{6,4},{7,5},{8,10},{9,11},{10,... | collective-permute-start | bytes 147464 | tf_op jit(solution)/shard_map/ppermute | solution.py:388
  59.7 28.1 %copy-start.5 = (bf16[1024,384]{1,0:T(8,128)(2,1)S(1)}, bf16[1024,384]{1,0:T(8,128)(2,1)}, u32[]{:S(2)}) copy-start(bf16[1024,384]{1,0:T(8,128)(2,1)} %weight.5) | copy-start | bytes 2359300
  88.2 1.4 %collective-permute-start.19 = (f32[72,384]{1,0:T(8,128)S(1)}, f32[72,384]{1,0:T(8,128)S(1)}, u32[]{:S(2)}, u32[]{:S(2)}) collective-permute-start(f32[72,384]{1,0:T(8,128)S(1)} %shard_map.175.own), channel_id=1, source_target_pairs={{0,1},{1,0},{2,3},{3,2},{4,5},{5,4},{6,7},{7,6},{8,9},{9,8},{10,11... | collective-permute-start | bytes 331784 | tf_op jit(solution)/shard_map/ppermute | solution.py:379
  89.6 5.8 %collective-permute-start.22 = (bf16[80,384]{1,0:T(8,128)(2,1)S(1)}, bf16[80,384]{1,0:T(8,128)(2,1)S(1)}, u32[]{:S(2)}, u32[]{:S(2)}) collective-permute-start(bf16[80,384]{1,0:T(8,128)(2,1)S(1)} %shard_map.176.own), channel_id=1, source_target_pairs={{0,4},{1,5},{2,6},{3,7},{4,0},{5,1},{6,2},{7,3},{8,12},{9,13},{10,... | collective-permute-start | bytes 184328 | tf_op jit(solution)/shard_map/ppermute | solution.py:388
  91.6 5.4 %collective-permute-start.21 = (bf16[80,384]{1,0:T(8,128)(2,1)S(1)}, bf16[80,384]{1,0:T(8,128)(2,1)S(1)}, u32[]{:S(2)}, u32[]{:S(2)}) collective-permute-start(bf16[80,384]{1,0:T(8,128)(2,1)S(1)} %shard_map.176.own), channel_id=1, source_target_pairs={{0,6},{1,7},{2,4},{3,5},{4,2},{5,3},{6,0},{7,1},{8,14},{9,15},{10,... | collective-permute-start | bytes 184328 | tf_op jit(solution)/shard_map/ppermute | solution.py:388
  92.6 4.4 %collective-permute-start.20 = (bf16[80,384]{1,0:T(8,128)(2,1)S(1)}, bf16[80,384]{1,0:T(8,128)(2,1)S(1)}, u32[]{:S(2)}, u32[]{:S(2)}) collective-permute-start(bf16[80,384]{1,0:T(8,128)(2,1)S(1)} %shard_map.176.own), channel_id=1, source_target_pairs={{0,2},{1,3},{2,0},{3,1},{4,6},{5,7},{6,4},{7,5},{8,10},{9,11},{10,... | collective-permute-start | bytes 184328 | tf_op jit(solution)/shard_map/ppermute | solution.py:388

commit v8 on v7

--- a/solution.py
+++ b/solution.py
@@ -114,11 +114,11 @@
         part[...] = whole[pl.ds(at, rows), :]
 
 
-def sum_kernel(own, near, far, cross, keys, values, out):
+def sum_kernel(own, near, far, cross, out):
     out[...] = four(own, near, far, cross)
 
 
-def normalise_kernel(one, near, far, cross, out, own, tiles):
+def normalise_kernel(one, near, far, cross, keys, values, out, own, tiles):
     total = four(one, near, far, cross)
     columns = own.shape[1]
     width = columns * HD
@@ -450,14 +450,14 @@
         *(in_hbm(row) for row in plan),
     )
     parts = kernel_call(
-        sum_kernel, block, [VMEM] * 4 + [HBM] * 2, 8 * MIB, 0, 20 * quarter * width,
-    )(*spread((own, near, far, cross), "kv", 1), in_hbm(keys), in_hbm(values))
+        sum_kernel, block, [VMEM] * 4, 8 * MIB, 0, 20 * quarter * width,
+    )(*spread((own, near, far, cross), "kv", 1))
     queries, own = kernel_call(
         normalise_kernel,
         (S((quarter, GQ, HD), BF16), S((rows, GQ + 2, HD), F32)),
-        [VMEM] * 4, 8 * MIB, 0, 20 * quarter * width,
+        [VMEM] * 4 + [HBM] * 2, 8 * MIB, 0, 20 * quarter * width,
         [pltpu.VMEM((quarter, GQ + 2, HD), F32)],
-    )(*along(parts, "kv", 4))
+    )(*along(parts, "kv", 4), in_hbm(keys), in_hbm(values))
     tiles = [pltpu.VMEM((slots, GQ, HD), F32)] * 3 + [pltpu.VMEM((requests + 1, GQ, HD), F32)] * 3
     tiles.append(pltpu.VMEM((requests, GQ, HD), BF16))
     partial = S((requests * GQ + LINES, HD), BF16)

time: 98 us -> 98 us (level)
  no operation moved by 1% of the time
where the time goes in v8:
time: 98 us; the launch traced here: 97.8 us
  waiting for transfers between devices  31.8 us (32%)
  starting transfers between devices  28.1 us (29%)
  blocking collectives  25.9 us (26%)
  Pallas kernels  11 us (11%)
    ppermute x21, waiting for transfers between devices, spread(): lax.ppermute(part, axis, [(i, i ^ k * stride) for i in range(size)])  29.2 us
    ppermute x21, starting transfers between devices, spread(): lax.ppermute(part, axis, [(i, i ^ k * stride) for i in range(size)])  28 us
    all_to_all x2, blocking collectives, exchange(): return lax.all_to_all(blocks, 'kv', 0, 0, tiled=True)  25.9 us
    pallas_call x1, Pallas kernels, per_device(): kernel_call(attention_kernel, partial, [VMEM] * 6 + [SMEM, VMEM], 24 * MI...  2.62 us
    ppermute x2, waiting for transfers between devices, other_core(): lax.ppermute(value, 'head', [(i, i ^ 1) for i in range(lax.axis_size('hea...  2.59 us
  transfers between devices with their start and end apart: 23, of which 18 were waited for; matrix products, arithmetic and copies ran while one was open for 0% of the time, Pallas kernels for 2%

profile of v8, /device:TPU:0, one launch (start us, length us, event | category | flops | bytes accessed | tf_op | source)
XLA Modules:
  0.0 97.8 jit_solution(17671212549198603129)
XLA Ops:
  0.6 1.7 %shard_map.167 = (f32[16,1408]{1,0:T(8,128)S(1)}, f32[16,1408]{1,0:T(8,128)S(1)}, f32[16,1408]{1,0:T(8,128)S(1)}, f32[16,1408]{1,0:T(8,128)S(1)}, s32[2,64]{1,0:T(2,128)S(1)}) custom-call(bf16[64,384]{1,0:T(8,128)(2,1)} %hidden.1, f32[3,128]{1,0:T(4,128)} %bitcast.20, bf16[384,1280]{1,0:T(8,128)(2,1)} %weight_hbm.1, s32[1,64]{1,0:T(1,128)} %bitcast.21, ...), custom_call_target="tpu_custom_call" | custom-call | flops 62914560 | bytes 983040 | tf_op jit(solution)/shard_map/pallas_call | solution.py:434
  2.4 1.7 %collective-permute-start = (f32[16,1408]{1,0:T(8,128)S(1)}, f32[16,1408]{1,0:T(8,128)S(1)}, u32[]{:S(2)}, u32[]{:S(2)}) collective-permute-start(f32[16,1408]{1,0:T(8,128)S(1)} %get-tuple-element.15), channel_id=1, source_target_pairs={{0,8},{8,0},{16,24},{24,16},{32,40},{40,32},{48,56},{56,48},{64,72... | collective-permute-start | bytes 270344 | tf_op jit(solution)/shard_map/ppermute | solution.py:388
  4.0 2.1 %collective-permute-start.1 = (f32[16,1408]{1,0:T(8,128)S(1)}, f32[16,1408]{1,0:T(8,128)S(1)}, u32[]{:S(2)}, u32[]{:S(2)}) collective-permute-start(f32[16,1408]{1,0:T(8,128)S(1)} %get-tuple-element.16), channel_id=1, source_target_pairs={{0,24},{8,16},{16,8},{24,0},{32,56},{40,48},{48,40},{56,32},{64,88... | collective-permute-start | bytes 270344 | tf_op jit(solution)/shard_map/ppermute | solution.py:388
  6.1 0.6 collective-permute-start.2
  6.8 0.2 collective-permute-done.near
  7.0 3.8 %collective-permute-done.1.far = f32[16,1408]{1,0:T(8,128)S(1)} collective-permute-done((f32[16,1408]{1,0:T(8,128)S(1)}, f32[16,1408]{1,0:T(8,128)S(1)}, u32[]{:S(2)}, u32[]{:S(2)}) %collective-permute-start.1) | collective-permute-done | bytes 90144 | tf_op jit(solution)/shard_map/ppermute | solution.py:388
  10.7 1.4 %collective-permute-done.2.cross = f32[16,1408]{1,0:T(8,128)S(1)} collective-permute-done((f32[16,1408]{1,0:T(8,128)S(1)}, f32[16,1408]{1,0:T(8,128)S(1)}, u32[]{:S(2)}, u32[]{:S(2)}) %collective-permute-start.2) | collective-permute-done | bytes 90144 | tf_op jit(solution)/shard_map/ppermute | solution.py:388
  12.2 3.3 %collective-permute-start.5 = (f32[16,1408]{1,0:T(8,128)S(1)}, f32[16,1408]{1,0:T(8,128)S(1)}, u32[]{:S(2)}, u32[]{:S(2)}) collective-permute-start(f32[16,1408]{1,0:T(8,128)S(1)} %shard_map.168.one), channel_id=1, source_target_pairs={{0,64},{8,72},{16,80},{24,88},{32,96},{40,104},{48,112},{56,120},{... | collective-permute-start | bytes 270344 | tf_op jit(solution)/shard_map/ppermute | solution.py:388
  15.4 1.1 %collective-permute-start.4 = (f32[16,1408]{1,0:T(8,128)S(1)}, f32[16,1408]{1,0:T(8,128)S(1)}, u32[]{:S(2)}, u32[]{:S(2)}) collective-permute-start(f32[16,1408]{1,0:T(8,128)S(1)} %shard_map.168.one), channel_id=1, source_target_pairs={{0,96},{8,104},{16,112},{24,120},{32,64},{40,72},{48,80},{56,88},{... | collective-permute-start | bytes 270344 | tf_op jit(solution)/shard_map/ppermute | solution.py:388
  16.5 0.0 collective-permute-start.3
  16.5 1.9 %collective-permute-done.5.cross = f32[16,1408]{1,0:T(8,128)S(1)} collective-permute-done((f32[16,1408]{1,0:T(8,128)S(1)}, f32[16,1408]{1,0:T(8,128)S(1)}, u32[]{:S(2)}, u32[]{:S(2)}) %collective-permute-start.5) | collective-permute-done | bytes 90144 | tf_op jit(solution)/shard_map/ppermute | solution.py:388
  18.4 2.8 %collective-permute-done.4.far = f32[16,1408]{1,0:T(8,128)S(1)} collective-permute-done((f32[16,1408]{1,0:T(8,128)S(1)}, f32[16,1408]{1,0:T(8,128)S(1)}, u32[]{:S(2)}, u32[]{:S(2)}) %collective-permute-start.4) | collective-permute-done | bytes 90144 | tf_op jit(solution)/shard_map/ppermute | solution.py:388
  21.2 0.0 collective-permute-done.3.near
  21.2 0.1 shard_map.169
  21.4 1.2 %collective-permute-start.8 = (bf16[16,8,128]{2,1,0:T(8,128)(2,1)S(1)}, bf16[16,8,128]{2,1,0:T(8,128)(2,1)S(1)}, u32[]{:S(2)}, u32[]{:S(2)}) collective-permute-start(bf16[16,8,128]{2,1,0:T(8,128)(2,1)S(1)} %get-tuple-element.18.one), channel_id=1, source_target_pairs={{0,16},{8,24},{16,0},{24,8},{32,48},{40,56},{48,32},{56,40},{64,80... | collective-permute-start | bytes 98312 | tf_op jit(solution)/shard_map/ppermute | solution.py:388
  22.5 2.2 %collective-permute-start.7 = (bf16[16,8,128]{2,1,0:T(8,128)(2,1)S(1)}, bf16[16,8,128]{2,1,0:T(8,128)(2,1)S(1)}, u32[]{:S(2)}, u32[]{:S(2)}) collective-permute-start(bf16[16,8,128]{2,1,0:T(8,128)(2,1)S(1)} %get-tuple-element.18.one), channel_id=1, source_target_pairs={{0,24},{8,16},{16,8},{24,0},{32,56},{40,48},{48,40},{56,32},{64,88... | collective-permute-start | bytes 98312 | tf_op jit(solution)/shard_map/ppermute | solution.py:388
  24.7 0.2 collective-permute-start.6
  24.9 1.9 %collective-permute-done.8.cross = bf16[16,8,128]{2,1,0:T(8,128)(2,1)S(1)} collective-permute-done((bf16[16,8,128]{2,1,0:T(8,128)(2,1)S(1)}, bf16[16,8,128]{2,1,0:T(8,128)(2,1)S(1)}, u32[]{:S(2)}, u32[]{:S(2)}) %collective-permute-start.8) | collective-permute-done | bytes 32800 | tf_op jit(solution)/shard_map/ppermute | solution.py:388
  26.9 0.8 collective-permute-done.7.far
  27.6 1.0 %collective-permute-done.6.near = bf16[16,8,128]{2,1,0:T(8,128)(2,1)S(1)} collective-permute-done((bf16[16,8,128]{2,1,0:T(8,128)(2,1)S(1)}, bf16[16,8,128]{2,1,0:T(8,128)(2,1)S(1)}, u32[]{:S(2)}, u32[]{:S(2)}) %collective-permute-start.6) | collective-permute-done | bytes 32800 | tf_op jit(solution)/shard_map/ppermute | solution.py:388
  28.6 0.0 copy-start.6
  28.6 0.0 copy-start.8
  28.7 0.0 copy-start.9
  28.7 2.6 %shard_map.170.own = bf16[528,128]{1,0:T(8,128)(2,1)S(1)} custom-call(bf16[16,8,128]{2,1,0:T(8,128)(2,1)S(1)} %get-tuple-element.18.one, bf16[16,8,128]{2,1,0:T(8,128)(2,1)S(1)} %collective-permute-done.6.near, bf16[16,8,128]{2,1,0:T(8,128)(2,1)S(1)} %collective-permute-done.7.far, bf16[16,8,128]{2,1,0:T(8,128)(2,1)S(1)} %collective-permute-done.8.cross, ...), custom_call_target="tpu_custom_call" | custom-call | flops 67108864 | bytes 8388608 | tf_op jit(solution)/shard_map/pallas_call | solution.py:464
  31.3 1.1 %collective-permute-start.11 = (bf16[528,128]{1,0:T(8,128)(2,1)S(1)}, bf16[528,128]{1,0:T(8,128)(2,1)S(1)}, u32[]{:S(2)}, u32[]{:S(2)}) collective-permute-start(bf16[528,128]{1,0:T(8,128)(2,1)S(1)} %shard_map.170.own), channel_id=1, source_target_pairs={{0,16},{8,24},{16,0},{24,8},{32,48},{40,56},{48,32},{56,40},{64,80... | collective-permute-start | bytes 405512 | tf_op jit(solution)/shard_map/ppermute | solution.py:388
  32.4 1.9 %collective-permute-start.10 = (bf16[528,128]{1,0:T(8,128)(2,1)S(1)}, bf16[528,128]{1,0:T(8,128)(2,1)S(1)}, u32[]{:S(2)}, u32[]{:S(2)}) collective-permute-start(bf16[528,128]{1,0:T(8,128)(2,1)S(1)} %shard_map.170.own), channel_id=1, source_target_pairs={{0,24},{8,16},{16,8},{24,0},{32,56},{40,48},{48,40},{56,32},{64,88... | collective-permute-start | bytes 405512 | tf_op jit(solution)/shard_map/ppermute | solution.py:388
  34.3 0.6 collective-permute-start.9
  34.9 3.1 %collective-permute-done.11.cross = bf16[528,128]{1,0:T(8,128)(2,1)S(1)} collective-permute-done((bf16[528,128]{1,0:T(8,128)(2,1)S(1)}, bf16[528,128]{1,0:T(8,128)(2,1)S(1)}, u32[]{:S(2)}, u32[]{:S(2)}) %collective-permute-start.11) | collective-permute-done | bytes 135200 | tf_op jit(solution)/shard_map/ppermute | solution.py:388
  38.0 1.4 %collective-permute-done.10.far = bf16[528,128]{1,0:T(8,128)(2,1)S(1)} collective-permute-done((bf16[528,128]{1,0:T(8,128)(2,1)S(1)}, bf16[528,128]{1,0:T(8,128)(2,1)S(1)}, u32[]{:S(2)}, u32[]{:S(2)}) %collective-permute-start.10) | collective-permute-done | bytes 135200 | tf_op jit(solution)/shard_map/ppermute | solution.py:388
  39.3 0.0 collective-permute-done.9.near
  39.3 0.6 shard_map.171.own
  40.0 0.0 copy-start.2
  40.0 0.0 copy-start.7
  40.0 0.0 copy-start.10
  40.0 1.6 %collective-permute-start.14 = (bf16[528,128]{1,0:T(8,128)(2,1)S(1)}, bf16[528,128]{1,0:T(8,128)(2,1)S(1)}, u32[]{:S(2)}, u32[]{:S(2)}) collective-permute-start(bf16[528,128]{1,0:T(8,128)(2,1)S(1)} %shard_map.171.own), channel_id=1, source_target_pairs={{0,64},{8,72},{16,80},{24,88},{32,96},{40,104},{48,112},{56,120},{... | collective-permute-start | bytes 405512 | tf_op jit(solution)/shard_map/ppermute | solution.py:388
  41.6 1.0 %collective-permute-start.13 = (bf16[528,128]{1,0:T(8,128)(2,1)S(1)}, bf16[528,128]{1,0:T(8,128)(2,1)S(1)}, u32[]{:S(2)}, u32[]{:S(2)}) collective-permute-start(bf16[528,128]{1,0:T(8,128)(2,1)S(1)} %shard_map.171.own), channel_id=1, source_target_pairs={{0,96},{8,104},{16,112},{24,120},{32,64},{40,72},{48,80},{56,88},{... | collective-permute-start | bytes 405512 | tf_op jit(solution)/shard_map/ppermute | solution.py:388
  42.6 1.0 collective-permute-start.12
  43.6 3.0 %collective-permute-done.14.cross = bf16[528,128]{1,0:T(8,128)(2,1)S(1)} collective-permute-done((bf16[528,128]{1,0:T(8,128)(2,1)S(1)}, bf16[528,128]{1,0:T(8,128)(2,1)S(1)}, u32[]{:S(2)}, u32[]{:S(2)}) %collective-permute-start.14) | collective-permute-done | bytes 135200 | tf_op jit(solution)/shard_map/ppermute | solution.py:388
  46.6 1.4 %collective-permute-done.13.far = bf16[528,128]{1,0:T(8,128)(2,1)S(1)} collective-permute-done((bf16[528,128]{1,0:T(8,128)(2,1)S(1)}, bf16[528,128]{1,0:T(8,128)(2,1)S(1)}, u32[]{:S(2)}, u32[]{:S(2)}) %collective-permute-start.13) | collective-permute-done | bytes 135200 | tf_op jit(solution)/shard_map/ppermute | solution.py:388
  48.1 0.9 shard_map.172
  49.0 0.1 collective-permute-start.15
  49.1 1.3 %collective-permute-done.15 = f32[64,384]{1,0:T(8,128)S(1)} collective-permute-done((f32[64,384]{1,0:T(8,128)S(1)}, f32[64,384]{1,0:T(8,128)S(1)}, u32[]{:S(2)}, u32[]{:S(2)}) %collective-permute-start.15) | collective-permute-done | bytes 98336 | tf_op jit(solution)/shard_map/ppermute | solution.py:379
  50.4 4.0 %collective-permute-start.18 = (bf16[64,384]{1,0:T(8,128)(2,1)S(1)}, bf16[64,384]{1,0:T(8,128)(2,1)S(1)}, u32[]{:S(2)}, u32[]{:S(2)}) collective-permute-start(bf16[64,384]{1,0:T(8,128)(2,1)S(1)} %add_convert_fusion.own), channel_id=1, source_target_pairs={{0,4},{1,5},{2,6},{3,7},{4,0},{5,1},{6,2},{7,3},{8,12},{9,13},{10,... | collective-permute-start | bytes 147464 | tf_op jit(solution)/shard_map/ppermute | solution.py:388
  54.4 0.7 collective-permute-start.17
  55.1 0.3 collective-permute-start.16
  55.4 1.1 %collective-permute-done.18.cross = bf16[64,384]{1,0:T(8,128)(2,1)S(1)} collective-permute-done((bf16[64,384]{1,0:T(8,128)(2,1)S(1)}, bf16[64,384]{1,0:T(8,128)(2,1)S(1)}, u32[]{:S(2)}, u32[]{:S(2)}) %collective-permute-start.18) | collective-permute-done | bytes 49184 | tf_op jit(solution)/shard_map/ppermute | solution.py:388
  56.5 3.2 %collective-permute-done.17.far = bf16[64,384]{1,0:T(8,128)(2,1)S(1)} collective-permute-done((bf16[64,384]{1,0:T(8,128)(2,1)S(1)}, bf16[64,384]{1,0:T(8,128)(2,1)S(1)}, u32[]{:S(2)}, u32[]{:S(2)}) %collective-permute-start.17) | collective-permute-done | bytes 49184 | tf_op jit(solution)/shard_map/ppermute | solution.py:388
  59.7 0.0 collective-permute-done.16.near
  59.7 0.0 copy-start.5
  59.7 0.9 shard_map.173
  60.6 14.8 %all_to_all.10.parts = bf16[16,4,4224]{2,1,0:T(4,128)(2,1)S(1)} all-to-all(bf16[16,4,4224]{2,1,0:T(4,128)(2,1)S(1)} %get-tuple-element.21), channel_id=1, replica_groups=mesh['kv'=16,'head'=8] {'kv'}, dimensions={0} | all-to-all | bytes 1081344 | tf_op jit(solution)/shard_map/all_to_all | solution.py:375
  75.4 1.3 %shard_map.174 = (bf16[16,4,1152]{2,1,0:T(4,128)(2,1)S(1)}, f32[128,64]{1,0:T(8,128)S(1)}, f32[8,16,128]{2,1,0:T(8,128)S(1)}) custom-call(bf16[16,4,4224]{2,1,0:T(4,128)(2,1)S(1)} %all_to_all.10.parts, f32[1,8]{1,0:T(1,128)S(1)} %bitcast.18, f32[4,8,128,128]{3,2,1,0:T(8,128)S(1)} %copy-done.2, f32[8,128]{1,0:T(8,128)S(1)} %bitcast.14), custom_call_target="tpu_custom_call" | custom-call | bytes 4194304 | tf_op jit(solution)/shard_map/pallas_call | solution.py:483
  76.7 11.1 %all_to_all.11.blocks = bf16[16,4,1152]{2,1,0:T(4,128)(2,1)S(1)} all-to-all(bf16[16,4,1152]{2,1,0:T(4,128)(2,1)S(1)} %get-tuple-element.22), channel_id=1, replica_groups=mesh['kv'=16,'head'=8] {'kv'}, dimensions={0} | all-to-all | bytes 294912 | tf_op jit(solution)/shard_map/all_to_all | solution.py:375
  87.8 0.4 shard_map.175.own
  88.2 0.1 collective-permute-start.19
  88.3 1.3 %collective-permute-done.19.near = f32[72,384]{1,0:T(8,128)S(1)} collective-permute-done((f32[72,384]{1,0:T(8,128)S(1)}, f32[72,384]{1,0:T(8,128)S(1)}, u32[]{:S(2)}, u32[]{:S(2)}) %collective-permute-start.19) | collective-permute-done | bytes 110624 | tf_op jit(solution)/shard_map/ppermute | solution.py:379
  89.6 2.0 %collective-permute-start.22 = (bf16[80,384]{1,0:T(8,128)(2,1)S(1)}, bf16[80,384]{1,0:T(8,128)(2,1)S(1)}, u32[]{:S(2)}, u32[]{:S(2)}) collective-permute-start(bf16[80,384]{1,0:T(8,128)(2,1)S(1)} %shard_map.176.own), channel_id=1, source_target_pairs={{0,4},{1,5},{2,6},{3,7},{4,0},{5,1},{6,2},{7,3},{8,12},{9,13},{10,... | collective-permute-start | bytes 184328 | tf_op jit(solution)/shard_map/ppermute | solution.py:388
  91.6 1.0 %collective-permute-start.21 = (bf16[80,384]{1,0:T(8,128)(2,1)S(1)}, bf16[80,384]{1,0:T(8,128)(2,1)S(1)}, u32[]{:S(2)}, u32[]{:S(2)}) collective-permute-start(bf16[80,384]{1,0:T(8,128)(2,1)S(1)} %shard_map.176.own), channel_id=1, source_target_pairs={{0,6},{1,7},{2,4},{3,5},{4,2},{5,3},{6,0},{7,1},{8,14},{9,15},{10,... | collective-permute-start | bytes 184328 | tf_op jit(solution)/shard_map/ppermute | solution.py:388
  92.6 0.6 collective-permute-start.20
  93.2 1.6 %shard_map.178 = f32[4,8,128,128]{3,2,1,0:T(8,128)} custom-call(f32[128,64]{1,0:T(8,128)S(1)} %get-tuple-element.24.turned, f32[8,16,128]{2,1,0:T(8,128)S(1)} %get-tuple-element.25.mixed, f32[1,8]{1,0:T(1,128)S(1)} %bitcast.19, f32[4,8,128,128]{3,2,1,0:T(8,128)S(1)} %copy-done.2), custom_call_target="tpu_custom_call" | custom-call | bytes 4194304 | tf_op jit(solution)/shard_map/pallas_call | solution.py:502
  94.8 0.7 collective-permute-done.22.cross
  95.5 1.6 %collective-permute-done.21.far = bf16[80,384]{1,0:T(8,128)(2,1)S(1)} collective-permute-done((bf16[80,384]{1,0:T(8,128)(2,1)S(1)}, bf16[80,384]{1,0:T(8,128)(2,1)S(1)}, u32[]{:S(2)}, u32[]{:S(2)}) %collective-permute-start.21) | collective-permute-done | bytes 61472 | tf_op jit(solution)/shard_map/ppermute | solution.py:388
  97.0 0.0 collective-permute-done.20.near
  97.0 0.7 shard_map.177
  (19 shorter events, 0.1 us)
Async XLA Ops:
  2.4 4.6 %collective-permute-start = (f32[16,1408]{1,0:T(8,128)S(1)}, f32[16,1408]{1,0:T(8,128)S(1)}, u32[]{:S(2)}, u32[]{:S(2)}) collective-permute-start(f32[16,1408]{1,0:T(8,128)S(1)} %get-tuple-element.15), channel_id=1, source_target_pairs={{0,8},{8,0},{16,24},{24,16},{32,40},{40,32},{48,56},{56,48},{64,72... | collective-permute-start | bytes 270344 | tf_op jit(solution)/shard_map/ppermute | solution.py:388
  4.0 6.7 %collective-permute-start.1 = (f32[16,1408]{1,0:T(8,128)S(1)}, f32[16,1408]{1,0:T(8,128)S(1)}, u32[]{:S(2)}, u32[]{:S(2)}) collective-permute-start(f32[16,1408]{1,0:T(8,128)S(1)} %get-tuple-element.16), channel_id=1, source_target_pairs={{0,24},{8,16},{16,8},{24,0},{32,56},{40,48},{48,40},{56,32},{64,88... | collective-permute-start | bytes 270344 | tf_op jit(solution)/shard_map/ppermute | solution.py:388
  6.1 6.0 %collective-permute-start.2 = (f32[16,1408]{1,0:T(8,128)S(1)}, f32[16,1408]{1,0:T(8,128)S(1)}, u32[]{:S(2)}, u32[]{:S(2)}) collective-permute-start(f32[16,1408]{1,0:T(8,128)S(1)} %get-tuple-element.17), channel_id=1, source_target_pairs={{0,16},{8,24},{16,0},{24,8},{32,48},{40,56},{48,32},{56,40},{64,80... | collective-permute-start | bytes 270344 | tf_op jit(solution)/shard_map/ppermute | solution.py:388
  12.2 6.2 %collective-permute-start.5 = (f32[16,1408]{1,0:T(8,128)S(1)}, f32[16,1408]{1,0:T(8,128)S(1)}, u32[]{:S(2)}, u32[]{:S(2)}) collective-permute-start(f32[16,1408]{1,0:T(8,128)S(1)} %shard_map.168.one), channel_id=1, source_target_pairs={{0,64},{8,72},{16,80},{24,88},{32,96},{40,104},{48,112},{56,120},{... | collective-permute-start | bytes 270344 | tf_op jit(solution)/shard_map/ppermute | solution.py:388
  15.4 5.7 %collective-permute-start.4 = (f32[16,1408]{1,0:T(8,128)S(1)}, f32[16,1408]{1,0:T(8,128)S(1)}, u32[]{:S(2)}, u32[]{:S(2)}) collective-permute-start(f32[16,1408]{1,0:T(8,128)S(1)} %shard_map.168.one), channel_id=1, source_target_pairs={{0,96},{8,104},{16,112},{24,120},{32,64},{40,72},{48,80},{56,88},{... | collective-permute-start | bytes 270344 | tf_op jit(solution)/shard_map/ppermute | solution.py:388
  16.5 4.7 %collective-permute-start.3 = (f32[16,1408]{1,0:T(8,128)S(1)}, f32[16,1408]{1,0:T(8,128)S(1)}, u32[]{:S(2)}, u32[]{:S(2)}) collective-permute-start(f32[16,1408]{1,0:T(8,128)S(1)} %shard_map.168.one), channel_id=1, source_target_pairs={{0,32},{8,40},{16,48},{24,56},{32,0},{40,8},{48,16},{56,24},{64,96... | collective-permute-start | bytes 270344 | tf_op jit(solution)/shard_map/ppermute | solution.py:388
  21.2 7.4 %copy-start = (bf16[64,1,256,128]{3,2,1,0:T(8,128)(2,1)S(1)}, bf16[64,1,256,128]{3,2,1,0:T(8,128)(2,1)}, u32[]{:S(2)}) copy-start(bf16[64,1,256,128]{3,2,1,0:T(8,128)(2,1)} %param.20) | copy-start | bytes 12582916
  21.2 7.4 %copy-start.1 = (bf16[64,1,256,128]{3,2,1,0:T(8,128)(2,1)S(1)}, bf16[64,1,256,128]{3,2,1,0:T(8,128)(2,1)}, u32[]{:S(2)}) copy-start(bf16[64,1,256,128]{3,2,1,0:T(8,128)(2,1)} %param.21) | copy-start | bytes 12582916
  21.4 5.5 %collective-permute-start.8 = (bf16[16,8,128]{2,1,0:T(8,128)(2,1)S(1)}, bf16[16,8,128]{2,1,0:T(8,128)(2,1)S(1)}, u32[]{:S(2)}, u32[]{:S(2)}) collective-permute-start(bf16[16,8,128]{2,1,0:T(8,128)(2,1)S(1)} %get-tuple-element.18.one), channel_id=1, source_target_pairs={{0,16},{8,24},{16,0},{24,8},{32,48},{40,56},{48,32},{56,40},{64,80... | collective-permute-start | bytes 98312 | tf_op jit(solution)/shard_map/ppermute | solution.py:388
  22.5 5.1 %collective-permute-start.7 = (bf16[16,8,128]{2,1,0:T(8,128)(2,1)S(1)}, bf16[16,8,128]{2,1,0:T(8,128)(2,1)S(1)}, u32[]{:S(2)}, u32[]{:S(2)}) collective-permute-start(bf16[16,8,128]{2,1,0:T(8,128)(2,1)S(1)} %get-tuple-element.18.one), channel_id=1, source_target_pairs={{0,24},{8,16},{16,8},{24,0},{32,56},{40,48},{48,40},{56,32},{64,88... | collective-permute-start | bytes 98312 | tf_op jit(solution)/shard_map/ppermute | solution.py:388
  24.7 3.9 %collective-permute-start.6 = (bf16[16,8,128]{2,1,0:T(8,128)(2,1)S(1)}, bf16[16,8,128]{2,1,0:T(8,128)(2,1)S(1)}, u32[]{:S(2)}, u32[]{:S(2)}) collective-permute-start(bf16[16,8,128]{2,1,0:T(8,128)(2,1)S(1)} %get-tuple-element.18.one), channel_id=1, source_target_pairs={{0,8},{8,0},{16,24},{24,16},{32,40},{40,32},{48,56},{56,48},{64,72... | collective-permute-start | bytes 98312 | tf_op jit(solution)/shard_map/ppermute | solution.py:388
  28.6 19.5 %copy-start.4 = (bf16[1024,384]{1,0:T(8,128)(2,1)S(1)}, bf16[1024,384]{1,0:T(8,128)(2,1)}, u32[]{:S(2)}) copy-start(bf16[1024,384]{1,0:T(8,128)(2,1)} %weight.3) | copy-start | bytes 2359300
  28.6 31.1 %copy-start.3 = (bf16[384,4096]{1,0:T(8,128)(2,1)S(1)}, bf16[384,4096]{1,0:T(8,128)(2,1)}, u32[]{:S(2)}) copy-start(bf16[384,4096]{1,0:T(8,128)(2,1)} %weight.4) | copy-start | bytes 9437188
  28.6 31.1 %copy-start.6 = (bf16[64,384]{1,0:T(8,128)(2,1)S(1)}, bf16[64,384]{1,0:T(8,128)(2,1)}, u32[]{:S(2)}) copy-start(bf16[64,384]{1,0:T(8,128)(2,1)} %hidden.1) | copy-start | bytes 147460
  28.6 31.1 %copy-start.8 = (f32[384]{0:T(512)S(1)}, f32[384]{0:T(512)}, u32[]{:S(2)}) copy-start(f32[384]{0:T(512)} %param.25) | copy-start | bytes 4612
  28.7 31.1 %copy-start.9 = (s32[64]{0:T(128)S(1)}, s32[64]{0:T(128)}, u32[]{:S(2)}) copy-start(s32[64]{0:T(128)} %param.31) | copy-start | bytes 772
  31.3 6.7 %collective-permute-start.11 = (bf16[528,128]{1,0:T(8,128)(2,1)S(1)}, bf16[528,128]{1,0:T(8,128)(2,1)S(1)}, u32[]{:S(2)}, u32[]{:S(2)}) collective-permute-start(bf16[528,128]{1,0:T(8,128)(2,1)S(1)} %shard_map.170.own), channel_id=1, source_target_pairs={{0,16},{8,24},{16,0},{24,8},{32,48},{40,56},{48,32},{56,40},{64,80... | collective-permute-start | bytes 405512 | tf_op jit(solution)/shard_map/ppermute | solution.py:388
  32.4 6.9 %collective-permute-start.10 = (bf16[528,128]{1,0:T(8,128)(2,1)S(1)}, bf16[528,128]{1,0:T(8,128)(2,1)S(1)}, u32[]{:S(2)}, u32[]{:S(2)}) collective-permute-start(bf16[528,128]{1,0:T(8,128)(2,1)S(1)} %shard_map.170.own), channel_id=1, source_target_pairs={{0,24},{8,16},{16,8},{24,0},{32,56},{40,48},{48,40},{56,32},{64,88... | collective-permute-start | bytes 405512 | tf_op jit(solution)/shard_map/ppermute | solution.py:388
  34.3 5.1 %collective-permute-start.9 = (bf16[528,128]{1,0:T(8,128)(2,1)S(1)}, bf16[528,128]{1,0:T(8,128)(2,1)S(1)}, u32[]{:S(2)}, u32[]{:S(2)}) collective-permute-start(bf16[528,128]{1,0:T(8,128)(2,1)S(1)} %shard_map.170.own), channel_id=1, source_target_pairs={{0,8},{8,0},{16,24},{24,16},{32,40},{40,32},{48,56},{56,48},{64,72... | collective-permute-start | bytes 405512 | tf_op jit(solution)/shard_map/ppermute | solution.py:388
  40.0 35.4 %copy-start.2 = (f32[4,8,128,128]{3,2,1,0:T(8,128)S(1)}, f32[4,8,128,128]{3,2,1,0:T(8,128)}, u32[]{:S(2)}) copy-start(f32[4,8,128,128]{3,2,1,0:T(8,128)} %states.3) | copy-start | bytes 6291460
  40.0 35.4 %copy-start.7 = (f32[1024]{0:T(1024)S(1)}, f32[1024]{0:T(1024)}, u32[]{:S(2)}) copy-start(f32[1024]{0:T(1024)} %param.29) | copy-start | bytes 12292
  40.0 35.4 %copy-start.10 = (f32[8]{0:T(128)S(1)}, f32[8]{0:T(128)}, u32[]{:S(2)}) copy-start(f32[8]{0:T(128)} %param.27) | copy-start | bytes 100
  40.0 6.6 %collective-permute-start.14 = (bf16[528,128]{1,0:T(8,128)(2,1)S(1)}, bf16[528,128]{1,0:T(8,128)(2,1)S(1)}, u32[]{:S(2)}, u32[]{:S(2)}) collective-permute-start(bf16[528,128]{1,0:T(8,128)(2,1)S(1)} %shard_map.171.own), channel_id=1, source_target_pairs={{0,64},{8,72},{16,80},{24,88},{32,96},{40,104},{48,112},{56,120},{... | collective-permute-start | bytes 405512 | tf_op jit(solution)/shard_map/ppermute | solution.py:388
  41.6 6.4 %collective-permute-start.13 = (bf16[528,128]{1,0:T(8,128)(2,1)S(1)}, bf16[528,128]{1,0:T(8,128)(2,1)S(1)}, u32[]{:S(2)}, u32[]{:S(2)}) collective-permute-start(bf16[528,128]{1,0:T(8,128)(2,1)S(1)} %shard_map.171.own), channel_id=1, source_target_pairs={{0,96},{8,104},{16,112},{24,120},{32,64},{40,72},{48,80},{56,88},{... | collective-permute-start | bytes 405512 | tf_op jit(solution)/shard_map/ppermute | solution.py:388
  42.6 5.4 %collective-permute-start.12 = (bf16[528,128]{1,0:T(8,128)(2,1)S(1)}, bf16[528,128]{1,0:T(8,128)(2,1)S(1)}, u32[]{:S(2)}, u32[]{:S(2)}) collective-permute-start(bf16[528,128]{1,0:T(8,128)(2,1)S(1)} %shard_map.171.own), channel_id=1, source_target_pairs={{0,32},{8,40},{16,48},{24,56},{32,0},{40,8},{48,16},{56,24},{64,96... | collective-permute-start | bytes 405512 | tf_op jit(solution)/shard_map/ppermute | solution.py:388
  49.0 1.4 %collective-permute-start.15 = (f32[64,384]{1,0:T(8,128)S(1)}, f32[64,384]{1,0:T(8,128)S(1)}, u32[]{:S(2)}, u32[]{:S(2)}) collective-permute-start(f32[64,384]{1,0:T(8,128)S(1)} %shard_map.172), channel_id=1, source_target_pairs={{0,1},{1,0},{2,3},{3,2},{4,5},{5,4},{6,7},{7,6},{8,9},{9,8},{10,11... | collective-permute-start | bytes 294920 | tf_op jit(solution)/shard_map/ppermute | solution.py:379
  50.4 6.0 %collective-permute-start.18 = (bf16[64,384]{1,0:T(8,128)(2,1)S(1)}, bf16[64,384]{1,0:T(8,128)(2,1)S(1)}, u32[]{:S(2)}, u32[]{:S(2)}) collective-permute-start(bf16[64,384]{1,0:T(8,128)(2,1)S(1)} %add_convert_fusion.own), channel_id=1, source_target_pairs={{0,4},{1,5},{2,6},{3,7},{4,0},{5,1},{6,2},{7,3},{8,12},{9,13},{10,... | collective-permute-start | bytes 147464 | tf_op jit(solution)/shard_map/ppermute | solution.py:388
  54.4 5.3 %collective-permute-start.17 = (bf16[64,384]{1,0:T(8,128)(2,1)S(1)}, bf16[64,384]{1,0:T(8,128)(2,1)S(1)}, u32[]{:S(2)}, u32[]{:S(2)}) collective-permute-start(bf16[64,384]{1,0:T(8,128)(2,1)S(1)} %add_convert_fusion.own), channel_id=1, source_target_pairs={{0,6},{1,7},{2,4},{3,5},{4,2},{5,3},{6,0},{7,1},{8,14},{9,15},{10,... | collective-permute-start | bytes 147464 | tf_op jit(solution)/shard_map/ppermute | solution.py:388
  55.1 4.6 %collective-permute-start.16 = (bf16[64,384]{1,0:T(8,128)(2,1)S(1)}, bf16[64,384]{1,0:T(8,128)(2,1)S(1)}, u32[]{:S(2)}, u32[]{:S(2)}) collective-permute-start(bf16[64,384]{1,0:T(8,128)(2,1)S(1)} %add_convert_fusion.own), channel_id=1, source_target_pairs={{0,2},{1,3},{2,0},{3,1},{4,6},{5,7},{6,4},{7,5},{8,10},{9,11},{10,... | collective-permute-start | bytes 147464 | tf_op jit(solution)/shard_map/ppermute | solution.py:388
  59.7 28.1 %copy-start.5 = (bf16[1024,384]{1,0:T(8,128)(2,1)S(1)}, bf16[1024,384]{1,0:T(8,128)(2,1)}, u32[]{:S(2)}) copy-start(bf16[1024,384]{1,0:T(8,128)(2,1)} %weight.5) | copy-start | bytes 2359300
  88.2 1.4 %collective-permute-start.19 = (f32[72,384]{1,0:T(8,128)S(1)}, f32[72,384]{1,0:T(8,128)S(1)}, u32[]{:S(2)}, u32[]{:S(2)}) collective-permute-start(f32[72,384]{1,0:T(8,128)S(1)} %shard_map.175.own), channel_id=1, source_target_pairs={{0,1},{1,0},{2,3},{3,2},{4,5},{5,4},{6,7},{7,6},{8,9},{9,8},{10,11... | collective-permute-start | bytes 331784 | tf_op jit(solution)/shard_map/ppermute | solution.py:379
  89.6 5.8 %collective-permute-start.22 = (bf16[80,384]{1,0:T(8,128)(2,1)S(1)}, bf16[80,384]{1,0:T(8,128)(2,1)S(1)}, u32[]{:S(2)}, u32[]{:S(2)}) collective-permute-start(bf16[80,384]{1,0:T(8,128)(2,1)S(1)} %shard_map.176.own), channel_id=1, source_target_pairs={{0,4},{1,5},{2,6},{3,7},{4,0},{5,1},{6,2},{7,3},{8,12},{9,13},{10,... | collective-permute-start | bytes 184328 | tf_op jit(solution)/shard_map/ppermute | solution.py:388
  91.6 5.4 %collective-permute-start.21 = (bf16[80,384]{1,0:T(8,128)(2,1)S(1)}, bf16[80,384]{1,0:T(8,128)(2,1)S(1)}, u32[]{:S(2)}, u32[]{:S(2)}) collective-permute-start(bf16[80,384]{1,0:T(8,128)(2,1)S(1)} %shard_map.176.own), channel_id=1, source_target_pairs={{0,6},{1,7},{2,4},{3,5},{4,2},{5,3},{6,0},{7,1},{8,14},{9,15},{10,... | collective-permute-start | bytes 184328 | tf_op jit(solution)/shard_map/ppermute | solution.py:388
  92.6 4.4 %collective-permute-start.20 = (bf16[80,384]{1,0:T(8,128)(2,1)S(1)}, bf16[80,384]{1,0:T(8,128)(2,1)S(1)}, u32[]{:S(2)}, u32[]{:S(2)}) collective-permute-start(bf16[80,384]{1,0:T(8,128)(2,1)S(1)} %shard_map.176.own), channel_id=1, source_target_pairs={{0,2},{1,3},{2,0},{3,1},{4,6},{5,7},{6,4},{7,5},{8,10},{9,11},{10,... | collective-permute-start | bytes 184328 | tf_op jit(solution)/shard_map/ppermute | solution.py:388

commit v9 on v8

--- a/solution.py
+++ b/solution.py
@@ -285,17 +285,17 @@
         out[p, :, width:] = tail[p * rows:(p + 1) * rows].astype(BF16)
 
 
-def lightning_kernel(parts, decay, states, gain, out, turned, mixed, flat, wide):
+def lightning_kernel(parts, decay, states, gain, out, turned, mixed, flat):
     rows, heads = states.shape[0], states.shape[1]
     total = parts[0].astype(F32)
     for p in range(1, parts.shape[0]):
         total = total + parts[p].astype(F32)
     width = 4 * heads * HD
-    scale = jnp.sqrt((total[:, width:width + 1] + total[:, width + 1:width + 2]) / D + EPS)
-    wide[0:rows, :] = total[:, :width] / scale
+    scale = 1.0 / jnp.sqrt((total[:, width:width + 1] + total[:, width + 1:width + 2]) / D + EPS)
     for h in range(heads):
         for k in range(4):
-            mixed[h, k * rows:(k + 1) * rows, :] = wide[0:rows, (4 * h + k) * HD:(4 * h + k + 1) * HD]
+            at = (4 * h + k) * HD
+            mixed[h, k * rows:(k + 1) * rows, :] = total[:, at:at + HD] * scale
     keep = jnp.exp(-decay[...])
     span = range(heads)
     mixing = [mixed[h] for h in span]
@@ -488,7 +488,7 @@
             S((heads, 4 * rows, HD), F32),
         ),
         [VMEM] * 4, 16 * MIB, 0, 8 * rows * size * HD,
-        [pltpu.VMEM((8, size), F32), pltpu.VMEM((8, lin_width), F32)],
+        [pltpu.VMEM((8, size), F32)],
     )(exchange(mixing), decay, states, out_gain.reshape(heads, HD))
     second = kernel_call(
         lightning_out_kernel,

time: 98 us -> 97.9 us (level)
  no operation moved by 1% of the time
where the time goes in v9:
time: 97.9 us; the launch traced here: 97.7 us
  waiting for transfers between devices  31.8 us (32%)
  starting transfers between devices  28.1 us (29%)
  blocking collectives  25.9 us (26%)
  Pallas kernels  11 us (11%)
    ppermute x21, waiting for transfers between devices, spread(): lax.ppermute(part, axis, [(i, i ^ k * stride) for i in range(size)])  29.2 us
    ppermute x21, starting transfers between devices, spread(): lax.ppermute(part, axis, [(i, i ^ k * stride) for i in range(size)])  28 us
    all_to_all x2, blocking collectives, exchange(): return lax.all_to_all(blocks, 'kv', 0, 0, tiled=True)  25.9 us
    pallas_call x1, Pallas kernels, per_device(): kernel_call(attention_kernel, partial, [VMEM] * 6 + [SMEM, VMEM], 24 * MI...  2.62 us
    ppermute x2, waiting for transfers between devices, other_core(): lax.ppermute(value, 'head', [(i, i ^ 1) for i in range(lax.axis_size('hea...  2.59 us
  transfers between devices with their start and end apart: 23, of which 18 were waited for; matrix products, arithmetic and copies ran while one was open for 0% of the time, Pallas kernels for 2%

profile of v9, /device:TPU:0, one launch (start us, length us, event | category | flops | bytes accessed | tf_op | source)
XLA Modules:
  0.0 97.7 jit_solution(12815644315547605356)
XLA Ops:
  0.6 1.7 %shard_map.167 = (f32[16,1408]{1,0:T(8,128)S(1)}, f32[16,1408]{1,0:T(8,128)S(1)}, f32[16,1408]{1,0:T(8,128)S(1)}, f32[16,1408]{1,0:T(8,128)S(1)}, s32[2,64]{1,0:T(2,128)S(1)}) custom-call(bf16[64,384]{1,0:T(8,128)(2,1)} %hidden.1, f32[3,128]{1,0:T(4,128)} %bitcast.20, bf16[384,1280]{1,0:T(8,128)(2,1)} %weight_hbm.1, s32[1,64]{1,0:T(1,128)} %bitcast.21, ...), custom_call_target="tpu_custom_call" | custom-call | flops 62914560 | bytes 983040 | tf_op jit(solution)/shard_map/pallas_call | solution.py:434
  2.4 1.7 %collective-permute-start = (f32[16,1408]{1,0:T(8,128)S(1)}, f32[16,1408]{1,0:T(8,128)S(1)}, u32[]{:S(2)}, u32[]{:S(2)}) collective-permute-start(f32[16,1408]{1,0:T(8,128)S(1)} %get-tuple-element.15), channel_id=1, source_target_pairs={{0,8},{8,0},{16,24},{24,16},{32,40},{40,32},{48,56},{56,48},{64,72... | collective-permute-start | bytes 270344 | tf_op jit(solution)/shard_map/ppermute | solution.py:388
  4.0 2.1 %collective-permute-start.1 = (f32[16,1408]{1,0:T(8,128)S(1)}, f32[16,1408]{1,0:T(8,128)S(1)}, u32[]{:S(2)}, u32[]{:S(2)}) collective-permute-start(f32[16,1408]{1,0:T(8,128)S(1)} %get-tuple-element.16), channel_id=1, source_target_pairs={{0,24},{8,16},{16,8},{24,0},{32,56},{40,48},{48,40},{56,32},{64,88... | collective-permute-start | bytes 270344 | tf_op jit(solution)/shard_map/ppermute | solution.py:388
  6.1 0.6 collective-permute-start.2
  6.8 0.2 collective-permute-done.near
  7.0 3.8 %collective-permute-done.1.far = f32[16,1408]{1,0:T(8,128)S(1)} collective-permute-done((f32[16,1408]{1,0:T(8,128)S(1)}, f32[16,1408]{1,0:T(8,128)S(1)}, u32[]{:S(2)}, u32[]{:S(2)}) %collective-permute-start.1) | collective-permute-done | bytes 90144 | tf_op jit(solution)/shard_map/ppermute | solution.py:388
  10.7 1.4 %collective-permute-done.2.cross = f32[16,1408]{1,0:T(8,128)S(1)} collective-permute-done((f32[16,1408]{1,0:T(8,128)S(1)}, f32[16,1408]{1,0:T(8,128)S(1)}, u32[]{:S(2)}, u32[]{:S(2)}) %collective-permute-start.2) | collective-permute-done | bytes 90144 | tf_op jit(solution)/shard_map/ppermute | solution.py:388
  12.2 3.3 %collective-permute-start.5 = (f32[16,1408]{1,0:T(8,128)S(1)}, f32[16,1408]{1,0:T(8,128)S(1)}, u32[]{:S(2)}, u32[]{:S(2)}) collective-permute-start(f32[16,1408]{1,0:T(8,128)S(1)} %shard_map.168.one), channel_id=1, source_target_pairs={{0,64},{8,72},{16,80},{24,88},{32,96},{40,104},{48,112},{56,120},{... | collective-permute-start | bytes 270344 | tf_op jit(solution)/shard_map/ppermute | solution.py:388
  15.4 1.1 %collective-permute-start.4 = (f32[16,1408]{1,0:T(8,128)S(1)}, f32[16,1408]{1,0:T(8,128)S(1)}, u32[]{:S(2)}, u32[]{:S(2)}) collective-permute-start(f32[16,1408]{1,0:T(8,128)S(1)} %shard_map.168.one), channel_id=1, source_target_pairs={{0,96},{8,104},{16,112},{24,120},{32,64},{40,72},{48,80},{56,88},{... | collective-permute-start | bytes 270344 | tf_op jit(solution)/shard_map/ppermute | solution.py:388
  16.5 0.0 collective-permute-start.3
  16.5 1.9 %collective-permute-done.5.cross = f32[16,1408]{1,0:T(8,128)S(1)} collective-permute-done((f32[16,1408]{1,0:T(8,128)S(1)}, f32[16,1408]{1,0:T(8,128)S(1)}, u32[]{:S(2)}, u32[]{:S(2)}) %collective-permute-start.5) | collective-permute-done | bytes 90144 | tf_op jit(solution)/shard_map/ppermute | solution.py:388
  18.4 2.8 %collective-permute-done.4.far = f32[16,1408]{1,0:T(8,128)S(1)} collective-permute-done((f32[16,1408]{1,0:T(8,128)S(1)}, f32[16,1408]{1,0:T(8,128)S(1)}, u32[]{:S(2)}, u32[]{:S(2)}) %collective-permute-start.4) | collective-permute-done | bytes 90144 | tf_op jit(solution)/shard_map/ppermute | solution.py:388
  21.2 0.0 collective-permute-done.3.near
  21.2 0.1 shard_map.169
  21.4 1.2 %collective-permute-start.8 = (bf16[16,8,128]{2,1,0:T(8,128)(2,1)S(1)}, bf16[16,8,128]{2,1,0:T(8,128)(2,1)S(1)}, u32[]{:S(2)}, u32[]{:S(2)}) collective-permute-start(bf16[16,8,128]{2,1,0:T(8,128)(2,1)S(1)} %get-tuple-element.18.one), channel_id=1, source_target_pairs={{0,16},{8,24},{16,0},{24,8},{32,48},{40,56},{48,32},{56,40},{64,80... | collective-permute-start | bytes 98312 | tf_op jit(solution)/shard_map/ppermute | solution.py:388
  22.5 2.2 %collective-permute-start.7 = (bf16[16,8,128]{2,1,0:T(8,128)(2,1)S(1)}, bf16[16,8,128]{2,1,0:T(8,128)(2,1)S(1)}, u32[]{:S(2)}, u32[]{:S(2)}) collective-permute-start(bf16[16,8,128]{2,1,0:T(8,128)(2,1)S(1)} %get-tuple-element.18.one), channel_id=1, source_target_pairs={{0,24},{8,16},{16,8},{24,0},{32,56},{40,48},{48,40},{56,32},{64,88... | collective-permute-start | bytes 98312 | tf_op jit(solution)/shard_map/ppermute | solution.py:388
  24.7 0.2 collective-permute-start.6
  24.9 1.9 %collective-permute-done.8.cross = bf16[16,8,128]{2,1,0:T(8,128)(2,1)S(1)} collective-permute-done((bf16[16,8,128]{2,1,0:T(8,128)(2,1)S(1)}, bf16[16,8,128]{2,1,0:T(8,128)(2,1)S(1)}, u32[]{:S(2)}, u32[]{:S(2)}) %collective-permute-start.8) | collective-permute-done | bytes 32800 | tf_op jit(solution)/shard_map/ppermute | solution.py:388
  26.9 0.8 collective-permute-done.7.far
  27.6 1.0 %collective-permute-done.6.near = bf16[16,8,128]{2,1,0:T(8,128)(2,1)S(1)} collective-permute-done((bf16[16,8,128]{2,1,0:T(8,128)(2,1)S(1)}, bf16[16,8,128]{2,1,0:T(8,128)(2,1)S(1)}, u32[]{:S(2)}, u32[]{:S(2)}) %collective-permute-start.6) | collective-permute-done | bytes 32800 | tf_op jit(solution)/shard_map/ppermute | solution.py:388
  28.6 0.0 copy-start.6
  28.6 0.0 copy-start.8
  28.7 0.0 copy-start.9
  28.7 2.6 %shard_map.170.own = bf16[528,128]{1,0:T(8,128)(2,1)S(1)} custom-call(bf16[16,8,128]{2,1,0:T(8,128)(2,1)S(1)} %get-tuple-element.18.one, bf16[16,8,128]{2,1,0:T(8,128)(2,1)S(1)} %collective-permute-done.6.near, bf16[16,8,128]{2,1,0:T(8,128)(2,1)S(1)} %collective-permute-done.7.far, bf16[16,8,128]{2,1,0:T(8,128)(2,1)S(1)} %collective-permute-done.8.cross, ...), custom_call_target="tpu_custom_call" | custom-call | flops 67108864 | bytes 8388608 | tf_op jit(solution)/shard_map/pallas_call | solution.py:464
  31.3 1.1 %collective-permute-start.11 = (bf16[528,128]{1,0:T(8,128)(2,1)S(1)}, bf16[528,128]{1,0:T(8,128)(2,1)S(1)}, u32[]{:S(2)}, u32[]{:S(2)}) collective-permute-start(bf16[528,128]{1,0:T(8,128)(2,1)S(1)} %shard_map.170.own), channel_id=1, source_target_pairs={{0,16},{8,24},{16,0},{24,8},{32,48},{40,56},{48,32},{56,40},{64,80... | collective-permute-start | bytes 405512 | tf_op jit(solution)/shard_map/ppermute | solution.py:388
  32.4 1.8 %collective-permute-start.10 = (bf16[528,128]{1,0:T(8,128)(2,1)S(1)}, bf16[528,128]{1,0:T(8,128)(2,1)S(1)}, u32[]{:S(2)}, u32[]{:S(2)}) collective-permute-start(bf16[528,128]{1,0:T(8,128)(2,1)S(1)} %shard_map.170.own), channel_id=1, source_target_pairs={{0,24},{8,16},{16,8},{24,0},{32,56},{40,48},{48,40},{56,32},{64,88... | collective-permute-start | bytes 405512 | tf_op jit(solution)/shard_map/ppermute | solution.py:388
  34.3 0.6 collective-permute-start.9
  34.9 3.1 %collective-permute-done.11.cross = bf16[528,128]{1,0:T(8,128)(2,1)S(1)} collective-permute-done((bf16[528,128]{1,0:T(8,128)(2,1)S(1)}, bf16[528,128]{1,0:T(8,128)(2,1)S(1)}, u32[]{:S(2)}, u32[]{:S(2)}) %collective-permute-start.11) | collective-permute-done | bytes 135200 | tf_op jit(solution)/shard_map/ppermute | solution.py:388
  38.0 1.4 %collective-permute-done.10.far = bf16[528,128]{1,0:T(8,128)(2,1)S(1)} collective-permute-done((bf16[528,128]{1,0:T(8,128)(2,1)S(1)}, bf16[528,128]{1,0:T(8,128)(2,1)S(1)}, u32[]{:S(2)}, u32[]{:S(2)}) %collective-permute-start.10) | collective-permute-done | bytes 135200 | tf_op jit(solution)/shard_map/ppermute | solution.py:388
  39.3 0.6 shard_map.171.own
  40.0 0.0 copy-start.2
  40.0 0.0 copy-start.7
  40.0 0.0 copy-start.10
  40.0 1.6 %collective-permute-start.14 = (bf16[528,128]{1,0:T(8,128)(2,1)S(1)}, bf16[528,128]{1,0:T(8,128)(2,1)S(1)}, u32[]{:S(2)}, u32[]{:S(2)}) collective-permute-start(bf16[528,128]{1,0:T(8,128)(2,1)S(1)} %shard_map.171.own), channel_id=1, source_target_pairs={{0,64},{8,72},{16,80},{24,88},{32,96},{40,104},{48,112},{56,120},{... | collective-permute-start | bytes 405512 | tf_op jit(solution)/shard_map/ppermute | solution.py:388
  41.6 1.0 %collective-permute-start.13 = (bf16[528,128]{1,0:T(8,128)(2,1)S(1)}, bf16[528,128]{1,0:T(8,128)(2,1)S(1)}, u32[]{:S(2)}, u32[]{:S(2)}) collective-permute-start(bf16[528,128]{1,0:T(8,128)(2,1)S(1)} %shard_map.171.own), channel_id=1, source_target_pairs={{0,96},{8,104},{16,112},{24,120},{32,64},{40,72},{48,80},{56,88},{... | collective-permute-start | bytes 405512 | tf_op jit(solution)/shard_map/ppermute | solution.py:388
  42.6 1.0 collective-permute-start.12
  43.6 3.0 %collective-permute-done.14.cross = bf16[528,128]{1,0:T(8,128)(2,1)S(1)} collective-permute-done((bf16[528,128]{1,0:T(8,128)(2,1)S(1)}, bf16[528,128]{1,0:T(8,128)(2,1)S(1)}, u32[]{:S(2)}, u32[]{:S(2)}) %collective-permute-start.14) | collective-permute-done | bytes 135200 | tf_op jit(solution)/shard_map/ppermute | solution.py:388
  46.7 1.4 %collective-permute-done.13.far = bf16[528,128]{1,0:T(8,128)(2,1)S(1)} collective-permute-done((bf16[528,128]{1,0:T(8,128)(2,1)S(1)}, bf16[528,128]{1,0:T(8,128)(2,1)S(1)}, u32[]{:S(2)}, u32[]{:S(2)}) %collective-permute-start.13) | collective-permute-done | bytes 135200 | tf_op jit(solution)/shard_map/ppermute | solution.py:388
  48.1 0.0 collective-permute-done.12.near
  48.1 0.9 shard_map.172
  49.0 0.1 collective-permute-start.15
  49.1 1.3 %collective-permute-done.15 = f32[64,384]{1,0:T(8,128)S(1)} collective-permute-done((f32[64,384]{1,0:T(8,128)S(1)}, f32[64,384]{1,0:T(8,128)S(1)}, u32[]{:S(2)}, u32[]{:S(2)}) %collective-permute-start.15) | collective-permute-done | bytes 98336 | tf_op jit(solution)/shard_map/ppermute | solution.py:379
  50.4 4.0 %collective-permute-start.18 = (bf16[64,384]{1,0:T(8,128)(2,1)S(1)}, bf16[64,384]{1,0:T(8,128)(2,1)S(1)}, u32[]{:S(2)}, u32[]{:S(2)}) collective-permute-start(bf16[64,384]{1,0:T(8,128)(2,1)S(1)} %add_convert_fusion.own), channel_id=1, source_target_pairs={{0,4},{1,5},{2,6},{3,7},{4,0},{5,1},{6,2},{7,3},{8,12},{9,13},{10,... | collective-permute-start | bytes 147464 | tf_op jit(solution)/shard_map/ppermute | solution.py:388
  54.4 0.7 collective-permute-start.17
  55.1 0.3 collective-permute-start.16
  55.4 1.1 %collective-permute-done.18.cross = bf16[64,384]{1,0:T(8,128)(2,1)S(1)} collective-permute-done((bf16[64,384]{1,0:T(8,128)(2,1)S(1)}, bf16[64,384]{1,0:T(8,128)(2,1)S(1)}, u32[]{:S(2)}, u32[]{:S(2)}) %collective-permute-start.18) | collective-permute-done | bytes 49184 | tf_op jit(solution)/shard_map/ppermute | solution.py:388
  56.5 3.2 %collective-permute-done.17.far = bf16[64,384]{1,0:T(8,128)(2,1)S(1)} collective-permute-done((bf16[64,384]{1,0:T(8,128)(2,1)S(1)}, bf16[64,384]{1,0:T(8,128)(2,1)S(1)}, u32[]{:S(2)}, u32[]{:S(2)}) %collective-permute-start.17) | collective-permute-done | bytes 49184 | tf_op jit(solution)/shard_map/ppermute | solution.py:388
  59.7 0.0 collective-permute-done.16.near
  59.7 0.0 copy-start.5
  59.7 0.9 shard_map.173
  60.6 14.8 %all_to_all.10.parts = bf16[16,4,4224]{2,1,0:T(4,128)(2,1)S(1)} all-to-all(bf16[16,4,4224]{2,1,0:T(4,128)(2,1)S(1)} %get-tuple-element.21), channel_id=1, replica_groups=mesh['kv'=16,'head'=8] {'kv'}, dimensions={0} | all-to-all | bytes 1081344 | tf_op jit(solution)/shard_map/all_to_all | solution.py:375
  75.4 1.3 %shard_map.174 = (bf16[16,4,1152]{2,1,0:T(4,128)(2,1)S(1)}, f32[128,64]{1,0:T(8,128)S(1)}, f32[8,16,128]{2,1,0:T(8,128)S(1)}) custom-call(bf16[16,4,4224]{2,1,0:T(4,128)(2,1)S(1)} %all_to_all.10.parts, f32[1,8]{1,0:T(1,128)S(1)} %bitcast.18, f32[4,8,128,128]{3,2,1,0:T(8,128)S(1)} %copy-done.2, f32[8,128]{1,0:T(8,128)S(1)} %bitcast.14), custom_call_target="tpu_custom_call" | custom-call | bytes 4194304 | tf_op jit(solution)/shard_map/pallas_call | solution.py:483
  76.7 11.1 %all_to_all.11.blocks = bf16[16,4,1152]{2,1,0:T(4,128)(2,1)S(1)} all-to-all(bf16[16,4,1152]{2,1,0:T(4,128)(2,1)S(1)} %get-tuple-element.22), channel_id=1, replica_groups=mesh['kv'=16,'head'=8] {'kv'}, dimensions={0} | all-to-all | bytes 294912 | tf_op jit(solution)/shard_map/all_to_all | solution.py:375
  87.8 0.4 shard_map.175.own
  88.2 0.1 collective-permute-start.19
  88.3 1.3 %collective-permute-done.19.near = f32[72,384]{1,0:T(8,128)S(1)} collective-permute-done((f32[72,384]{1,0:T(8,128)S(1)}, f32[72,384]{1,0:T(8,128)S(1)}, u32[]{:S(2)}, u32[]{:S(2)}) %collective-permute-start.19) | collective-permute-done | bytes 110624 | tf_op jit(solution)/shard_map/ppermute | solution.py:379
  89.6 1.9 %collective-permute-start.22 = (bf16[80,384]{1,0:T(8,128)(2,1)S(1)}, bf16[80,384]{1,0:T(8,128)(2,1)S(1)}, u32[]{:S(2)}, u32[]{:S(2)}) collective-permute-start(bf16[80,384]{1,0:T(8,128)(2,1)S(1)} %shard_map.176.own), channel_id=1, source_target_pairs={{0,4},{1,5},{2,6},{3,7},{4,0},{5,1},{6,2},{7,3},{8,12},{9,13},{10,... | collective-permute-start | bytes 184328 | tf_op jit(solution)/shard_map/ppermute | solution.py:388
  91.6 1.0 %collective-permute-start.21 = (bf16[80,384]{1,0:T(8,128)(2,1)S(1)}, bf16[80,384]{1,0:T(8,128)(2,1)S(1)}, u32[]{:S(2)}, u32[]{:S(2)}) collective-permute-start(bf16[80,384]{1,0:T(8,128)(2,1)S(1)} %shard_map.176.own), channel_id=1, source_target_pairs={{0,6},{1,7},{2,4},{3,5},{4,2},{5,3},{6,0},{7,1},{8,14},{9,15},{10,... | collective-permute-start | bytes 184328 | tf_op jit(solution)/shard_map/ppermute | solution.py:388
  92.6 0.6 collective-permute-start.20
  93.2 1.6 %shard_map.178 = f32[4,8,128,128]{3,2,1,0:T(8,128)} custom-call(f32[128,64]{1,0:T(8,128)S(1)} %get-tuple-element.24.turned, f32[8,16,128]{2,1,0:T(8,128)S(1)} %get-tuple-element.25.mixed, f32[1,8]{1,0:T(1,128)S(1)} %bitcast.19, f32[4,8,128,128]{3,2,1,0:T(8,128)S(1)} %copy-done.2), custom_call_target="tpu_custom_call" | custom-call | bytes 4194304 | tf_op jit(solution)/shard_map/pallas_call | solution.py:502
  94.8 0.7 collective-permute-done.22.cross
  95.4 1.6 %collective-permute-done.21.far = bf16[80,384]{1,0:T(8,128)(2,1)S(1)} collective-permute-done((bf16[80,384]{1,0:T(8,128)(2,1)S(1)}, bf16[80,384]{1,0:T(8,128)(2,1)S(1)}, u32[]{:S(2)}, u32[]{:S(2)}) %collective-permute-start.21) | collective-permute-done | bytes 61472 | tf_op jit(solution)/shard_map/ppermute | solution.py:388
  97.0 0.0 collective-permute-done.20.near
  97.0 0.7 shard_map.177
  (19 shorter events, 0.1 us)
Async XLA Ops:
  2.4 4.6 %collective-permute-start = (f32[16,1408]{1,0:T(8,128)S(1)}, f32[16,1408]{1,0:T(8,128)S(1)}, u32[]{:S(2)}, u32[]{:S(2)}) collective-permute-start(f32[16,1408]{1,0:T(8,128)S(1)} %get-tuple-element.15), channel_id=1, source_target_pairs={{0,8},{8,0},{16,24},{24,16},{32,40},{40,32},{48,56},{56,48},{64,72... | collective-permute-start | bytes 270344 | tf_op jit(solution)/shard_map/ppermute | solution.py:388
  4.0 6.7 %collective-permute-start.1 = (f32[16,1408]{1,0:T(8,128)S(1)}, f32[16,1408]{1,0:T(8,128)S(1)}, u32[]{:S(2)}, u32[]{:S(2)}) collective-permute-start(f32[16,1408]{1,0:T(8,128)S(1)} %get-tuple-element.16), channel_id=1, source_target_pairs={{0,24},{8,16},{16,8},{24,0},{32,56},{40,48},{48,40},{56,32},{64,88... | collective-permute-start | bytes 270344 | tf_op jit(solution)/shard_map/ppermute | solution.py:388
  6.1 6.0 %collective-permute-start.2 = (f32[16,1408]{1,0:T(8,128)S(1)}, f32[16,1408]{1,0:T(8,128)S(1)}, u32[]{:S(2)}, u32[]{:S(2)}) collective-permute-start(f32[16,1408]{1,0:T(8,128)S(1)} %get-tuple-element.17), channel_id=1, source_target_pairs={{0,16},{8,24},{16,0},{24,8},{32,48},{40,56},{48,32},{56,40},{64,80... | collective-permute-start | bytes 270344 | tf_op jit(solution)/shard_map/ppermute | solution.py:388
  12.2 6.2 %collective-permute-start.5 = (f32[16,1408]{1,0:T(8,128)S(1)}, f32[16,1408]{1,0:T(8,128)S(1)}, u32[]{:S(2)}, u32[]{:S(2)}) collective-permute-start(f32[16,1408]{1,0:T(8,128)S(1)} %shard_map.168.one), channel_id=1, source_target_pairs={{0,64},{8,72},{16,80},{24,88},{32,96},{40,104},{48,112},{56,120},{... | collective-permute-start | bytes 270344 | tf_op jit(solution)/shard_map/ppermute | solution.py:388
  15.4 5.7 %collective-permute-start.4 = (f32[16,1408]{1,0:T(8,128)S(1)}, f32[16,1408]{1,0:T(8,128)S(1)}, u32[]{:S(2)}, u32[]{:S(2)}) collective-permute-start(f32[16,1408]{1,0:T(8,128)S(1)} %shard_map.168.one), channel_id=1, source_target_pairs={{0,96},{8,104},{16,112},{24,120},{32,64},{40,72},{48,80},{56,88},{... | collective-permute-start | bytes 270344 | tf_op jit(solution)/shard_map/ppermute | solution.py:388
  16.5 4.7 %collective-permute-start.3 = (f32[16,1408]{1,0:T(8,128)S(1)}, f32[16,1408]{1,0:T(8,128)S(1)}, u32[]{:S(2)}, u32[]{:S(2)}) collective-permute-start(f32[16,1408]{1,0:T(8,128)S(1)} %shard_map.168.one), channel_id=1, source_target_pairs={{0,32},{8,40},{16,48},{24,56},{32,0},{40,8},{48,16},{56,24},{64,96... | collective-permute-start | bytes 270344 | tf_op jit(solution)/shard_map/ppermute | solution.py:388
  21.2 7.4 %copy-start = (bf16[64,1,256,128]{3,2,1,0:T(8,128)(2,1)S(1)}, bf16[64,1,256,128]{3,2,1,0:T(8,128)(2,1)}, u32[]{:S(2)}) copy-start(bf16[64,1,256,128]{3,2,1,0:T(8,128)(2,1)} %param.20) | copy-start | bytes 12582916
  21.2 7.4 %copy-start.1 = (bf16[64,1,256,128]{3,2,1,0:T(8,128)(2,1)S(1)}, bf16[64,1,256,128]{3,2,1,0:T(8,128)(2,1)}, u32[]{:S(2)}) copy-start(bf16[64,1,256,128]{3,2,1,0:T(8,128)(2,1)} %param.21) | copy-start | bytes 12582916
  21.4 5.5 %collective-permute-start.8 = (bf16[16,8,128]{2,1,0:T(8,128)(2,1)S(1)}, bf16[16,8,128]{2,1,0:T(8,128)(2,1)S(1)}, u32[]{:S(2)}, u32[]{:S(2)}) collective-permute-start(bf16[16,8,128]{2,1,0:T(8,128)(2,1)S(1)} %get-tuple-element.18.one), channel_id=1, source_target_pairs={{0,16},{8,24},{16,0},{24,8},{32,48},{40,56},{48,32},{56,40},{64,80... | collective-permute-start | bytes 98312 | tf_op jit(solution)/shard_map/ppermute | solution.py:388
  22.5 5.1 %collective-permute-start.7 = (bf16[16,8,128]{2,1,0:T(8,128)(2,1)S(1)}, bf16[16,8,128]{2,1,0:T(8,128)(2,1)S(1)}, u32[]{:S(2)}, u32[]{:S(2)}) collective-permute-start(bf16[16,8,128]{2,1,0:T(8,128)(2,1)S(1)} %get-tuple-element.18.one), channel_id=1, source_target_pairs={{0,24},{8,16},{16,8},{24,0},{32,56},{40,48},{48,40},{56,32},{64,88... | collective-permute-start | bytes 98312 | tf_op jit(solution)/shard_map/ppermute | solution.py:388
  24.7 3.9 %collective-permute-start.6 = (bf16[16,8,128]{2,1,0:T(8,128)(2,1)S(1)}, bf16[16,8,128]{2,1,0:T(8,128)(2,1)S(1)}, u32[]{:S(2)}, u32[]{:S(2)}) collective-permute-start(bf16[16,8,128]{2,1,0:T(8,128)(2,1)S(1)} %get-tuple-element.18.one), channel_id=1, source_target_pairs={{0,8},{8,0},{16,24},{24,16},{32,40},{40,32},{48,56},{56,48},{64,72... | collective-permute-start | bytes 98312 | tf_op jit(solution)/shard_map/ppermute | solution.py:388
  28.6 19.5 %copy-start.4 = (bf16[1024,384]{1,0:T(8,128)(2,1)S(1)}, bf16[1024,384]{1,0:T(8,128)(2,1)}, u32[]{:S(2)}) copy-start(bf16[1024,384]{1,0:T(8,128)(2,1)} %weight.3) | copy-start | bytes 2359300
  28.6 31.1 %copy-start.3 = (bf16[384,4096]{1,0:T(8,128)(2,1)S(1)}, bf16[384,4096]{1,0:T(8,128)(2,1)}, u32[]{:S(2)}) copy-start(bf16[384,4096]{1,0:T(8,128)(2,1)} %weight.4) | copy-start | bytes 9437188
  28.6 31.1 %copy-start.6 = (bf16[64,384]{1,0:T(8,128)(2,1)S(1)}, bf16[64,384]{1,0:T(8,128)(2,1)}, u32[]{:S(2)}) copy-start(bf16[64,384]{1,0:T(8,128)(2,1)} %hidden.1) | copy-start | bytes 147460
  28.6 31.1 %copy-start.8 = (f32[384]{0:T(512)S(1)}, f32[384]{0:T(512)}, u32[]{:S(2)}) copy-start(f32[384]{0:T(512)} %param.25) | copy-start | bytes 4612
  28.7 31.1 %copy-start.9 = (s32[64]{0:T(128)S(1)}, s32[64]{0:T(128)}, u32[]{:S(2)}) copy-start(s32[64]{0:T(128)} %param.31) | copy-start | bytes 772
  31.3 6.7 %collective-permute-start.11 = (bf16[528,128]{1,0:T(8,128)(2,1)S(1)}, bf16[528,128]{1,0:T(8,128)(2,1)S(1)}, u32[]{:S(2)}, u32[]{:S(2)}) collective-permute-start(bf16[528,128]{1,0:T(8,128)(2,1)S(1)} %shard_map.170.own), channel_id=1, source_target_pairs={{0,16},{8,24},{16,0},{24,8},{32,48},{40,56},{48,32},{56,40},{64,80... | collective-permute-start | bytes 405512 | tf_op jit(solution)/shard_map/ppermute | solution.py:388
  32.4 6.9 %collective-permute-start.10 = (bf16[528,128]{1,0:T(8,128)(2,1)S(1)}, bf16[528,128]{1,0:T(8,128)(2,1)S(1)}, u32[]{:S(2)}, u32[]{:S(2)}) collective-permute-start(bf16[528,128]{1,0:T(8,128)(2,1)S(1)} %shard_map.170.own), channel_id=1, source_target_pairs={{0,24},{8,16},{16,8},{24,0},{32,56},{40,48},{48,40},{56,32},{64,88... | collective-permute-start | bytes 405512 | tf_op jit(solution)/shard_map/ppermute | solution.py:388
  34.3 5.1 %collective-permute-start.9 = (bf16[528,128]{1,0:T(8,128)(2,1)S(1)}, bf16[528,128]{1,0:T(8,128)(2,1)S(1)}, u32[]{:S(2)}, u32[]{:S(2)}) collective-permute-start(bf16[528,128]{1,0:T(8,128)(2,1)S(1)} %shard_map.170.own), channel_id=1, source_target_pairs={{0,8},{8,0},{16,24},{24,16},{32,40},{40,32},{48,56},{56,48},{64,72... | collective-permute-start | bytes 405512 | tf_op jit(solution)/shard_map/ppermute | solution.py:388
  40.0 35.4 %copy-start.2 = (f32[4,8,128,128]{3,2,1,0:T(8,128)S(1)}, f32[4,8,128,128]{3,2,1,0:T(8,128)}, u32[]{:S(2)}) copy-start(f32[4,8,128,128]{3,2,1,0:T(8,128)} %states.3) | copy-start | bytes 6291460
  40.0 35.4 %copy-start.7 = (f32[1024]{0:T(1024)S(1)}, f32[1024]{0:T(1024)}, u32[]{:S(2)}) copy-start(f32[1024]{0:T(1024)} %param.29) | copy-start | bytes 12292
  40.0 35.3 %copy-start.10 = (f32[8]{0:T(128)S(1)}, f32[8]{0:T(128)}, u32[]{:S(2)}) copy-start(f32[8]{0:T(128)} %param.27) | copy-start | bytes 100
  40.0 6.6 %collective-permute-start.14 = (bf16[528,128]{1,0:T(8,128)(2,1)S(1)}, bf16[528,128]{1,0:T(8,128)(2,1)S(1)}, u32[]{:S(2)}, u32[]{:S(2)}) collective-permute-start(bf16[528,128]{1,0:T(8,128)(2,1)S(1)} %shard_map.171.own), channel_id=1, source_target_pairs={{0,64},{8,72},{16,80},{24,88},{32,96},{40,104},{48,112},{56,120},{... | collective-permute-start | bytes 405512 | tf_op jit(solution)/shard_map/ppermute | solution.py:388
  41.6 6.4 %collective-permute-start.13 = (bf16[528,128]{1,0:T(8,128)(2,1)S(1)}, bf16[528,128]{1,0:T(8,128)(2,1)S(1)}, u32[]{:S(2)}, u32[]{:S(2)}) collective-permute-start(bf16[528,128]{1,0:T(8,128)(2,1)S(1)} %shard_map.171.own), channel_id=1, source_target_pairs={{0,96},{8,104},{16,112},{24,120},{32,64},{40,72},{48,80},{56,88},{... | collective-permute-start | bytes 405512 | tf_op jit(solution)/shard_map/ppermute | solution.py:388
  42.6 5.4 %collective-permute-start.12 = (bf16[528,128]{1,0:T(8,128)(2,1)S(1)}, bf16[528,128]{1,0:T(8,128)(2,1)S(1)}, u32[]{:S(2)}, u32[]{:S(2)}) collective-permute-start(bf16[528,128]{1,0:T(8,128)(2,1)S(1)} %shard_map.171.own), channel_id=1, source_target_pairs={{0,32},{8,40},{16,48},{24,56},{32,0},{40,8},{48,16},{56,24},{64,96... | collective-permute-start | bytes 405512 | tf_op jit(solution)/shard_map/ppermute | solution.py:388
  49.0 1.4 %collective-permute-start.15 = (f32[64,384]{1,0:T(8,128)S(1)}, f32[64,384]{1,0:T(8,128)S(1)}, u32[]{:S(2)}, u32[]{:S(2)}) collective-permute-start(f32[64,384]{1,0:T(8,128)S(1)} %shard_map.172), channel_id=1, source_target_pairs={{0,1},{1,0},{2,3},{3,2},{4,5},{5,4},{6,7},{7,6},{8,9},{9,8},{10,11... | collective-permute-start | bytes 294920 | tf_op jit(solution)/shard_map/ppermute | solution.py:379
  50.4 6.0 %collective-permute-start.18 = (bf16[64,384]{1,0:T(8,128)(2,1)S(1)}, bf16[64,384]{1,0:T(8,128)(2,1)S(1)}, u32[]{:S(2)}, u32[]{:S(2)}) collective-permute-start(bf16[64,384]{1,0:T(8,128)(2,1)S(1)} %add_convert_fusion.own), channel_id=1, source_target_pairs={{0,4},{1,5},{2,6},{3,7},{4,0},{5,1},{6,2},{7,3},{8,12},{9,13},{10,... | collective-permute-start | bytes 147464 | tf_op jit(solution)/shard_map/ppermute | solution.py:388
  54.4 5.3 %collective-permute-start.17 = (bf16[64,384]{1,0:T(8,128)(2,1)S(1)}, bf16[64,384]{1,0:T(8,128)(2,1)S(1)}, u32[]{:S(2)}, u32[]{:S(2)}) collective-permute-start(bf16[64,384]{1,0:T(8,128)(2,1)S(1)} %add_convert_fusion.own), channel_id=1, source_target_pairs={{0,6},{1,7},{2,4},{3,5},{4,2},{5,3},{6,0},{7,1},{8,14},{9,15},{10,... | collective-permute-start | bytes 147464 | tf_op jit(solution)/shard_map/ppermute | solution.py:388
  55.1 4.6 %collective-permute-start.16 = (bf16[64,384]{1,0:T(8,128)(2,1)S(1)}, bf16[64,384]{1,0:T(8,128)(2,1)S(1)}, u32[]{:S(2)}, u32[]{:S(2)}) collective-permute-start(bf16[64,384]{1,0:T(8,128)(2,1)S(1)} %add_convert_fusion.own), channel_id=1, source_target_pairs={{0,2},{1,3},{2,0},{3,1},{4,6},{5,7},{6,4},{7,5},{8,10},{9,11},{10,... | collective-permute-start | bytes 147464 | tf_op jit(solution)/shard_map/ppermute | solution.py:388
  59.7 28.1 %copy-start.5 = (bf16[1024,384]{1,0:T(8,128)(2,1)S(1)}, bf16[1024,384]{1,0:T(8,128)(2,1)}, u32[]{:S(2)}) copy-start(bf16[1024,384]{1,0:T(8,128)(2,1)} %weight.5) | copy-start | bytes 2359300
  88.2 1.4 %collective-permute-start.19 = (f32[72,384]{1,0:T(8,128)S(1)}, f32[72,384]{1,0:T(8,128)S(1)}, u32[]{:S(2)}, u32[]{:S(2)}) collective-permute-start(f32[72,384]{1,0:T(8,128)S(1)} %shard_map.175.own), channel_id=1, source_target_pairs={{0,1},{1,0},{2,3},{3,2},{4,5},{5,4},{6,7},{7,6},{8,9},{9,8},{10,11... | collective-permute-start | bytes 331784 | tf_op jit(solution)/shard_map/ppermute | solution.py:379
  89.6 5.8 %collective-permute-start.22 = (bf16[80,384]{1,0:T(8,128)(2,1)S(1)}, bf16[80,384]{1,0:T(8,128)(2,1)S(1)}, u32[]{:S(2)}, u32[]{:S(2)}) collective-permute-start(bf16[80,384]{1,0:T(8,128)(2,1)S(1)} %shard_map.176.own), channel_id=1, source_target_pairs={{0,4},{1,5},{2,6},{3,7},{4,0},{5,1},{6,2},{7,3},{8,12},{9,13},{10,... | collective-permute-start | bytes 184328 | tf_op jit(solution)/shard_map/ppermute | solution.py:388
  91.6 5.4 %collective-permute-start.21 = (bf16[80,384]{1,0:T(8,128)(2,1)S(1)}, bf16[80,384]{1,0:T(8,128)(2,1)S(1)}, u32[]{:S(2)}, u32[]{:S(2)}) collective-permute-start(bf16[80,384]{1,0:T(8,128)(2,1)S(1)} %shard_map.176.own), channel_id=1, source_target_pairs={{0,6},{1,7},{2,4},{3,5},{4,2},{5,3},{6,0},{7,1},{8,14},{9,15},{10,... | collective-permute-start | bytes 184328 | tf_op jit(solution)/shard_map/ppermute | solution.py:388
  92.6 4.4 %collective-permute-start.20 = (bf16[80,384]{1,0:T(8,128)(2,1)S(1)}, bf16[80,384]{1,0:T(8,128)(2,1)S(1)}, u32[]{:S(2)}, u32[]{:S(2)}) collective-permute-start(bf16[80,384]{1,0:T(8,128)(2,1)S(1)} %shard_map.176.own), channel_id=1, source_target_pairs={{0,2},{1,3},{2,0},{3,1},{4,6},{5,7},{6,4},{7,5},{8,10},{9,11},{10,... | collective-permute-start | bytes 184328 | tf_op jit(solution)/shard_map/ppermute | solution.py:388
